TPU v7x, 256 devices: a whole 4x4x8 slice. The times are simulated.
256 devices in a mesh: leaf: 64 (over x, z, core), rhs: 4 (over y).
Axes of the slice: x: 4, y: 4, z: 8, core: 2. Of those that a mesh axis runs over, the one named last changes fastest.
Arguments:
- coords: float32 [2, 1048576], P(None, 'leaf'), may hold values from 0 to 1
- charges: float32 [8, 1048576], P('rhs', 'leaf'), may hold values from -6 to 6
- leaf_basis: float32 [1024, 64, 1024], P('leaf'), may hold values from -0.1875 to 0.1875
- transfer: float32 [128, 15, 64, 64], P('leaf'), may hold values from -0.75 to 0.75
- coupling: float32 [128, 124, 64, 64], P('leaf'), may hold values from -0.25 to 0.25
- far_pairs: int32 [128, 124], P('leaf'), may hold values from 0 to 1023, as said below
- near_list: int32 [1024, 9], P('leaf'), may hold values from 0 to 1023, as said below
- near_count: int32 [1024], P('leaf'), may hold values from 1 to 9, as said below
Outputs:
- potential: float32 [8, 1048576], P('rhs', 'leaf')
Inputs may be any that keep to these rules, and one draw needn't show every extreme that they name: `near_list`: row i names the leaves that act on leaf i directly: its first entry is i, its first near_count[i] entries are distinct, the rest repeat i. Every named leaf j lies at most one strip row and one column from i, so |j - i| <= 5; j names i whenever i names j. `near_count`: the number of live entries of the matching row of near_list. `far_pairs`: each entry names a cluster of its pair's level other than the pair's target.
All inputs are finite; a program needn't handle non-finite values.
Results may differ from a plain program's by a relative error of at most 0.0003.
Values sent between devices are 32-bit elements; how exact they have to be, the bound alone decides.
No kernel may reach another device: no remote copies, remote signals or barrier semaphores. Data moves between devices by JAX's collectives and lax.ppermute only.
A program may use at most 128 MiB of HBM per device.

v0:
```python
import jax
import jax.numpy as jnp
from jax import lax
from jax.sharding import PartitionSpec as P

FAR = 8
STRIP = 4


TOP_PRECISION = lax.Precision.HIGHEST
TRANSFER_OFFSETS = (0, 8, 12, 14)
DECAY_RATE = 4.0


def with_halo(value, sides, width):
    for axis, dim in sides:
        count, length = (lax.axis_size(axis), value.shape[dim])
        up = [(i, (i + 1) % count) for i in range(count - 1)]
        down = [(j, i) for i, j in up]
        last = lax.slice_in_dim(value, length - width, length, axis=dim)
        initial = lax.slice_in_dim(value, 0, width, axis=dim)
        before = lax.ppermute(last, axis, up)
        after = lax.ppermute(initial, axis, down)
        value = jnp.concatenate([before, value, after], axis=dim)
    return value


def shards(coords, charges, leaf_basis, transfer, coupling, far_pairs, near_list, near_count):
    columns = charges.shape[0]
    leaves = near_count.shape[0]
    basis_rank = leaf_basis.shape[1]
    points = leaf_basis.shape[2]
    quarter = points // lax.axis_size("rhs")
    device = lax.axis_index("leaf")
    rhs_index = lax.axis_index("rhs")
    rim_leaves = STRIP + 1
    all_charges = lax.all_gather(charges, "rhs", axis=0, tiled=True)
    stacked = with_halo(
        jnp.concatenate([coords, all_charges], axis=0), (("leaf", 1),), rim_leaves * points
    )
    ext_points = stacked[:2]
    ext_charges = stacked[2:]
    ext_leaves = leaves + 2 * rim_leaves
    ext_points = ext_points.reshape(2, ext_leaves, points)
    ext_charges = ext_charges.reshape(-1, ext_leaves, points)
    first_leaf = device * leaves
    own_leaf = first_leaf + jnp.arange(leaves, dtype=jnp.int32)
    own_pos = lax.dynamic_slice_in_dim(
        coords.reshape(2, leaves, points), rhs_index * quarter, quarter, 2
    )
    target_row = own_pos[0] + (own_leaf // STRIP).astype(jnp.float32)[:, None]
    target_col = own_pos[1] + (own_leaf % STRIP).astype(jnp.float32)[:, None]
    variance = points ** (-0.5)

    def add_slot(slot_index, running):
        partner = near_list[:, slot_index]
        local_index = partner - first_leaf + rim_leaves
        source_pos = jnp.take(ext_points, local_index, axis=1)
        source_charge = jnp.take(ext_charges, local_index, axis=1)
        source_row = source_pos[0] + (partner // STRIP).astype(jnp.float32)[:, None]
        source_col = source_pos[1] + (partner % STRIP).astype(jnp.float32)[:, None]
        distance = jnp.sqrt(
            (target_row[:, :, None] - source_row[:, None, :]) ** 2
            + (target_col[:, :, None] - source_col[:, None, :]) ** 2
        )
        weight = jnp.where(slot_index < near_count, variance, 0.0)[:, None, None]
        kernel = jnp.exp(-DECAY_RATE * distance) * weight
        return running + jnp.einsum("atp,cap->cat", kernel, source_charge, precision=TOP_PRECISION)

    near_rows = lax.fori_loop(
        0,
        jnp.max(near_count),
        add_slot,
        jnp.zeros((ext_charges.shape[0], leaves, quarter), jnp.float32),
    )
    near_mine = lax.all_to_all(near_rows, "rhs", split_axis=0, concat_axis=2, tiled=True)
    charge_leaf = charges.reshape(columns, leaves, points)
    skeleton = jnp.einsum("arp,cap->acr", leaf_basis, charge_leaf, precision=TOP_PRECISION)
    levels_up = [skeleton]
    transfer_sets = []
    current = skeleton
    for height in range(1, 5):
        slot_count = 8 // 2 ** (height - 1)
        start = TRANSFER_OFFSETS[height - 1]
        transfer_block = transfer[:, start : start + slot_count].reshape(-1, basis_rank, basis_rank)
        transfer_sets.append(transfer_block)
        lifted = jnp.einsum("ncr,nrq->ncq", current, transfer_block, precision=TOP_PRECISION)
        current = lifted if height == 4 else lifted.reshape(-1, 2, columns, basis_rank).sum(1)
        levels_up.append(current)
    gathered = [lax.all_gather(piece, "leaf", axis=0, tiled=True) for piece in levels_up]
    gathered[4] = gathered[4].reshape(-1, 2, columns, basis_rank).sum(1)
    targets = []
    offset = 0
    for height in range(5):
        slot_count = 8 * FAR // 2**height
        local_blocks = coupling[:, offset : offset + slot_count].reshape(-1, basis_rank, basis_rank)
        sources = far_pairs[:, offset : offset + slot_count].reshape(-1)
        selected = jnp.take(gathered[height], sources, axis=0)
        matvec_output = jnp.einsum("vde,vte->vdt", selected, local_blocks, precision=TOP_PRECISION)
        offset = offset + slot_count
        targets.append(matvec_output.reshape(-1, FAR, columns, basis_rank).sum(1))
    downward = targets[4]
    for height in range(4, 0, -1):
        transfer_block = transfer_sets[height - 1]
        parent = jnp.repeat(downward, 2, axis=0)
        downward = targets[height - 1] + jnp.einsum(
            "ncs,nrs->ncr", parent, transfer_block, precision=TOP_PRECISION
        )
    distant_portion = jnp.einsum("arp,acr->cap", leaf_basis, downward, precision=TOP_PRECISION)
    return (distant_portion + near_mine).reshape(columns, leaves * points)


def solution(mesh):
    return jax.shard_map(
        shards,
        mesh=mesh,
        in_specs=(
            P(None, "leaf"),
            P("rhs", "leaf"),
            P("leaf", None, None),
            P("leaf", None, None, None),
            P("leaf", None, None, None),
            P("leaf", None),
            P("leaf", None),
            P("leaf"),
        ),
        out_specs=P("rhs", "leaf"),
        check_vma=False,
    )
```

profile of v0, /device:TPU:6, one launch (start us, length us, event | category | flops | bytes accessed | tf_op | source)
XLA Modules:
  0.0 632.1 jit_solution(6453089518955259127)
XLA Ops:
  0.0 13.5 %all-gather = f32[4,2,16384]{2,1,0:T(2,128)S(1)} all-gather(f32[1,2,16384]{2,1,0:T(2,128)} %bitcast.148), channel_id=1, replica_groups=mesh['leaf'=64,'rhs'=4] {'rhs'}, dimensions={0}, use_global_device_ids=true | all-gather | bytes 655360 | tf_op jit(solution)/shard_map/all_gather | solution.py:37
  15.6 5.9 collective-permute-start.1
  25.9 5.4 slice.76
  31.3 3.1 slice.79
  35.8 5.3 slice.82
  42.6 5.5 slice.85
  48.0 3.6 fusion.79
  51.6 55.0 %all_gather.18 = f32[1024,2,64]{2,1,0:T(2,128)} all-gather(f32[16,2,64]{2,1,0:T(2,128)S(1)} %fusion.79), channel_id=1, replica_groups=mesh['leaf'=64,'rhs'=4] {'leaf'}, dimensions={0}, use_global_device_ids=true | all-gather | bytes 532480 | tf_op jit(solution)/shard_map/all_gather | solution.py:90
  107.1 52.6 %all_gather.19 = f32[512,2,64]{2,1,0:T(2,128)} all-gather(f32[8,2,64]{2,1,0:T(2,128)S(1)} %bitcast_reduce_fusion.5), channel_id=1, replica_groups=mesh['leaf'=64,'rhs'=4] {'leaf'}, dimensions={0}, use_global_device_ids=true | all-gather | bytes 266240 | tf_op jit(solution)/shard_map/all_gather | solution.py:90
  160.0 47.0 %all_gather.20 = f32[256,2,64]{2,1,0:T(2,128)} all-gather(f32[4,2,64]{2,1,0:T(2,128)S(1)} %bitcast_reduce_fusion.6), channel_id=1, replica_groups=mesh['leaf'=64,'rhs'=4] {'leaf'}, dimensions={0}, use_global_device_ids=true | all-gather | bytes 133120 | tf_op jit(solution)/shard_map/all_gather | solution.py:90
  207.2 50.9 %all_gather.21 = f32[128,2,64]{2,1,0:T(2,128)} all-gather(f32[2,2,64]{2,1,0:T(2,128)S(1)} %bitcast_reduce_fusion.7), channel_id=1, replica_groups=mesh['leaf'=64,'rhs'=4] {'leaf'}, dimensions={0}, use_global_device_ids=true | all-gather | bytes 66560 | tf_op jit(solution)/shard_map/all_gather | solution.py:90
  261.5 5.4 copy.29
  267.4 3.5 copy.30
  271.5 3.7 copy.31
  277.2 3.5 copy.32
  283.2 3.6 copy.42
  286.8 50.1 %all_gather.22 = f32[128,2,64]{2,1,0:T(2,128)S(1)} all-gather(f32[2,2,64]{2,1,0:T(2,128)S(1)} %fusion.37), channel_id=1, replica_groups=mesh['leaf'=64,'rhs'=4] {'leaf'}, dimensions={0}, use_global_device_ids=true | all-gather | bytes 66560 | tf_op jit(solution)/shard_map/all_gather | solution.py:90
  361.0 4.3 bitcast_reduce_fusion.2
  365.8 6.9 %bitcast_reduce_fusion.1 = f32[16,2,64]{2,1,0:T(2,128)S(1)} fusion(f32[128,64,64]{2,1,0:T(8,128)S(1)} %bitcast.134, f32[128,2,64]{2,1,0:T(2,128)S(1)} %copy-done.7, pred[128]{0:T(512)(128)(4,1)S(1)} %copy-done.12), kind=kOutput, calls=%fused_computation.60 | convolution fusion | flops 12613632 | bytes 2171008 | tf_op jit(solution)/shard_map/vde,vte->vdt/dot_general | solution.py:99
  376.0 239.6 %while.12 = (s32[]{:T(128)}, f32[8,16,256]{2,0,1:T(8,128)S(1)}, s32[]{:T(128)}, s32[16,9]{0,1:T(8,128)}, s32[]{:T(128)}, /*index=5*/f32[8,26,1024]{2,0,1:T(8,128...) while((s32[]{:T(128)}, f32[8,16,256]{2,0,1:T(8,128)S(1)}, ...), condition=%wide.region_10.11_spmd, body=%wide.region_9.10_spmd.sunk | while | flops 432244224 | bytes 3052711 | solution.py:70
  379.7 22.9 %fusion.111 = f32[8,16,256]{2,0,1:T(8,128)S(1)} fusion(f32[8,16,256]{2,0,1:T(8,128)S(1)} %get-tuple-element.294, f32[16]{0:T(128)S(1)} %compare_select_fusion.21, f32[16,1024]{1,0:T(8,128)S(1)} %get-tuple-element.278, f32[16,256]{1,0:T(8,128)S(1)} %get-tuple-element.314, f32[16,1024]{1,0:T(8,128)S(1)} %get-tuple-element.279, ...), kind=kOutput, calls=%fused_computation.24.clone.1 | convolution fusion | flops 432177152 | bytes 950352 | tf_op jit(solution)/shard_map/while/body/atp,cap->cat/dot_general | solution.py:68
  406.2 22.9 %fusion.111 = f32[8,16,256]{2,0,1:T(8,128)S(1)} fusion(f32[8,16,256]{2,0,1:T(8,128)S(1)} %get-tuple-element.294, f32[16]{0:T(128)S(1)} %compare_select_fusion.21, f32[16,1024]{1,0:T(8,128)S(1)} %get-tuple-element.278, f32[16,256]{1,0:T(8,128)S(1)} %get-tuple-element.314, f32[16,1024]{1,0:T(8,128)S(1)} %get-tuple-element.279, ...), kind=kOutput, calls=%fused_computation.24.clone.1 | convolution fusion | flops 432177152 | bytes 950352 | tf_op jit(solution)/shard_map/while/body/atp,cap->cat/dot_general | solution.py:68
  432.8 22.9 %fusion.111 = f32[8,16,256]{2,0,1:T(8,128)S(1)} fusion(f32[8,16,256]{2,0,1:T(8,128)S(1)} %get-tuple-element.294, f32[16]{0:T(128)S(1)} %compare_select_fusion.21, f32[16,1024]{1,0:T(8,128)S(1)} %get-tuple-element.278, f32[16,256]{1,0:T(8,128)S(1)} %get-tuple-element.314, f32[16,1024]{1,0:T(8,128)S(1)} %get-tuple-element.279, ...), kind=kOutput, calls=%fused_computation.24.clone.1 | convolution fusion | flops 432177152 | bytes 950352 | tf_op jit(solution)/shard_map/while/body/atp,cap->cat/dot_general | solution.py:68
  459.3 22.9 %fusion.111 = f32[8,16,256]{2,0,1:T(8,128)S(1)} fusion(f32[8,16,256]{2,0,1:T(8,128)S(1)} %get-tuple-element.294, f32[16]{0:T(128)S(1)} %compare_select_fusion.21, f32[16,1024]{1,0:T(8,128)S(1)} %get-tuple-element.278, f32[16,256]{1,0:T(8,128)S(1)} %get-tuple-element.314, f32[16,1024]{1,0:T(8,128)S(1)} %get-tuple-element.279, ...), kind=kOutput, calls=%fused_computation.24.clone.1 | convolution fusion | flops 432177152 | bytes 950352 | tf_op jit(solution)/shard_map/while/body/atp,cap->cat/dot_general | solution.py:68
  485.9 22.9 %fusion.111 = f32[8,16,256]{2,0,1:T(8,128)S(1)} fusion(f32[8,16,256]{2,0,1:T(8,128)S(1)} %get-tuple-element.294, f32[16]{0:T(128)S(1)} %compare_select_fusion.21, f32[16,1024]{1,0:T(8,128)S(1)} %get-tuple-element.278, f32[16,256]{1,0:T(8,128)S(1)} %get-tuple-element.314, f32[16,1024]{1,0:T(8,128)S(1)} %get-tuple-element.279, ...), kind=kOutput, calls=%fused_computation.24.clone.1 | convolution fusion | flops 432177152 | bytes 950352 | tf_op jit(solution)/shard_map/while/body/atp,cap->cat/dot_general | solution.py:68
  512.4 22.9 %fusion.111 = f32[8,16,256]{2,0,1:T(8,128)S(1)} fusion(f32[8,16,256]{2,0,1:T(8,128)S(1)} %get-tuple-element.294, f32[16]{0:T(128)S(1)} %compare_select_fusion.21, f32[16,1024]{1,0:T(8,128)S(1)} %get-tuple-element.278, f32[16,256]{1,0:T(8,128)S(1)} %get-tuple-element.314, f32[16,1024]{1,0:T(8,128)S(1)} %get-tuple-element.279, ...), kind=kOutput, calls=%fused_computation.24.clone.1 | convolution fusion | flops 432177152 | bytes 950352 | tf_op jit(solution)/shard_map/while/body/atp,cap->cat/dot_general | solution.py:68
  539.0 22.9 %fusion.111 = f32[8,16,256]{2,0,1:T(8,128)S(1)} fusion(f32[8,16,256]{2,0,1:T(8,128)S(1)} %get-tuple-element.294, f32[16]{0:T(128)S(1)} %compare_select_fusion.21, f32[16,1024]{1,0:T(8,128)S(1)} %get-tuple-element.278, f32[16,256]{1,0:T(8,128)S(1)} %get-tuple-element.314, f32[16,1024]{1,0:T(8,128)S(1)} %get-tuple-element.279, ...), kind=kOutput, calls=%fused_computation.24.clone.1 | convolution fusion | flops 432177152 | bytes 950352 | tf_op jit(solution)/shard_map/while/body/atp,cap->cat/dot_general | solution.py:68
  565.5 22.9 %fusion.111 = f32[8,16,256]{2,0,1:T(8,128)S(1)} fusion(f32[8,16,256]{2,0,1:T(8,128)S(1)} %get-tuple-element.294, f32[16]{0:T(128)S(1)} %compare_select_fusion.21, f32[16,1024]{1,0:T(8,128)S(1)} %get-tuple-element.278, f32[16,256]{1,0:T(8,128)S(1)} %get-tuple-element.314, f32[16,1024]{1,0:T(8,128)S(1)} %get-tuple-element.279, ...), kind=kOutput, calls=%fused_computation.24.clone.1 | convolution fusion | flops 432177152 | bytes 950352 | tf_op jit(solution)/shard_map/while/body/atp,cap->cat/dot_general | solution.py:68
  592.1 22.9 %fusion.111 = f32[8,16,256]{2,0,1:T(8,128)S(1)} fusion(f32[8,16,256]{2,0,1:T(8,128)S(1)} %get-tuple-element.294, f32[16]{0:T(128)S(1)} %compare_select_fusion.21, f32[16,1024]{1,0:T(8,128)S(1)} %get-tuple-element.278, f32[16,256]{1,0:T(8,128)S(1)} %get-tuple-element.314, f32[16,1024]{1,0:T(8,128)S(1)} %get-tuple-element.279, ...), kind=kOutput, calls=%fused_computation.24.clone.1 | convolution fusion | flops 432177152 | bytes 950352 | tf_op jit(solution)/shard_map/while/body/atp,cap->cat/dot_general | solution.py:68
  616.3 4.4 all-to-all-start
  621.7 5.0 all-to-all-done
  627.0 4.9 fusion.30
  (187 shorter events, 75.6 us)
Async XLA Ops:
  15.6 358.0 %collective-permute-start.1 = (f32[10,5120]{1,0:T(8,128)}, f32[10,5120]{1,0:T(8,128)}, u32[]{:S(2)}, u32[]{:S(2)}) collective-permute-start(f32[10,5120]{1,0:T(8,128)} %get-tuple-element.197), channel_id=1, source_target_pairs={{4,0},{8,4},{12,8},{16,12},{20,16},{24,20},{28,24},{32,28},{36,32}... | collective-permute-start | bytes 614408 | tf_op jit(solution)/shard_map/ppermute | solution.py:23
  21.5 352.0 %collective-permute-start = (f32[10,5120]{1,0:T(8,128)}, f32[10,5120]{1,0:T(8,128)}, u32[]{:S(2)}, u32[]{:S(2)}) collective-permute-start(f32[10,5120]{1,0:T(8,128)} %get-tuple-element.196), channel_id=1, source_target_pairs={{0,4},{4,8},{8,12},{12,16},{16,20},{20,24},{24,28},{28,32},{32,36}... | collective-permute-start | bytes 614408 | tf_op jit(solution)/shard_map/ppermute | solution.py:22
  25.9 5.4 copy-start
  31.3 3.1 copy-start.5
  31.3 3.2 copy-start.8
  41.2 165.8 %copy-start.4 = (f32[2,2,64,64]{3,2,1,0:T(8,128)}, f32[2,2,64,64]{3,2,1,0:T(8,128)S(1)}, u32[]{:S(2)}) copy-start(f32[2,2,64,64]{3,2,1,0:T(8,128)S(1)} %slice.81) | copy-start | bytes 196612
  42.6 5.5 copy-start.1
  42.6 5.5 copy-start.6
  48.0 211.5 %copy-start.9 = (s32[16,9]{1,0:T(8,128)S(1)}, s32[16,9]{1,0:T(8,128)}, u32[]{:S(2)}) copy-start(s32[16,9]{1,0:T(8,128)} %param.16) | copy-start | bytes 1732
  48.0 212.2 %copy-start.3 = (f32[2,16384]{1,0:T(2,128)S(1)}, f32[2,16384]{1,0:T(2,128)}, u32[]{:S(2)}) copy-start(f32[2,16384]{1,0:T(2,128)} %param.10) | copy-start | bytes 393220
  352.1 13.7 %copy-start.2 = (f32[2,64,64,64]{3,2,1,0:T(8,128)S(1)}, f32[2,64,64,64]{3,2,1,0:T(8,128)}, u32[]{:S(2)}) copy-start(f32[2,64,64,64]{3,2,1,0:T(8,128)} %copy.29) | copy-start | bytes 6291460
  352.1 13.7 %copy-start.7 = (f32[128,2,64]{2,1,0:T(2,128)S(1)}, f32[128,2,64]{2,1,0:T(2,128)}, u32[]{:S(2)}) copy-start(f32[128,2,64]{2,1,0:T(2,128)} %gather_fusion.2) | copy-start | bytes 196612
  352.1 13.7 %copy-start.12 = (pred[128]{0:T(512)(128)(4,1)S(1)}, pred[128]{0:T(512)(128)(4,1)}, u32[]{:S(2)}) copy-start(pred[128]{0:T(512)(128)(4,1)} %compare_and_fusion.4) | copy-start | bytes 388
  354.3 18.4 %copy-start.10 = (f32[16]{0:T(128)S(1)}, f32[16]{0:T(128)}, u32[]{:S(2)}) copy-start(f32[16]{0:T(128)} %get-tuple-element.200) | copy-start | bytes 196
  354.3 18.4 %copy-start.11 = (f32[16]{0:T(128)S(1)}, f32[16]{0:T(128)}, u32[]{:S(2)}) copy-start(f32[16]{0:T(128)} %get-tuple-element.201) | copy-start | bytes 196
  372.7 3.3 copy-start.13
  616.3 10.4 %all-to-all-start = ((f32[8,16,256]{2,1,0:T(8,128)}), f32[8,16,256]{2,1,0:T(8,128)S(1)}, u32[]{:S(2)}, u32[]{:S(2)}) async-start(f32[8,16,256]{2,1,0:T(8,128)} %copy.37), calls=%async_computation | async-start | bytes 262144 | tf_op jit(solution)/shard_map/all_to_all | solution.py:76
where the time goes:
time: 642 us; the launch traced here: 632 us
  blocking collectives  269 us (42%)
  matrix products  237 us (37%)
  local copies, waits for them, and re-layouts  71.5 us (11%)
  other arithmetic  29.7 us (5%)
  starting transfers between devices  12.3 us (2%)
  loops' own time  7.16 us (1%)
    all_gather x5, blocking collectives, shards(): lax.all_gather(piece, 'leaf', axis=0, tiled=True)  255 us
    dot_general x9, matrix products, add_slot(): jnp.einsum('atp,cap->cat', kernel, source_charge, precision=TOP_PRECISION)  206 us
    slice x8, local copies, waits for them, and re-layouts, shards(): coupling[:, offset:offset + slot_count].reshape(-1, basis_rank, basis_rank)  35.4 us
    dot_general x5, matrix products, shards(): jnp.einsum('vde,vte->vdt', selected, local_blocks, precision=TOP_PRECISION)  17.7 us
    all_gather x1, blocking collectives, shards(): all_charges = lax.all_gather(charges, 'rhs', axis=0, tiled=True)  13.5 us
  transfers between devices with their start and end apart: 3, of which 1 were waited for; matrix products, arithmetic and copies ran while one was open for 15% of the time, Pallas kernels for 0%

commit v1 on v0

v1 whole, which is shorter than its diff:
```python
import functools

import jax
import jax.numpy as jnp
from jax import lax
from jax.experimental import pallas as pl
from jax.experimental.pallas import tpu as pltpu
from jax.sharding import PartitionSpec as P

F = jnp.float32
B = jnp.bfloat16
NN = (((1,), (0,)), ((), ()))
NT = (((1,), (1,)), ((), ()))
HI = lax.Precision.HIGHEST

FAR = 8
STRIP = 4
LEAVES = 16
PTS = 1024
QUART = 256
RANK = 64
NEAR = 9
RHS = 4
NX, NZ, NC = 4, 8, 2
LEVEL_ROW = (0, 16, 24, 28, 30)
TRANSFER_OFFSETS = (0, 8, 12, 14)
RATE = -4.0 * 1.4426950408889634
S_LIMB = (0, 0, 1, 1, 0, 2, 1, 2)
T_LIMB = (0, 1, 0, 1, 2, 0, 2, 1)
PAIRS = 124
WINDOWS = 6
OVER = 152
ANY = pl.BlockSpec(memory_space=pl.ANY)
HBM = pl.BlockSpec(memory_space=pltpu.HBM)
VMEM = pl.BlockSpec(memory_space=pltpu.VMEM)
SMEM = pl.BlockSpec(memory_space=pltpu.SMEM)
PARAMS = pltpu.CompilerParams(vmem_limit_bytes=48 * 2**20)


def dot(a, b, dims):
    return lax.dot_general(a, b, dims, preferred_element_type=F)


def dot_hi(a, b, dims):
    return lax.dot_general(a, b, dims, preferred_element_type=F, precision=HI)


def call(kernel, outs, in_specs, scratch=(), micros=1.0, smem_outs=0):
    outs = [v if isinstance(v, jax.ShapeDtypeStruct) else jax.ShapeDtypeStruct(v, F) for v in outs]
    return pl.pallas_call(
        kernel,
        out_shape=outs,
        in_specs=in_specs,
        out_specs=[SMEM if n < smem_outs else VMEM for n in range(len(outs))],
        scratch_shapes=list(scratch),
        compiler_params=PARAMS,
        cost_estimate=pl.CostEstimate(
            flops=int(micros * 10**9), bytes_accessed=10**5, transcendentals=0
        ),
    )


def pre_kernel(meta, coords_hbm, charges_hbm, own, first, second, place, coords, charges, sems):
    copies = [
        pltpu.make_async_copy(charges_hbm, charges, sems.at[0]),
        pltpu.make_async_copy(coords_hbm, coords, sems.at[1]),
    ]
    for copy in copies:
        copy.start()
    r = meta[1]
    copies[0].wait()
    for k, (ref, at) in enumerate(((own, 0), (first, 0), (second, 0), (first, 2))):
        q = (r ^ k) * QUART
        for i in range(LEAVES):
            source = pl.ds(pl.multiple_of(q + i * PTS, QUART), QUART)
            ref[at : at + 2, i * QUART : (i + 1) * QUART] = charges[:, source]
    copies[1].wait()
    for i in range(LEAVES):
        source = pl.ds(pl.multiple_of(r * QUART + i * PTS, QUART), QUART)
        place[:, i * QUART : (i + 1) * QUART] = coords[:, source]


def limbs(v):
    first = v.astype(B).astype(F)
    rest = v - first
    second = rest.astype(B).astype(F)
    return first, second, rest - second


def pick(row, values, rest):
    out = rest
    for n, v in reversed(list(enumerate(values))):
        out = jnp.where(row == n, v, out)
    return out


def source_rows(x, y):
    shape = (8, x.shape[1])
    row = lax.broadcasted_iota(jnp.int32, shape, 0)
    x, y = jnp.broadcast_to(x, shape), jnp.broadcast_to(y, shape)
    lx, ly, ls = limbs(-2.0 * x), limbs(-2.0 * y), limbs(x * x + y * y)
    zero = jnp.zeros(shape, F)
    one = zero + 1.0
    return jnp.concatenate(
        [
            pick(row, [lx[a] for a in S_LIMB], zero),
            pick(row, [ly[a] for a in S_LIMB], zero),
            pick(row, [one, one, one, *ls], zero),
            pick(row, [*lx, *ly], zero),
        ],
        axis=0,
    )


def target_rows(x, y):
    shape = (8, x.shape[1])
    row = lax.broadcasted_iota(jnp.int32, shape, 0)
    lx, ly = (limbs(jnp.broadcast_to(v, shape)) for v in (x, y))
    zero = jnp.zeros(shape, F)
    return jnp.concatenate(
        [pick(row, [lx[b] for b in T_LIMB], zero), pick(row, [ly[b] for b in T_LIMB], zero)], axis=0
    ).astype(B)


def prep_kernel(meta, list_hbm, count_hbm, coords, place, _, lists, sf, tab, near_list, near_count, sems):
    copies = [
        pltpu.make_async_copy(list_hbm, near_list, sems.at[0]),
        pltpu.make_async_copy(count_hbm, near_count, sems.at[1]),
    ]
    for copy in copies:
        copy.start()
    for n in range(4):
        xy = place[:, 4 * n * QUART : 4 * (n + 1) * QUART] - 0.5
        put_sources(xy, sf, 4 * n)
    for i in range(LEAVES):
        xy = coords[:, i * PTS : (i + 1) * PTS] - 0.5
        tab[i] = target_rows(xy[0:1], xy[1:2])
    for copy in copies:
        copy.wait()
    first = meta[0]

    def leaf_pairs(i, counts):
        def slot(s, counts):
            local = near_list[i, s] - first
            before, after = local < 0, local >= LEAVES
            over = (before | after).astype(jnp.int32)
            p = jnp.where(over == 1, OVER + counts[1], counts[0])
            lists[0, p] = i
            lists[1, p] = jnp.where(before, local + 20, jnp.where(after, local + 4, local))
            lists[2, p] = i
            lists[3, p] = lax.shift_right_arithmetic(local, 2) - lax.shift_right_arithmetic(i, 2)
            lists[4, p] = (local & 3) - (i & 3)
            return counts[0] + 1 - over, counts[1] + over

        return lax.fori_loop(0, near_count[i], slot, counts)

    inside, over = lax.fori_loop(0, LEAVES, leaf_pairs, (jnp.int32(0), jnp.int32(0)))
    lists[5, 0] = inside
    lists[5, 1] = over
    for p in range(4):
        for field in range(5):
            lists[field, OVER + over + p] = LEAVES if field == 2 else 0


def put_sources(xy, sf, at):
    rows = source_rows(xy[0:1], xy[1:2])
    rows = jnp.concatenate([rows[:, n * QUART : (n + 1) * QUART] for n in range(4)], axis=0)
    turned = rows.T
    for n in range(4):
        sf[at + n] = turned[:, n * 32 : (n + 1) * 32].astype(B)


def weights(c):
    high = c.astype(B).astype(F)
    return jnp.concatenate([high, c - high], axis=0).astype(B)


def near_kernel(w, n_carried, *refs):
    refs = list(refs)

    def take(n):
        taken = refs[:n]
        del refs[:n]
        return taken

    last = w == WINDOWS - 1
    lists, coords, tab, sf = take(4)
    if w == 0:
        own, first, second, place = take(4)
    else:
        cw, acc_in = take(2)
    if w >= 4:
        halos = take(2)
    carried = take(n_carried)
    outs = take(4 if last else 1)
    if w == 0:
        cw, to_before, to_after = take(3)
    for ref, out in zip(carried, take(n_carried)):
        out[...] = ref[...]
    kh_a, kl_a, kh_b, kl_b = take(4)
    acc = take(1)[0] if last else outs[0]

    if w == 0:
        whole = jnp.concatenate([own[...], first[...], second[...]], axis=0)
        whole = jnp.concatenate([whole[0:4], whole[6:10]], axis=0)
        for j in range(LEAVES):
            cw[j] = weights(whole[:, j * QUART : (j + 1) * QUART])
        for ref, at in ((to_before, slice(0, 4 * QUART)), (to_after, slice(12 * QUART, 16 * QUART))):
            ref[0:2] = place[:, at]
            ref[2:10] = whole[:, at]
        acc[...] = jnp.zeros_like(acc)
    else:
        acc[...] = acc_in[...]
    if w >= 4:
        sf_own, cw_own = sf, cw
        sf, cw = take(2)
        sf[0:LEAVES] = sf_own[...]
        cw[0:LEAVES] = cw_own[...]
        for n, halo in enumerate(halos):
            put_sources(halo[0:2] - 0.5, sf, LEAVES + 4 * n)
            for j in range(4):
                cw[LEAVES + 4 * n + j] = weights(halo[2:10, j * QUART : (j + 1) * QUART])
    kh_b[...] = jnp.zeros_like(kh_b)
    kl_b[...] = jnp.zeros_like(kl_b)

    inside = lists[5, 0]
    total = inside + lists[5, 1]

    def bound(n):
        if n == 0:
            return jnp.int32(0)
        if n == WINDOWS:
            return total
        at = lax.div(total * n, WINDOWS)
        return (jnp.minimum(at, inside) if n <= 4 else at) & -2

    begin, end = bound(w), bound(w + 1)

    def entry(p):
        return jnp.where(p < inside, p, p - inside + OVER)

    row = lax.broadcasted_iota(jnp.int32, (8, PTS), 0)
    low, middle = row < 3, (row >= 3) & (row < 6)
    ones = jnp.where(middle, 1.0, 0.0)

    def evaluate(p, kh, kl):
        p = entry(p)
        i, j = lists[0, p], lists[1, p]
        ox, oy = lists[3, p].astype(F), lists[4, p].astype(F)
        xy = coords[:, pl.ds(pl.multiple_of(i * PTS, PTS), PTS)] - 0.5
        x = jnp.broadcast_to(xy[0:1], (8, PTS)) - ox
        y = jnp.broadcast_to(xy[1:2], (8, PTS)) - oy
        ls = limbs(x * x + y * y)
        squares = pick(row, ls, ones)
        offsets = jnp.where(low, -ox, jnp.where(middle, -oy, 0.0))
        t_rows = jnp.concatenate(
            [tab[i], jnp.concatenate([squares, offsets], axis=0).astype(B)], axis=0
        )
        s_rows = sf[j]
        for c in range(4):
            lanes = slice(c * 256, (c + 1) * 256)
            dist2 = dot(s_rows, t_rows[:, lanes], NN)
            for g in range(16):
                at = slice(g * 16, (g + 1) * 16)
                d2 = jnp.maximum(dist2[at], 1e-35)
                k = jnp.exp2((d2 * lax.rsqrt(d2)) * RATE)
                high = k.astype(B)
                kh[at, lanes] = high
                kl[at, lanes] = (k - high.astype(F)).astype(B)

    def multiply(p, kh, kl):
        p = entry(p)
        c = cw[lists[1, p]]
        acc[lists[2, p]] += dot(c, kh[...], NN) + dot(c, kl[...], NN)

    def step(n, _):
        p = begin + 2 * n
        evaluate(p, kh_a, kl_a)
        multiply(jnp.maximum(p - 1, 0), kh_b, kl_b)
        evaluate(p + 1, kh_b, kl_b)
        multiply(p, kh_a, kl_a)
        return 0

    steps = (end - begin + 1) // 2
    lax.fori_loop(0, steps, step, 0)
    multiply(jnp.maximum(begin + 2 * steps - 1, 0), kh_b, kl_b)

    if last:
        for i in range(LEAVES):
            v = (acc[i, 0:8, :] + acc[i, 8:16, :]) * (PTS**-0.5)
            for k in range(RHS):
                outs[k][:, i * PTS : (i + 1) * PTS] = v[2 * k : 2 * k + 2]


def bf16(*shape):
    return jax.ShapeDtypeStruct(shape, B)


def split_rows(v):
    high = v.astype(B).astype(F)
    return jnp.concatenate([high, v - high], axis=0).astype(B)


def split_dot(rows, matrix, dims):
    high = matrix.astype(B)
    low = (matrix - high.astype(F)).astype(B)
    v = dot(rows, high, dims) + dot(rows, low, dims)
    return v[0:8] + v[8:16]


def up_kernel(charges, basis, transfer, _, out):
    row = lax.broadcasted_iota(jnp.int32, (8, PTS), 0)

    def put(at, v):
        out[at : at + 1, 0:RANK] = v[0:1]
        out[at : at + 1, RANK : 2 * RANK] = v[1:2]

    current = []
    for i in range(LEAVES):
        c = charges[:, i * PTS : (i + 1) * PTS]
        c = jnp.where(row == 0, c[0:1], jnp.where(row == 1, c[1:2], 0.0))
        v = split_dot(split_rows(c), basis[i], NT)
        put(i, v)
        current.append(v)
    for level in range(1, 5):
        per_block = 8 >> (level - 1)
        lifted = [
            dot_hi(v, transfer[d // per_block, TRANSFER_OFFSETS[level - 1] + d % per_block], NN)
            for d, v in enumerate(current)
        ]
        current = [lifted[d] + lifted[d + 1] for d in range(0, len(lifted), 2)]
        for d, v in enumerate(current):
            put(LEVEL_ROW[level] + d, v)
    out[31:32, :] = jnp.zeros((1, 2 * RANK), F)


def couple(block, rows, table, coupling, picked, products):
    picked[120:128, :] = jnp.zeros((8, 2 * RANK), F)
    for q in range(PAIRS):
        picked[q : q + 1, :] = table[pl.ds(rows[block, q], 1), :]
    turned = picked[...].T
    g = [turned[c * RANK : (c + 1) * RANK, 0:PAIRS] for c in range(2)]

    def part(n, _):
        at = pl.ds(pl.multiple_of(n * 8, 8), 8)
        b = coupling[block, at]
        for c in range(2):
            products[c, at, :] = jnp.sum(b * g[c][None], axis=1)
        return 0

    lax.fori_loop(0, RANK // 8, part, 0)
    pair = lax.broadcasted_iota(jnp.int32, (16, PAIRS), 1)
    target = lax.broadcasted_iota(jnp.int32, (16, PAIRS), 0)
    member = jnp.where(lax.shift_right_arithmetic(pair, 3) == target, 1.0, 0.0)
    return [dot_hi(member, products[c], NT) for c in range(2)]


def first_kernel(rows, own, other, coupling, carried, table, out, carry, picked, products):
    half = own.shape[0]
    table[0:half, :] = own[...]
    table[half : 2 * half, :] = other[...]
    carry[...] = carried[...]
    for c, t in enumerate(couple(0, rows, table, coupling, picked, products)):
        out[c] = t


def second_kernel(rows, table, coupling, start, transfer, carried, out, carry, picked, products, held):
    carry[...] = carried[...]
    held[...] = jnp.zeros_like(held)
    for c, t in enumerate(couple(1, rows, table, coupling, picked, products)):
        for n in range(16):
            held[n, c : c + 1, :] = start[c, n : n + 1, :]
            held[16 + n, c : c + 1, :] = t[n : n + 1]
    current = [held[15] + held[31]]
    first = (0, 8, 12, 14)
    for level in range(4, 0, -1):
        per_block = 8 >> (level - 1)
        current = [
            held[16 * (d // per_block) + first[level - 1] + d % per_block]
            + dot_hi(
                current[d // 2],
                transfer[d // per_block, TRANSFER_OFFSETS[level - 1] + d % per_block],
                NT,
            )
            for d in range(2 * per_block)
        ]
    for i in range(LEAVES):
        out[i] = current[i]


def expand_kernel(coefficients, basis, _, out):
    for i in range(LEAVES):
        v = split_dot(split_rows(coefficients[i]), basis[i], NN)
        out[:, i * PTS : (i + 1) * PTS] = v[0:2]


def shards(coords, charges, leaf_basis, transfer, coupling, far_pairs, near_list, near_count):
    device = lax.axis_index("leaf").astype(jnp.int32)
    rhs_index = lax.axis_index("rhs").astype(jnp.int32)
    meta = jnp.stack([device * LEAVES, rhs_index])
    count = NX * NZ * NC

    def swap_rhs(v, k):
        return lax.ppermute(v, "rhs", [(i, i ^ k) for i in range(RHS)])

    def swap_leaf(v, bit):
        return lax.ppermute(v, "leaf", [(d, d ^ bit) for d in range(count)])

    own, first, second, place = call(
        pre_kernel,
        [(2, LEAVES * QUART), (4, LEAVES * QUART), (2, LEAVES * QUART), (2, LEAVES * QUART)],
        [SMEM, HBM, HBM],
        [
            pltpu.VMEM((2, LEAVES * PTS), F),
            pltpu.VMEM((2, LEAVES * PTS), F),
            pltpu.SemaphoreType.DMA((2,)),
        ],
    )(meta, coords, charges)
    first = swap_rhs(first, 1)
    lists, sf, tab = call(
        prep_kernel,
        [jax.ShapeDtypeStruct((6, 320), jnp.int32), bf16(LEAVES, QUART, 32), bf16(LEAVES, 16, PTS)],
        [SMEM, HBM, HBM, VMEM, VMEM, ANY],
        [
            pltpu.SMEM((LEAVES, NEAR), jnp.int32),
            pltpu.SMEM((LEAVES,), jnp.int32),
            pltpu.SemaphoreType.DMA((2,)),
        ],
        micros=4,
        smem_outs=1,
    )(meta, near_list, near_count, coords, place, own)
    onward = jnp.concatenate([second, first[2:4]], 0)
    second = swap_rhs(onward, 2)
    (table,) = call(up_kernel, [(32, 2 * RANK)], [VMEM] * 3 + [ANY], micros=4)(
        charges, leaf_basis, transfer, onward
    )

    acc_shape, halo_shape = (LEAVES + 1, 16, PTS), (10, 4 * QUART)
    values = [pltpu.VMEM((QUART, PTS), B)] * 4
    after = table
    halos = []
    for w, bit in enumerate((2, 4, 8, 16, 32, 1)):
        swapped = swap_leaf(after, bit)
        carried = [after] if w < WINDOWS - 1 else []
        data, extra, scratch = [lists, coords, tab, sf], [], [*values]
        if w == 0:
            data += [own, first, second, place]
            extra = [bf16(LEAVES, 16, QUART), halo_shape, halo_shape]
        else:
            data += [cw, acc]
        if w == 1:
            carried.append(to_after)
        if w == WINDOWS - 1:
            scratch.append(pltpu.VMEM(acc_shape, F))
        if w >= 4:
            data += halos
            scratch += [pltpu.VMEM((24, QUART, 32), B), pltpu.VMEM((24, 16, QUART), B)]
        outs = [(2, LEAVES * PTS)] * 4 if w == WINDOWS - 1 else [acc_shape]
        data += carried
        result = call(
            functools.partial(near_kernel, w, len(carried)),
            [*outs, *extra, *(v.shape for v in carried)],
            [SMEM] + [VMEM] * (len(data) - 1),
            scratch,
            micros=9,
        )(*data)
        if w == WINDOWS - 1:
            whole = result
            break
        acc = result[0]
        if w == 0:
            cw, to_before, to_after = result[1:4]
            up = lax.ppermute(to_before, "leaf", [(i + 1, i) for i in range(count - 1)])
        if w == 1:
            down = lax.ppermute(result[2], "leaf", [(i, i + 1) for i in range(count - 1)])
            halos = [down, up]
        after = jnp.concatenate([result[1 + len(extra)], swapped], 0)
    other = swapped

    level = jnp.asarray([k for k in range(5) for _ in range(64 >> k)], jnp.int32)[None, :]
    owner = lax.shift_right_logical(far_pairs, 4 - level)
    inside = far_pairs & (lax.shift_left(jnp.int32(1), 4 - level) - 1)
    start = jnp.asarray([LEVEL_ROW[k] for k in range(5) for _ in range(64 >> k)], jnp.int32)[None, :]
    apart = device ^ owner
    rows = ((apart & 1) * (count // 2) + (apart >> 1)) * 32 + start + inside
    back = [swap_rhs(whole[2], 2)]
    coupling = coupling.transpose(0, 2, 3, 1)
    scratch = [pltpu.VMEM((128, 2 * RANK), F), pltpu.VMEM((2, RANK, PAIRS), F)]
    table, upper, passed = call(
        first_kernel,
        [(2048, 2 * RANK), (2, 16, RANK), (2, LEAVES * PTS)],
        [SMEM] + [VMEM] * 4,
        scratch,
        micros=0.5,
    )(rows, after, other, coupling, whole[1])
    back.append(swap_rhs(passed, 1))
    coefficients, passed = call(
        second_kernel,
        [(LEAVES, 8, RANK), (2, LEAVES * PTS)],
        [SMEM] + [VMEM] * 5,
        [*scratch, pltpu.VMEM((32, 8, RANK), F)],
        micros=0.5,
    )(rows, table, coupling, upper, transfer, whole[3])
    back.append(swap_rhs(passed, 3))
    (distant,) = call(
        expand_kernel, [(2, LEAVES * PTS)], [VMEM] * 2 + [ANY], micros=0.3
    )(coefficients, leaf_basis, passed)
    return distant + whole[0] + back[0] + back[1] + back[2]


def solution(mesh):
    return jax.shard_map(
        shards,
        mesh=mesh,
        in_specs=(
            P(None, "leaf"),
            P("rhs", "leaf"),
            P("leaf", None, None),
            P("leaf", None, None, None),
            P("leaf", None, None, None),
            P("leaf", None),
            P("leaf", None),
            P("leaf"),
        ),
        out_specs=P("rhs", "leaf"),
        check_vma=False,
    )
```

time: 642 us -> 108 us (0.17); the launches traced: 632 us -> 107 us
  blocking collectives: 269 us -> 0 us
  matrix products: 237 us -> 0 us
  Pallas kernels: 0 us -> 73.8 us
  local copies, waits for them, and re-layouts: 71.5 us -> 2 us
  other arithmetic: 29.7 us -> 0.92 us
  starting transfers between devices: 12.3 us -> 23.5 us
  loops' own time: 7.16 us -> 0 us
    all_gather x6 -> x0, blocking collectives: 269 us -> none  [the longest x5 255 us: shards(): lax.all_gather(piece, 'leaf', axis=0, tiled=True)]
    dot_general x24 -> x0, matrix products: 237 us -> none  [the longest x9 206 us: add_slot(): jnp.einsum('atp,cap->cat', kernel, source_charge, precision=TOP_PRECISION)]
    pallas_call x0 -> x12, Pallas kernels: none -> 73.8 us  [the longest x6 57 us: shards(): call(functools.partial(near_kernel, w, len(carried)), [*outs, *extra, *(v...]
    slice x25 -> x1, local copies, waits for them, and re-layouts: 37.5 us -> 0.02 us  [shards(): onward = jnp.concatenate([second, first[2:4]], 0)]
    gather x23 -> x0, local copies, waits for them, and re-layouts: 22.2 us -> none  [the longest x5 10.8 us: shards(): selected = jnp.take(gathered[height], sources, axis=0)]
    ppermute x2 -> x13, starting transfers between devices: 7.85 us -> 23.5 us  [the longest x5 8.31 us: swap_rhs(): return lax.ppermute(v, 'rhs', [(i, i ^ k) for i in range(RHS)])]
    another operation x1 -> x0, loops' own time: 7.16 us -> none  [shards(): lax.fori_loop(0, jnp.max(near_count), add_slot, jnp.zeros((ext_charges.sh...]
    add x28 -> x2, other arithmetic: 7.82 us -> 0.81 us  [the longest x1 0.79 us: shards(): return distant + whole[0] + back[0] + back[1] + back[2]]
  transfers between devices with their start and end apart: 3 -> 13, of which waited for: 1 -> 1; matrix products, arithmetic and copies ran while one was open for 15% -> 0% of each run, Pallas kernels for 0% -> 68%
where the time goes in v1:
time: 108 us; the launch traced here: 107 us
  Pallas kernels  73.8 us (68%)
  starting transfers between devices  23.5 us (22%)
  waiting for transfers between devices  6.11 us (6%)
  local copies, waits for them, and re-layouts  2 us (2%)
    pallas_call x6, Pallas kernels, shards(): call(functools.partial(near_kernel, w, len(carried)), [*outs, *extra, *(v...  57 us
    ppermute x5, starting transfers between devices, swap_rhs(): return lax.ppermute(v, 'rhs', [(i, i ^ k) for i in range(RHS)])  8.31 us
    ppermute x6, starting transfers between devices, swap_leaf(): return lax.ppermute(v, 'leaf', [(d, d ^ bit) for d in range(count)])  7.47 us
    ppermute x5, waiting for transfers between devices, swap_rhs(): return lax.ppermute(v, 'rhs', [(i, i ^ k) for i in range(RHS)])  6.08 us
    ppermute x1, starting transfers between devices, shards(): up = lax.ppermute(to_before, 'leaf', [(i + 1, i) for i in range(count - 1)])  5.75 us
    pallas_call x1, Pallas kernels, shards(): call(second_kernel, [(LEAVES, 8, RANK), (2, LEAVES * PTS)], [SMEM] + [VME...  4.87 us
    pallas_call x1, Pallas kernels, shards(): call(prep_kernel, [jax.ShapeDtypeStruct((6, 320), jnp.int32), bf16(LEAVES...  4.67 us
    pallas_call x1, Pallas kernels, shards(): call(first_kernel, [(2048, 2 * RANK), (2, 16, RANK), (2, LEAVES * PTS)],...  3.26 us
  transfers between devices with their start and end apart: 13, of which 1 were waited for; matrix products, arithmetic and copies ran while one was open for 0% of the time, Pallas kernels for 68%

profile of v1, /device:TPU:6, one launch (start us, length us, event | category | flops | bytes accessed | tf_op | source)
XLA Modules:
  0.0 106.6 jit_solution(12650041642350646617)
XLA Ops:
  0.0 0.1 pad_add_fusion.meta
  0.1 0.9 copy-done.2
  1.0 0.9 copy-done.4
  1.9 1.0 shard_map.100
  2.9 1.7 %collective-permute-start = (f32[4,4096]{1,0:T(4,128)S(1)}, f32[4,4096]{1,0:T(4,128)S(1)}, u32[]{:S(2)}, u32[]{:S(2)}) collective-permute-start(f32[4,4096]{1,0:T(4,128)S(1)} %get-tuple-element.40), channel_id=1, source_target_pairs={{0,1},{1,0},{2,3},{3,2},{4,5},{5,4},{6,7},{7,6},{8,9},{9,8},{10,11... | collective-permute-start | bytes 196616 | tf_op jit(solution)/shard_map/ppermute | solution.py:404
  4.6 0.0 copy-start.10
  4.6 4.7 %shard_map.101 = (s32[6,320]{1,0:T(8,128)S(1)}, bf16[16,256,32]{2,1,0:T(8,128)(2,1)S(1)}, bf16[16,16,1024]{2,1,0:T(8,128)(2,1)S(1)}) custom-call(s32[2]{0:T(128)S(1)} %pad_add_fusion.meta, s32[16,9]{1,0:T(8,128)S(1)} %copy-done.6, s32[16]{0:T(128)S(1)} %copy-done.7, f32[2,16384]{1,0:T(2,128)S(1)} %copy-done.4, ...), custom_call_target="tpu_custom_call" | custom-call | flops 4000000000 | bytes 100000 | tf_op jit(solution)/shard_map/pallas_call | solution.py:420
  9.4 3.0 %collective-permute-start.1 = (f32[4,4096]{1,0:T(4,128)S(1)}, f32[4,4096]{1,0:T(4,128)S(1)}, u32[]{:S(2)}, u32[]{:S(2)}) collective-permute-start(f32[4,4096]{1,0:T(4,128)S(1)} %pad_maximum_fusion._), channel_id=1, source_target_pairs={{0,2},{1,3},{2,0},{3,1},{4,6},{5,7},{6,4},{7,5},{8,10},{9,11},{10,... | collective-permute-start | bytes 196616 | tf_op jit(solution)/shard_map/ppermute | solution.py:404
  12.4 2.4 %shard_map.102.refs_8_ = f32[32,128]{1,0:T(8,128)S(1)} custom-call(f32[2,16384]{1,0:T(2,128)S(1)} %copy-done.3, f32[16,64,1024]{2,1,0:T(8,128)S(1)} %copy-done, f32[2,15,64,64]{3,2,1,0:T(8,128)S(1)} %copy-done.1, f32[4,4096]{1,0:T(4,128)S(1)} %pad_maximum_fusion._), custom_call_target="tpu_custom_call" | custom-call | flops 4000000000 | bytes 100000 | tf_op jit(solution)/shard_map/pallas_call | solution.py:434
  14.8 2.0 %collective-permute-start.2 = (f32[32,128]{1,0:T(8,128)S(1)}, f32[32,128]{1,0:T(8,128)S(1)}, u32[]{:S(2)}, u32[]{:S(2)}) collective-permute-start(f32[32,128]{1,0:T(8,128)S(1)} %shard_map.102.refs_8_), channel_id=1, source_target_pairs={{0,8},{4,12},{8,0},{12,4},{16,24},{20,28},{24,16},{28,20},{32,40},... | collective-permute-start | bytes 49160 | tf_op jit(solution)/shard_map/ppermute | solution.py:407
  16.8 8.7 %shard_map.103 = (f32[17,16,1024]{2,1,0:T(8,128)S(1)}, bf16[16,16,256]{2,1,0:T(8,128)(2,1)S(1)}, f32[10,1024]{1,0:T(8,128)S(1)}, f32[10,1024]{1,0:T(8,128)S(1)}, f32[32,128]{1,0:T(8,128)S(1)}) custom-call(s32[6,320]{1,0:T(8,128)S(1)} %get-tuple-element.37.refs_0_, f32[2,16384]{1,0:T(2,128)S(1)} %copy-done.5, ...), custom_call_target="tpu_custom_call" | custom-call | flops 8999999488 | bytes 100000 | tf_op jit(solution)/shard_map/pallas_call | solution.py:460
  25.5 0.0 collective-permute-done.2
  25.6 2.4 %collective-permute-start.3 = (f32[64,128]{1,0:T(8,128)S(1)}, f32[64,128]{1,0:T(8,128)S(1)}, u32[]{:S(2)}, u32[]{:S(2)}) collective-permute-start(f32[64,128]{1,0:T(8,128)S(1)} %constant_dynamic-update-slice_fusion.refs_6_), channel_id=1, source_target_pairs={{0,16},{4,20},{8,24},{12,28},{16,0},{20,4},{24,8},{28,12},{32,48},... | collective-permute-start | bytes 98312 | tf_op jit(solution)/shard_map/ppermute | solution.py:407
  27.9 9.6 %shard_map.104 = (f32[17,16,1024]{2,1,0:T(8,128)S(1)}, f32[64,128]{1,0:T(8,128)S(1)}, f32[10,1024]{1,0:T(8,128)S(1)}) custom-call(s32[6,320]{1,0:T(8,128)S(1)} %get-tuple-element.37.refs_0_, f32[2,16384]{1,0:T(2,128)S(1)} %copy-done.5, bf16[16,16,1024]{2,1,0:T(8,128)(2,1)S(1)} %get-tuple-element.38.refs_2_, ...), custom_call_target="tpu_custom_call" | custom-call | flops 8999999488 | bytes 100000 | tf_op jit(solution)/shard_map/pallas_call | solution.py:460
  37.5 1.9 %collective-permute-start.5 = (f32[10,1024]{1,0:T(8,128)S(1)}, f32[10,1024]{1,0:T(8,128)S(1)}, u32[]{:S(2)}, u32[]{:S(2)}) collective-permute-start(f32[10,1024]{1,0:T(8,128)S(1)} %get-tuple-element.51), channel_id=1, source_target_pairs={{0,4},{4,8},{8,12},{12,16},{16,20},{20,24},{24,28},{28,32},{32,36}... | collective-permute-start | bytes 122888 | tf_op jit(solution)/shard_map/ppermute | solution.py:475
  39.5 5.8 %collective-permute-start.6 = (f32[10,1024]{1,0:T(8,128)S(1)}, f32[10,1024]{1,0:T(8,128)S(1)}, u32[]{:S(2)}, u32[]{:S(2)}) collective-permute-start(f32[10,1024]{1,0:T(8,128)S(1)} %get-tuple-element.52), channel_id=1, source_target_pairs={{4,0},{8,4},{12,8},{16,12},{20,16},{24,20},{28,24},{32,28},{36,32}... | collective-permute-start | bytes 122888 | tf_op jit(solution)/shard_map/ppermute | solution.py:473
  45.3 2.6 %collective-permute-start.4 = (f32[128,128]{1,0:T(8,128)S(1)}, f32[128,128]{1,0:T(8,128)S(1)}, u32[]{:S(2)}, u32[]{:S(2)}) collective-permute-start(f32[128,128]{1,0:T(8,128)S(1)} %constant_dynamic-update-slice_fusion.2.refs_6_), channel_id=1, source_target_pairs={{0,32},{4,36},{8,40},{12,44},{16,48},{20,52},{24,56},{28,60},{32,0... | collective-permute-start | bytes 196616 | tf_op jit(solution)/shard_map/ppermute | solution.py:407
  47.9 9.6 %shard_map.105 = (f32[17,16,1024]{2,1,0:T(8,128)S(1)}, f32[128,128]{1,0:T(8,128)S(1)}) custom-call(s32[6,320]{1,0:T(8,128)S(1)} %get-tuple-element.37.refs_0_, f32[2,16384]{1,0:T(2,128)S(1)} %copy-done.5, bf16[16,16,1024]{2,1,0:T(8,128)(2,1)S(1)} %get-tuple-element.38.refs_2_, bf16[16,256,32]{2,1,0:T(8,128)(2,1)S(1)} %get-tuple-element.39.refs_3_, ...), custom_call_target="tpu_custom_call" | custom-call | flops 8999999488 | bytes 100000 | tf_op jit(solution)/shard_map/pallas_call | solution.py:460
  57.5 0.1 collective-permute-start.7
  57.6 8.7 %shard_map.106 = (f32[17,16,1024]{2,1,0:T(8,128)S(1)}, f32[256,128]{1,0:T(8,128)S(1)}) custom-call(s32[6,320]{1,0:T(8,128)S(1)} %get-tuple-element.37.refs_0_, f32[2,16384]{1,0:T(2,128)S(1)} %copy-done.5, bf16[16,16,1024]{2,1,0:T(8,128)(2,1)S(1)} %get-tuple-element.38.refs_2_, bf16[16,256,32]{2,1,0:T(8,128)(2,1)S(1)} %get-tuple-element.39.refs_3_, ...), custom_call_target="tpu_custom_call" | custom-call | flops 8999999488 | bytes 100000 | tf_op jit(solution)/shard_map/pallas_call | solution.py:460
  66.4 0.4 collective-permute-start.8
  66.7 10.1 %shard_map.107 = (f32[17,16,1024]{2,1,0:T(8,128)S(1)}, f32[512,128]{1,0:T(8,128)S(1)}) custom-call(s32[6,320]{1,0:T(8,128)S(1)} %get-tuple-element.37.refs_0_, f32[2,16384]{1,0:T(2,128)S(1)} %copy-done.5, bf16[16,16,1024]{2,1,0:T(8,128)(2,1)S(1)} %get-tuple-element.38.refs_2_, bf16[16,256,32]{2,1,0:T(8,128)(2,1)S(1)} %get-tuple-element.39.refs_3_, ...), custom_call_target="tpu_custom_call" | custom-call | flops 8999999488 | bytes 100000 | tf_op jit(solution)/shard_map/pallas_call | solution.py:460
  77.0 0.1 collective-permute-start.9
  77.1 10.2 %shard_map.108 = (f32[2,16384]{1,0:T(2,128)S(1)}, f32[2,16384]{1,0:T(2,128)S(1)}, f32[2,16384]{1,0:T(2,128)S(1)}, f32[2,16384]{1,0:T(2,128)S(1)}) custom-call(s32[6,320]{1,0:T(8,128)S(1)} %get-tuple-element.37.refs_0_, f32[2,16384]{1,0:T(2,128)S(1)} %copy-done.5, bf16[16,16,1024]{2,1,0:T(8,128)(2,1)S(1)} %get-tuple-element.38.refs_2_, ...), custom_call_target="tpu_custom_call" | custom-call | flops 8999999488 | bytes 100000 | tf_op jit(solution)/shard_map/pallas_call | solution.py:460
  87.3 2.9 %collective-permute-start.10 = (f32[2,16384]{1,0:T(2,128)S(1)}, f32[2,16384]{1,0:T(2,128)S(1)}, u32[]{:S(2)}, u32[]{:S(2)}) collective-permute-start(f32[2,16384]{1,0:T(2,128)S(1)} %get-tuple-element.63), channel_id=1, source_target_pairs={{0,2},{1,3},{2,0},{3,1},{4,6},{5,7},{6,4},{7,5},{8,10},{9,11},{10,... | collective-permute-start | bytes 393224 | tf_op jit(solution)/shard_map/ppermute | solution.py:404
  90.2 3.3 %shard_map.109 = (f32[2048,128]{1,0:T(8,128)S(1)}, f32[2,16,64]{2,1,0:T(8,128)S(1)}, f32[2,16384]{1,0:T(2,128)S(1)}) custom-call(s32[2,124]{1,0:T(2,128)S(1)} %and_add_fusion.rows, f32[1024,128]{1,0:T(8,128)S(1)} %constant_dynamic-update-slice_fusion.8.own, f32[1024,128]{1,0:T(8,128)S(1)} %collective-permute-done.9.other, f32[2,64,64,124]{3,2,1,0:T(8,128)} %bitcast.3, ...), custom_call_target="tpu_custom_call" | custom-call | flops 500000000 | bytes 100000 | tf_op jit(solution)/shard_map/pallas_call | solution.py:489
  93.4 4.9 %shard_map.110 = (f32[16,8,64]{2,1,0:T(8,128)S(1)}, f32[2,16384]{1,0:T(2,128)S(1)}) custom-call(s32[2,124]{1,0:T(2,128)S(1)} %and_add_fusion.rows, f32[2048,128]{1,0:T(8,128)S(1)} %get-tuple-element.57.table, f32[2,64,64,124]{3,2,1,0:T(8,128)} %bitcast.4, f32[2,16,64]{2,1,0:T(8,128)S(1)} %get-tuple-element.58.start, f32[2,15,64,64]{3,2,1,0:T(8,128)S(1)} %copy-done.1, ...), custom_call_target="tpu_custom_call" | custom-call | flops 500000000 | bytes 100000 | tf_op jit(solution)/shard_map/pallas_call | solution.py:497
  98.3 0.3 collective-permute-start.12
  98.6 0.4 collective-permute-start.11
  99.1 0.7 shard_map.111
  99.8 6.1 %collective-permute-done.12 = f32[2,16384]{1,0:T(2,128)S(1)} collective-permute-done((f32[2,16384]{1,0:T(2,128)S(1)}, f32[2,16384]{1,0:T(2,128)S(1)}, u32[]{:S(2)}, u32[]{:S(2)}) %collective-permute-start.12) | collective-permute-done | bytes 131104 | tf_op jit(solution)/shard_map/ppermute | solution.py:404
  105.8 0.8 add_add_fusion
  (45 shorter events, 0.3 us)
Async XLA Ops:
  0.1 0.9 copy-start.2
  1.0 0.9 copy-start.4
  1.9 2.7 %copy-start.6 = (s32[16,9]{1,0:T(8,128)S(1)}, s32[16,9]{1,0:T(8,128)}, u32[]{:S(2)}) copy-start(s32[16,9]{1,0:T(8,128)} %list_hbm.1) | copy-start | bytes 1732
  1.9 2.7 %copy-start.7 = (s32[16]{0:T(128)S(1)}, s32[16]{0:T(128)}, u32[]{:S(2)}) copy-start(s32[16]{0:T(128)} %count_hbm.1) | copy-start | bytes 196
  2.9 6.5 %collective-permute-start = (f32[4,4096]{1,0:T(4,128)S(1)}, f32[4,4096]{1,0:T(4,128)S(1)}, u32[]{:S(2)}, u32[]{:S(2)}) collective-permute-start(f32[4,4096]{1,0:T(4,128)S(1)} %get-tuple-element.40), channel_id=1, source_target_pairs={{0,1},{1,0},{2,3},{3,2},{4,5},{5,4},{6,7},{7,6},{8,9},{9,8},{10,11... | collective-permute-start | bytes 196616 | tf_op jit(solution)/shard_map/ppermute | solution.py:404
  4.5 4.7 %copy-start.8 = (s32[2,124]{1,0:T(2,128)S(1)}, s32[2,124]{1,0:T(2,128)}, u32[]{:S(2)}) copy-start(s32[2,124]{1,0:T(2,128)} %param.15) | copy-start | bytes 2980
  4.5 4.8 %copy-start.9 = (s32[124]{0:T(128)S(1)}, s32[124]{0:T(128)}, u32[]{:S(2)}) copy-start(s32[124]{0:T(128)} %constant.25.clone) | copy-start | bytes 1492
  4.6 4.8 %copy-start.10 = (s32[124]{0:T(128)S(1)}, s32[124]{0:T(128)}, u32[]{:S(2)}) copy-start(s32[124]{0:T(128)} %constant.34) | copy-start | bytes 1492
  4.6 4.8 %copy-start.11 = (s32[124]{0:T(128)S(1)}, s32[124]{0:T(128)}, u32[]{:S(2)}) copy-start(s32[124]{0:T(128)} %constant.36) | copy-start | bytes 1492
  4.6 7.9 %copy-start = (f32[16,64,1024]{2,1,0:T(8,128)S(1)}, f32[16,64,1024]{2,1,0:T(8,128)}, u32[]{:S(2)}) copy-start(f32[16,64,1024]{2,1,0:T(8,128)} %basis.3) | copy-start | bytes 12582916
  4.6 7.8 %copy-start.1 = (f32[2,15,64,64]{3,2,1,0:T(8,128)S(1)}, f32[2,15,64,64]{3,2,1,0:T(8,128)}, u32[]{:S(2)}) copy-start(f32[2,15,64,64]{3,2,1,0:T(8,128)} %transfer.3) | copy-start | bytes 1474564
  4.6 7.8 %copy-start.3 = (f32[2,16384]{1,0:T(2,128)S(1)}, f32[2,16384]{1,0:T(2,128)}, u32[]{:S(2)}) copy-start(f32[2,16384]{1,0:T(2,128)} %charges.1) | copy-start | bytes 393220
  9.4 7.4 %copy-start.5 = (f32[2,16384]{1,0:T(2,128)S(1)}, f32[2,16384]{1,0:T(2,128)}, u32[]{:S(2)}) copy-start(f32[2,16384]{1,0:T(2,128)} %refs_1_.11) | copy-start | bytes 393220
  9.4 7.4 %collective-permute-start.1 = (f32[4,4096]{1,0:T(4,128)S(1)}, f32[4,4096]{1,0:T(4,128)S(1)}, u32[]{:S(2)}, u32[]{:S(2)}) collective-permute-start(f32[4,4096]{1,0:T(4,128)S(1)} %pad_maximum_fusion._), channel_id=1, source_target_pairs={{0,2},{1,3},{2,0},{3,1},{4,6},{5,7},{6,4},{7,5},{8,10},{9,11},{10,... | collective-permute-start | bytes 196616 | tf_op jit(solution)/shard_map/ppermute | solution.py:404
  14.8 10.7 %collective-permute-start.2 = (f32[32,128]{1,0:T(8,128)S(1)}, f32[32,128]{1,0:T(8,128)S(1)}, u32[]{:S(2)}, u32[]{:S(2)}) collective-permute-start(f32[32,128]{1,0:T(8,128)S(1)} %shard_map.102.refs_8_), channel_id=1, source_target_pairs={{0,8},{4,12},{8,0},{12,4},{16,24},{20,28},{24,16},{28,20},{32,40},... | collective-permute-start | bytes 49160 | tf_op jit(solution)/shard_map/ppermute | solution.py:407
  25.6 19.7 %collective-permute-start.3 = (f32[64,128]{1,0:T(8,128)S(1)}, f32[64,128]{1,0:T(8,128)S(1)}, u32[]{:S(2)}, u32[]{:S(2)}) collective-permute-start(f32[64,128]{1,0:T(8,128)S(1)} %constant_dynamic-update-slice_fusion.refs_6_), channel_id=1, source_target_pairs={{0,16},{4,20},{8,24},{12,28},{16,0},{20,4},{24,8},{28,12},{32,48},... | collective-permute-start | bytes 98312 | tf_op jit(solution)/shard_map/ppermute | solution.py:407
  37.5 29.2 %collective-permute-start.5 = (f32[10,1024]{1,0:T(8,128)S(1)}, f32[10,1024]{1,0:T(8,128)S(1)}, u32[]{:S(2)}, u32[]{:S(2)}) collective-permute-start(f32[10,1024]{1,0:T(8,128)S(1)} %get-tuple-element.51), channel_id=1, source_target_pairs={{0,4},{4,8},{8,12},{12,16},{16,20},{20,24},{24,28},{28,32},{32,36}... | collective-permute-start | bytes 122888 | tf_op jit(solution)/shard_map/ppermute | solution.py:475
  39.5 27.3 %collective-permute-start.6 = (f32[10,1024]{1,0:T(8,128)S(1)}, f32[10,1024]{1,0:T(8,128)S(1)}, u32[]{:S(2)}, u32[]{:S(2)}) collective-permute-start(f32[10,1024]{1,0:T(8,128)S(1)} %get-tuple-element.52), channel_id=1, source_target_pairs={{4,0},{8,4},{12,8},{16,12},{20,16},{24,20},{28,24},{32,28},{36,32}... | collective-permute-start | bytes 122888 | tf_op jit(solution)/shard_map/ppermute | solution.py:473
  45.3 12.3 %collective-permute-start.4 = (f32[128,128]{1,0:T(8,128)S(1)}, f32[128,128]{1,0:T(8,128)S(1)}, u32[]{:S(2)}, u32[]{:S(2)}) collective-permute-start(f32[128,128]{1,0:T(8,128)S(1)} %constant_dynamic-update-slice_fusion.2.refs_6_), channel_id=1, source_target_pairs={{0,32},{4,36},{8,40},{12,44},{16,48},{20,52},{24,56},{28,60},{32,0... | collective-permute-start | bytes 196616 | tf_op jit(solution)/shard_map/ppermute | solution.py:407
  57.5 8.8 %collective-permute-start.7 = (f32[256,128]{1,0:T(8,128)S(1)}, f32[256,128]{1,0:T(8,128)S(1)}, u32[]{:S(2)}, u32[]{:S(2)}) collective-permute-start(f32[256,128]{1,0:T(8,128)S(1)} %constant_dynamic-update-slice_fusion.4.refs_6_), channel_id=1, source_target_pairs={{0,64},{4,68},{8,72},{12,76},{16,80},{20,84},{24,88},{28,92},{32,9... | collective-permute-start | bytes 393224 | tf_op jit(solution)/shard_map/ppermute | solution.py:407
  66.4 10.5 %collective-permute-start.8 = (f32[512,128]{1,0:T(8,128)S(1)}, f32[512,128]{1,0:T(8,128)S(1)}, u32[]{:S(2)}, u32[]{:S(2)}) collective-permute-start(f32[512,128]{1,0:T(8,128)S(1)} %constant_dynamic-update-slice_fusion.6.refs_8_), channel_id=1, source_target_pairs={{0,128},{4,132},{8,136},{12,140},{16,144},{20,148},{24,152},{28,15... | collective-permute-start | bytes 786440 | tf_op jit(solution)/shard_map/ppermute | solution.py:407
  77.0 13.2 %collective-permute-start.9 = (f32[1024,128]{1,0:T(8,128)S(1)}, f32[1024,128]{1,0:T(8,128)S(1)}, u32[]{:S(2)}, u32[]{:S(2)}) collective-permute-start(f32[1024,128]{1,0:T(8,128)S(1)} %constant_dynamic-update-slice_fusion.8.own), channel_id=1, source_target_pairs={{0,4},{4,0},{8,12},{12,8},{16,20},{20,16},{24,28},{28,24},{32,36},... | collective-permute-start | bytes 1572872 | tf_op jit(solution)/shard_map/ppermute | solution.py:407
  87.3 12.5 %collective-permute-start.10 = (f32[2,16384]{1,0:T(2,128)S(1)}, f32[2,16384]{1,0:T(2,128)S(1)}, u32[]{:S(2)}, u32[]{:S(2)}) collective-permute-start(f32[2,16384]{1,0:T(2,128)S(1)} %get-tuple-element.63), channel_id=1, source_target_pairs={{0,2},{1,3},{2,0},{3,1},{4,6},{5,7},{6,4},{7,5},{8,10},{9,11},{10,... | collective-permute-start | bytes 393224 | tf_op jit(solution)/shard_map/ppermute | solution.py:404
  98.3 7.5 %collective-permute-start.12 = (f32[2,16384]{1,0:T(2,128)S(1)}, f32[2,16384]{1,0:T(2,128)S(1)}, u32[]{:S(2)}, u32[]{:S(2)}) collective-permute-start(f32[2,16384]{1,0:T(2,128)S(1)} %get-tuple-element.61._), channel_id=1, source_target_pairs={{0,3},{1,2},{2,1},{3,0},{4,7},{5,6},{6,5},{7,4},{8,11},{9,10},{10,... | collective-permute-start | bytes 393224 | tf_op jit(solution)/shard_map/ppermute | solution.py:404
  98.6 7.2 %collective-permute-start.11 = (f32[2,16384]{1,0:T(2,128)S(1)}, f32[2,16384]{1,0:T(2,128)S(1)}, u32[]{:S(2)}, u32[]{:S(2)}) collective-permute-start(f32[2,16384]{1,0:T(2,128)S(1)} %get-tuple-element.64), channel_id=1, source_target_pairs={{0,1},{1,0},{2,3},{3,2},{4,5},{5,4},{6,7},{7,6},{8,9},{9,8},{10,11... | collective-permute-start | bytes 393224 | tf_op jit(solution)/shard_map/ppermute | solution.py:404

commit v2 on v1

--- a/solution.py
+++ b/solution.py
@@ -29,7 +29,7 @@
 T_LIMB = (0, 1, 0, 1, 2, 0, 2, 1)
 PAIRS = 124
 WINDOWS = 6
-OVER = 152
+SINGLE = 80
 ANY = pl.BlockSpec(memory_space=pl.ANY)
 HBM = pl.BlockSpec(memory_space=pltpu.HBM)
 VMEM = pl.BlockSpec(memory_space=pltpu.VMEM)
@@ -58,26 +58,6 @@
             flops=int(micros * 10**9), bytes_accessed=10**5, transcendentals=0
         ),
     )
-
-
-def pre_kernel(meta, coords_hbm, charges_hbm, own, first, second, place, coords, charges, sems):
-    copies = [
-        pltpu.make_async_copy(charges_hbm, charges, sems.at[0]),
-        pltpu.make_async_copy(coords_hbm, coords, sems.at[1]),
-    ]
-    for copy in copies:
-        copy.start()
-    r = meta[1]
-    copies[0].wait()
-    for k, (ref, at) in enumerate(((own, 0), (first, 0), (second, 0), (first, 2))):
-        q = (r ^ k) * QUART
-        for i in range(LEAVES):
-            source = pl.ds(pl.multiple_of(q + i * PTS, QUART), QUART)
-            ref[at : at + 2, i * QUART : (i + 1) * QUART] = charges[:, source]
-    copies[1].wait()
-    for i in range(LEAVES):
-        source = pl.ds(pl.multiple_of(r * QUART + i * PTS, QUART), QUART)
-        place[:, i * QUART : (i + 1) * QUART] = coords[:, source]
 
 
 def limbs(v):
@@ -122,13 +102,17 @@
     ).astype(B)
 
 
-def prep_kernel(meta, list_hbm, count_hbm, coords, place, _, lists, sf, tab, near_list, near_count, sems):
+def prep_kernel(meta, list_hbm, count_hbm, coords, lists, sf, tab, place, near_list, near_count, sems):
     copies = [
         pltpu.make_async_copy(list_hbm, near_list, sems.at[0]),
         pltpu.make_async_copy(count_hbm, near_count, sems.at[1]),
     ]
     for copy in copies:
         copy.start()
+    first, r = meta[0], meta[1]
+    for i in range(LEAVES):
+        source = pl.ds(pl.multiple_of(r * QUART + i * PTS, QUART), QUART)
+        place[:, i * QUART : (i + 1) * QUART] = coords[:, source]
     for n in range(4):
         xy = place[:, 4 * n * QUART : 4 * (n + 1) * QUART] - 0.5
         put_sources(xy, sf, 4 * n)
@@ -137,29 +121,45 @@
         tab[i] = target_rows(xy[0:1], xy[1:2])
     for copy in copies:
         copy.wait()
-    first = meta[0]
+
+    def put(p, *values):
+        for field, value in zip((0, 1, 2, 3, 4, 6), values):
+            lists[field, p] = value
 
     def leaf_pairs(i, counts):
         def slot(s, counts):
             local = near_list[i, s] - first
             before, after = local < 0, local >= LEAVES
             over = (before | after).astype(jnp.int32)
-            p = jnp.where(over == 1, OVER + counts[1], counts[0])
-            lists[0, p] = i
-            lists[1, p] = jnp.where(before, local + 20, jnp.where(after, local + 4, local))
-            lists[2, p] = i
-            lists[3, p] = lax.shift_right_arithmetic(local, 2) - lax.shift_right_arithmetic(i, 2)
-            lists[4, p] = (local & 3) - (i & 3)
-            return counts[0] + 1 - over, counts[1] + over
+            both = 1 - over
+            same = (local == i).astype(jnp.int32)
+            later = (local > i).astype(jnp.int32) * both
+            p = jnp.where(over == 1, SINGLE + LEAVES + counts[1], counts[0])
+            p = jnp.where(same == 1, SINGLE + i, p)
+
+            @pl.when(over + same + later > 0)
+            def _():
+                put(
+                    p,
+                    i,
+                    jnp.where(before, local + 20, jnp.where(after, local + 4, local)),
+                    i,
+                    lax.shift_right_arithmetic(local, 2) - lax.shift_right_arithmetic(i, 2),
+                    (local & 3) - (i & 3),
+                    local,
+                )
+
+            return counts[0] + later, counts[1] + over
 
         return lax.fori_loop(0, near_count[i], slot, counts)
 
-    inside, over = lax.fori_loop(0, LEAVES, leaf_pairs, (jnp.int32(0), jnp.int32(0)))
-    lists[5, 0] = inside
-    lists[5, 1] = over
+    twice, over = lax.fori_loop(0, LEAVES, leaf_pairs, (jnp.int32(0), jnp.int32(0)))
+    put(twice, 0, 0, LEAVES, 0, 0, LEAVES)
     for p in range(4):
-        for field in range(5):
-            lists[field, OVER + over + p] = LEAVES if field == 2 else 0
+        put(SINGLE + LEAVES + over + p, 0, 0, LEAVES, 0, 0, LEAVES)
+    lists[5, 0] = (twice + 1) & -2
+    lists[5, 1] = LEAVES + over
+    lists[5, 2] = r
 
 
 def put_sources(xy, sf, at):
@@ -188,30 +188,39 @@
     if w == 0:
         own, first, second, place = take(4)
     else:
-        cw, acc_in = take(2)
-    if w >= 4:
+        cw, call_w, acc_in, quart_in = take(4)
+    if w >= WINDOWS - 2:
         halos = take(2)
     carried = take(n_carried)
-    outs = take(4 if last else 1)
+    outs = take(4 if last else 2)
     if w == 0:
-        cw, to_before, to_after = take(3)
+        cw, call_w, to_before, to_after = take(4)
     for ref, out in zip(carried, take(n_carried)):
         out[...] = ref[...]
     kh_a, kl_a, kh_b, kl_b = take(4)
-    acc = take(1)[0] if last else outs[0]
+    acc, quart = take(2) if last else outs
+    r = lists[5, 2]
+    mine = pl.ds(pl.multiple_of(r * QUART, QUART), QUART)
 
     if w == 0:
-        whole = jnp.concatenate([own[...], first[...], second[...]], axis=0)
-        whole = jnp.concatenate([whole[0:4], whole[6:10]], axis=0)
         for j in range(LEAVES):
-            cw[j] = weights(whole[:, j * QUART : (j + 1) * QUART])
-        for ref, at in ((to_before, slice(0, 4 * QUART)), (to_after, slice(12 * QUART, 16 * QUART))):
-            ref[0:2] = place[:, at]
-            ref[2:10] = whole[:, at]
+            at = slice(j * PTS, (j + 1) * PTS)
+            call_w[j] = weights(jnp.concatenate([own[:, at], first[:, at], second[:, at]], axis=0))
+            cw[j] = call_w[j, :, mine]
+        for ref, start in ((to_before, 0), (to_after, 12)):
+            ref[0:2] = place[:, start * QUART : (start + 4) * QUART]
+            for j in range(4):
+                at = slice(j * QUART, (j + 1) * QUART)
+                source = pl.ds(pl.multiple_of(r * QUART + (start + j) * PTS, QUART), QUART)
+                ref[2:4, at] = own[:, source]
+                ref[4:6, at] = first[:, source]
+                ref[6:10, at] = second[:, source]
         acc[...] = jnp.zeros_like(acc)
+        quart[...] = jnp.zeros_like(quart)
     else:
         acc[...] = acc_in[...]
-    if w >= 4:
+        quart[...] = quart_in[...]
+    if w >= WINDOWS - 2:
         sf_own, cw_own = sf, cw
         sf, cw = take(2)
         sf[0:LEAVES] = sf_own[...]
@@ -220,31 +229,26 @@
             put_sources(halo[0:2] - 0.5, sf, LEAVES + 4 * n)
             for j in range(4):
                 cw[LEAVES + 4 * n + j] = weights(halo[2:10, j * QUART : (j + 1) * QUART])
-    kh_b[...] = jnp.zeros_like(kh_b)
-    kl_b[...] = jnp.zeros_like(kl_b)
-
-    inside = lists[5, 0]
-    total = inside + lists[5, 1]
-
-    def bound(n):
+
+    n_twice, n_single = lists[5, 0], lists[5, 1]
+
+    def bounds(n):
         if n == 0:
-            return jnp.int32(0)
+            return jnp.int32(0), jnp.int32(0)
         if n == WINDOWS:
-            return total
-        at = lax.div(total * n, WINDOWS)
-        return (jnp.minimum(at, inside) if n <= 4 else at) & -2
-
-    begin, end = bound(w), bound(w + 1)
-
-    def entry(p):
-        return jnp.where(p < inside, p, p - inside + OVER)
+            return n_twice, n_single
+        at = lax.div((3 * n_twice + 2 * n_single) * n, WINDOWS)
+        here = n_single if n > WINDOWS - 2 else LEAVES
+        single = jnp.maximum(lax.shift_right_arithmetic(at - 3 * n_twice, 1), 0)
+        return jnp.minimum(n_twice, lax.div(at, 3)) & -2, jnp.minimum(here, single) & -2
+
+    (twice_0, single_0), (twice_1, single_1) = bounds(w), bounds(w + 1)
 
     row = lax.broadcasted_iota(jnp.int32, (8, PTS), 0)
     low, middle = row < 3, (row >= 3) & (row < 6)
     ones = jnp.where(middle, 1.0, 0.0)
 
     def evaluate(p, kh, kl):
-        p = entry(p)
         i, j = lists[0, p], lists[1, p]
         ox, oy = lists[3, p].astype(F), lists[4, p].astype(F)
         xy = coords[:, pl.ds(pl.multiple_of(i * PTS, PTS), PTS)] - 0.5
@@ -268,28 +272,43 @@
                 kh[at, lanes] = high
                 kl[at, lanes] = (k - high.astype(F)).astype(B)
 
-    def multiply(p, kh, kl):
-        p = entry(p)
-        c = cw[lists[1, p]]
-        acc[lists[2, p]] += dot(c, kh[...], NN) + dot(c, kl[...], NN)
-
-    def step(n, _):
-        p = begin + 2 * n
-        evaluate(p, kh_a, kl_a)
-        multiply(jnp.maximum(p - 1, 0), kh_b, kl_b)
-        evaluate(p + 1, kh_b, kl_b)
-        multiply(p, kh_a, kl_a)
-        return 0
-
-    steps = (end - begin + 1) // 2
-    lax.fori_loop(0, steps, step, 0)
-    multiply(jnp.maximum(begin + 2 * steps - 1, 0), kh_b, kl_b)
+    def multiply(p, kh, kl, both):
+        i, j = lists[0, p], lists[1, p]
+        high, low_part = kh[...], kl[...]
+        acc[lists[2, p]] += dot(cw[j], high, NN) + dot(cw[j], low_part, NN)
+        if both:
+            quart[lists[6, p]] += dot(call_w[i], high, NT) + dot(call_w[i], low_part, NT)
+
+    def run(begin, end, both):
+        def step(n, _):
+            p = begin + 2 * n
+            evaluate(p, kh_a, kl_a)
+            multiply(jnp.maximum(p - 1, begin), kh_b, kl_b, both)
+            evaluate(p + 1, kh_b, kl_b)
+            multiply(p, kh_a, kl_a, both)
+            return 0
+
+        steps = (end - begin + 1) // 2
+
+        @pl.when(steps > 0)
+        def _():
+            kh_b[...] = jnp.zeros_like(kh_b)
+            kl_b[...] = jnp.zeros_like(kl_b)
+            lax.fori_loop(0, steps, step, 0)
+            multiply(begin + 2 * steps - 1, kh_b, kl_b, both)
+
+    run(twice_0, twice_1, True)
+    run(single_0 + SINGLE, single_1 + SINGLE, False)
 
     if last:
         for i in range(LEAVES):
             v = (acc[i, 0:8, :] + acc[i, 8:16, :]) * (PTS**-0.5)
             for k in range(RHS):
                 outs[k][:, i * PTS : (i + 1) * PTS] = v[2 * k : 2 * k + 2]
+            q = (quart[i, 0:8, :] + quart[i, 8:16, :]) * (PTS**-0.5)
+            at = pl.ds(pl.multiple_of(r * QUART + i * PTS, QUART), QUART)
+            for k in range(RHS):
+                outs[k][:, at] += q[2 * k : 2 * k + 2]
 
 
 def bf16(*shape):
@@ -355,22 +374,15 @@
     return [dot_hi(member, products[c], NT) for c in range(2)]
 
 
-def first_kernel(rows, own, other, coupling, carried, table, out, carry, picked, products):
+def down_kernel(rows, own, other, coupling, transfer, basis, out, table, picked, products, held):
     half = own.shape[0]
     table[0:half, :] = own[...]
     table[half : 2 * half, :] = other[...]
-    carry[...] = carried[...]
-    for c, t in enumerate(couple(0, rows, table, coupling, picked, products)):
-        out[c] = t
-
-
-def second_kernel(rows, table, coupling, start, transfer, carried, out, carry, picked, products, held):
-    carry[...] = carried[...]
     held[...] = jnp.zeros_like(held)
-    for c, t in enumerate(couple(1, rows, table, coupling, picked, products)):
-        for n in range(16):
-            held[n, c : c + 1, :] = start[c, n : n + 1, :]
-            held[16 + n, c : c + 1, :] = t[n : n + 1]
+    for block in range(2):
+        for c, t in enumerate(couple(block, rows, table, coupling, picked.at[block], products.at[block])):
+            for n in range(16):
+                held[16 * block + n, c : c + 1, :] = t[n : n + 1]
     current = [held[15] + held[31]]
     first = (0, 8, 12, 14)
     for level in range(4, 0, -1):
@@ -385,12 +397,7 @@
             for d in range(2 * per_block)
         ]
     for i in range(LEAVES):
-        out[i] = current[i]
-
-
-def expand_kernel(coefficients, basis, _, out):
-    for i in range(LEAVES):
-        v = split_dot(split_rows(coefficients[i]), basis[i], NN)
+        v = split_dot(split_rows(current[i]), basis[i], NN)
         out[:, i * PTS : (i + 1) * PTS] = v[0:2]
 
 
@@ -406,21 +413,16 @@
     def swap_leaf(v, bit):
         return lax.ppermute(v, "leaf", [(d, d ^ bit) for d in range(count)])
 
-    own, first, second, place = call(
-        pre_kernel,
-        [(2, LEAVES * QUART), (4, LEAVES * QUART), (2, LEAVES * QUART), (2, LEAVES * QUART)],
-        [SMEM, HBM, HBM],
+    first = swap_rhs(charges, 1)
+    lists, sf, tab, place = call(
+        prep_kernel,
         [
-            pltpu.VMEM((2, LEAVES * PTS), F),
-            pltpu.VMEM((2, LEAVES * PTS), F),
-            pltpu.SemaphoreType.DMA((2,)),
+            jax.ShapeDtypeStruct((8, 320), jnp.int32),
+            bf16(LEAVES, QUART, 32),
+            bf16(LEAVES, 16, PTS),
+            (2, LEAVES * QUART),
         ],
-    )(meta, coords, charges)
-    first = swap_rhs(first, 1)
-    lists, sf, tab = call(
-        prep_kernel,
-        [jax.ShapeDtypeStruct((6, 320), jnp.int32), bf16(LEAVES, QUART, 32), bf16(LEAVES, 16, PTS)],
-        [SMEM, HBM, HBM, VMEM, VMEM, ANY],
+        [SMEM, HBM, HBM, VMEM],
         [
             pltpu.SMEM((LEAVES, NEAR), jnp.int32),
             pltpu.SMEM((LEAVES,), jnp.int32),
@@ -428,53 +430,49 @@
         ],
         micros=4,
         smem_outs=1,
-    )(meta, near_list, near_count, coords, place, own)
-    onward = jnp.concatenate([second, first[2:4]], 0)
+    )(meta, near_list, near_count, coords)
+    onward = jnp.concatenate([charges, first], 0)
     second = swap_rhs(onward, 2)
     (table,) = call(up_kernel, [(32, 2 * RANK)], [VMEM] * 3 + [ANY], micros=4)(
         charges, leaf_basis, transfer, onward
     )
 
-    acc_shape, halo_shape = (LEAVES + 1, 16, PTS), (10, 4 * QUART)
+    acc_shape, quart_shape = (LEAVES + 1, 16, PTS), (LEAVES + 1, 16, QUART)
+    halo_shape = (10, 4 * QUART)
     values = [pltpu.VMEM((QUART, PTS), B)] * 4
-    after = table
-    halos = []
+    after, halos = table, []
     for w, bit in enumerate((2, 4, 8, 16, 32, 1)):
         swapped = swap_leaf(after, bit)
-        carried = [after] if w < WINDOWS - 1 else []
         data, extra, scratch = [lists, coords, tab, sf], [], [*values]
         if w == 0:
-            data += [own, first, second, place]
-            extra = [bf16(LEAVES, 16, QUART), halo_shape, halo_shape]
+            data += [charges, first, second, place]
+            extra = [bf16(LEAVES, 16, QUART), bf16(LEAVES, 16, PTS), halo_shape, halo_shape]
         else:
-            data += [cw, acc]
-        if w == 1:
-            carried.append(to_after)
+            data += [cw, call_w, acc, quart]
         if w == WINDOWS - 1:
-            scratch.append(pltpu.VMEM(acc_shape, F))
-        if w >= 4:
+            scratch += [pltpu.VMEM(acc_shape, F), pltpu.VMEM(quart_shape, F)]
+        if w >= WINDOWS - 2:
             data += halos
             scratch += [pltpu.VMEM((24, QUART, 32), B), pltpu.VMEM((24, 16, QUART), B)]
-        outs = [(2, LEAVES * PTS)] * 4 if w == WINDOWS - 1 else [acc_shape]
-        data += carried
+        carried = [after] if w < WINDOWS - 1 else []
+        outs = [(2, LEAVES * PTS)] * 4 if w == WINDOWS - 1 else [acc_shape, quart_shape]
         result = call(
             functools.partial(near_kernel, w, len(carried)),
             [*outs, *extra, *(v.shape for v in carried)],
-            [SMEM] + [VMEM] * (len(data) - 1),
+            [SMEM] + [VMEM] * (len(data) + len(carried) - 1),
             scratch,
             micros=9,
-        )(*data)
+        )(*data, *carried)
         if w == WINDOWS - 1:
             whole = result
             break
-        acc = result[0]
+        acc, quart = result[:2]
+        after = jnp.concatenate([result[-1], swapped], 0)
         if w == 0:
-            cw, to_before, to_after = result[1:4]
+            cw, call_w, to_before, to_after = result[2:6]
             up = lax.ppermute(to_before, "leaf", [(i + 1, i) for i in range(count - 1)])
-        if w == 1:
-            down = lax.ppermute(result[2], "leaf", [(i, i + 1) for i in range(count - 1)])
+            down = lax.ppermute(to_after, "leaf", [(i, i + 1) for i in range(count - 1)])
             halos = [down, up]
-        after = jnp.concatenate([result[1 + len(extra)], swapped], 0)
     other = swapped
 
     level = jnp.asarray([k for k in range(5) for _ in range(64 >> k)], jnp.int32)[None, :]
@@ -483,28 +481,19 @@
     start = jnp.asarray([LEVEL_ROW[k] for k in range(5) for _ in range(64 >> k)], jnp.int32)[None, :]
     apart = device ^ owner
     rows = ((apart & 1) * (count // 2) + (apart >> 1)) * 32 + start + inside
-    back = [swap_rhs(whole[2], 2)]
-    coupling = coupling.transpose(0, 2, 3, 1)
-    scratch = [pltpu.VMEM((128, 2 * RANK), F), pltpu.VMEM((2, RANK, PAIRS), F)]
-    table, upper, passed = call(
-        first_kernel,
-        [(2048, 2 * RANK), (2, 16, RANK), (2, LEAVES * PTS)],
-        [SMEM] + [VMEM] * 4,
-        scratch,
-        micros=0.5,
-    )(rows, after, other, coupling, whole[1])
-    back.append(swap_rhs(passed, 1))
-    coefficients, passed = call(
-        second_kernel,
-        [(LEAVES, 8, RANK), (2, LEAVES * PTS)],
+    back = [swap_rhs(whole[k], k) for k in (2, 1, 3)]
+    (distant,) = call(
+        down_kernel,
+        [(2, LEAVES * PTS)],
         [SMEM] + [VMEM] * 5,
-        [*scratch, pltpu.VMEM((32, 8, RANK), F)],
-        micros=0.5,
-    )(rows, table, coupling, upper, transfer, whole[3])
-    back.append(swap_rhs(passed, 3))
-    (distant,) = call(
-        expand_kernel, [(2, LEAVES * PTS)], [VMEM] * 2 + [ANY], micros=0.3
-    )(coefficients, leaf_basis, passed)
+        [
+            pltpu.VMEM((2048, 2 * RANK), F),
+            pltpu.VMEM((2, 128, 2 * RANK), F),
+            pltpu.VMEM((2, 2, RANK, PAIRS), F),
+            pltpu.VMEM((32, 8, RANK), F),
+        ],
+        micros=8,
+    )(rows, after, other, coupling.transpose(0, 2, 3, 1), transfer, leaf_basis)
     return distant + whole[0] + back[0] + back[1] + back[2]
 
 

time: 108 us -> 100 us (0.926); the launches traced: 107 us -> 102 us
  Pallas kernels: 73.8 us -> 67.2 us
  starting transfers between devices: 23.5 us -> 29.2 us
  waiting for transfers between devices: 6.11 us -> 1.98 us
    ppermute x6, starting transfers between devices: 7.47 us -> 12.7 us  [swap_leaf(): return lax.ppermute(v, 'leaf', [(d, d ^ bit) for d in range(count)])]
    pallas_call x6, Pallas kernels: 57 us -> 52 us  [shards(): call(functools.partial(near_kernel, w, len(carried)), [*outs, *extra, *(v...]
    ppermute x5, waiting for transfers between devices: 6.08 us -> 1.93 us  [swap_rhs(): return lax.ppermute(v, 'rhs', [(i, i ^ k) for i in range(RHS)])]
    pallas_call x5 -> x2, Pallas kernels: 14.5 us -> 12.8 us  [the longest x1 7.65 us: shards(): call(down_kernel, [(2, LEAVES * PTS)], [SMEM] + [VMEM] * 5, [pltpu.VMEM((...]
    unnamed x29 -> x27, local copies, waits for them, and re-layouts: 1.93 us -> 2.38 us
  transfers between devices with their start and end apart: 13 -> 13, of which waited for: 1 -> 1; matrix products, arithmetic and copies ran while one was open for 0% -> 0% of each run, Pallas kernels for 68% -> 66%
where the time goes in v2:
time: 100 us; the launch traced here: 102 us
  Pallas kernels  67.2 us (67%)
  starting transfers between devices  29.2 us (29%)
  local copies, waits for them, and re-layouts  2.43 us (2%)
  waiting for transfers between devices  1.98 us (2%)
  other arithmetic  1.01 us (1%)
    pallas_call x6, Pallas kernels, shards(): call(functools.partial(near_kernel, w, len(carried)), [*outs, *extra, *(v...  52 us
    ppermute x6, starting transfers between devices, swap_leaf(): return lax.ppermute(v, 'leaf', [(d, d ^ bit) for d in range(count)])  12.7 us
    ppermute x5, starting transfers between devices, swap_rhs(): return lax.ppermute(v, 'rhs', [(i, i ^ k) for i in range(RHS)])  8.74 us
    pallas_call x1, Pallas kernels, shards(): call(down_kernel, [(2, LEAVES * PTS)], [SMEM] + [VMEM] * 5, [pltpu.VMEM((...  7.65 us
    ppermute x1, starting transfers between devices, shards(): up = lax.ppermute(to_before, 'leaf', [(i + 1, i) for i in range(count - 1)])  5.75 us
    pallas_call x1, Pallas kernels, shards(): call(prep_kernel, [jax.ShapeDtypeStruct((8, 320), jnp.int32), bf16(LEAVES...  5.11 us
    pallas_call x1, Pallas kernels, shards(): call(up_kernel, [(32, 2 * RANK)], [VMEM] * 3 + [ANY], micros=4)  2.4 us
    unnamed x27, local copies, waits for them, and re-layouts  2.38 us
  transfers between devices with their start and end apart: 13, of which 1 were waited for; matrix products, arithmetic and copies ran while one was open for 0% of the time, Pallas kernels for 66%

profile of v2, /device:TPU:6, one launch (start us, length us, event | category | flops | bytes accessed | tf_op | source)
XLA Modules:
  0.0 102.0 jit_solution(5253019378736227640)
XLA Ops:
  0.0 1.6 %collective-permute-start = (f32[2,16384]{1,0:T(2,128)}, f32[2,16384]{1,0:T(2,128)S(1)}, u32[]{:S(2)}, u32[]{:S(2)}) collective-permute-start(f32[2,16384]{1,0:T(2,128)} %refs_4_.1), channel_id=1, source_target_pairs={{0,1},{1,0},{2,3},{3,2},{4,5},{5,4},{6,7},{7,6},{8,9},{9,8},{10,11... | collective-permute-start | bytes 393224 | tf_op jit(solution)/shard_map/ppermute | solution.py:411
  1.6 0.1 pad_add_fusion.meta
  1.7 0.9 copy-done.3
  2.6 0.7 copy-done.5
  3.3 0.7 copy-done.6
  3.9 0.0 copy-start.2
  4.0 5.1 %shard_map.100 = (s32[8,320]{1,0:T(8,128)S(1)}, bf16[16,256,32]{2,1,0:T(8,128)(2,1)S(1)}, bf16[16,16,1024]{2,1,0:T(8,128)(2,1)S(1)}, f32[2,4096]{1,0:T(2,128)S(1)}) custom-call(s32[2]{0:T(128)S(1)} %pad_add_fusion.meta, s32[16,9]{1,0:T(8,128)S(1)} %copy-done.5, s32[16]{0:T(128)S(1)} %copy-done.6, f32[2,16384]{1,0:T(2,128)S(1)} %copy-done.3), custom_call_target="tpu_custom_call" | custom-call | flops 4000000000 | bytes 100000 | tf_op jit(solution)/shard_map/pallas_call | solution.py:417
  9.2 0.1 pad_maximum_fusion._
  9.3 0.0 copy-start.4
  9.3 3.0 %collective-permute-start.1 = (f32[4,16384]{1,0:T(4,128)S(1)}, f32[4,16384]{1,0:T(4,128)S(1)}, u32[]{:S(2)}, u32[]{:S(2)}) collective-permute-start(f32[4,16384]{1,0:T(4,128)S(1)} %pad_maximum_fusion._), channel_id=1, source_target_pairs={{0,2},{1,3},{2,0},{3,1},{4,6},{5,7},{6,4},{7,5},{8,10},{9,11},{10,... | collective-permute-start | bytes 786440 | tf_op jit(solution)/shard_map/ppermute | solution.py:411
  12.3 2.4 %shard_map.101.refs_8_ = f32[32,128]{1,0:T(8,128)S(1)} custom-call(f32[2,16384]{1,0:T(2,128)S(1)} %copy-done, f32[16,64,1024]{2,1,0:T(8,128)S(1)} %copy-done.1, f32[2,15,64,64]{3,2,1,0:T(8,128)S(1)} %copy-done.2, f32[4,16384]{1,0:T(4,128)S(1)} %pad_maximum_fusion._), custom_call_target="tpu_custom_call" | custom-call | flops 4000000000 | bytes 100000 | tf_op jit(solution)/shard_map/pallas_call | solution.py:436
  14.7 1.2 %collective-permute-start.2 = (f32[32,128]{1,0:T(8,128)S(1)}, f32[32,128]{1,0:T(8,128)S(1)}, u32[]{:S(2)}, u32[]{:S(2)}) collective-permute-start(f32[32,128]{1,0:T(8,128)S(1)} %shard_map.101.refs_8_), channel_id=1, source_target_pairs={{0,8},{4,12},{8,0},{12,4},{16,24},{20,28},{24,16},{28,20},{32,40},... | collective-permute-start | bytes 49160 | tf_op jit(solution)/shard_map/ppermute | solution.py:414
  15.9 1.9 %collective-permute-done.1.refs_6_ = f32[4,16384]{1,0:T(4,128)S(1)} collective-permute-done((f32[4,16384]{1,0:T(4,128)S(1)}, f32[4,16384]{1,0:T(4,128)S(1)}, u32[]{:S(2)}, u32[]{:S(2)}) %collective-permute-start.1) | collective-permute-done | bytes 262176 | tf_op jit(solution)/shard_map/ppermute | solution.py:411
  17.8 7.2 %shard_map.102 = (f32[17,16,1024]{2,1,0:T(8,128)S(1)}, f32[17,16,256]{2,1,0:T(8,128)S(1)}, bf16[16,16,256]{2,1,0:T(8,128)(2,1)S(1)}, bf16[16,16,1024]{2,1,0:T(8,...) custom-call(s32[8,320]{1,0:T(8,128)S(1)} %get-tuple-element.32.refs_0_, ...), custom_call_target="tpu_custom_call" | custom-call | flops 8999999488 | bytes 100000 | tf_op jit(solution)/shard_map/pallas_call | solution.py:459
  25.0 0.0 collective-permute-done.2
  25.0 4.9 %collective-permute-start.3 = (f32[64,128]{1,0:T(8,128)S(1)}, f32[64,128]{1,0:T(8,128)S(1)}, u32[]{:S(2)}, u32[]{:S(2)}) collective-permute-start(f32[64,128]{1,0:T(8,128)S(1)} %constant_dynamic-update-slice_fusion.refs_8_), channel_id=1, source_target_pairs={{0,16},{4,20},{8,24},{12,28},{16,0},{20,4},{24,8},{28,12},{32,48},... | collective-permute-start | bytes 98312 | tf_op jit(solution)/shard_map/ppermute | solution.py:414
  30.0 8.4 %shard_map.103 = (f32[17,16,1024]{2,1,0:T(8,128)S(1)}, f32[17,16,256]{2,1,0:T(8,128)S(1)}, f32[64,128]{1,0:T(8,128)S(1)}) custom-call(s32[8,320]{1,0:T(8,128)S(1)} %get-tuple-element.32.refs_0_, f32[2,16384]{1,0:T(2,128)S(1)} %copy-done.4, bf16[16,16,1024]{2,1,0:T(8,128)(2,1)S(1)} %get-tuple-element.33.refs_2_, ...), custom_call_target="tpu_custom_call" | custom-call | flops 8999999488 | bytes 100000 | tf_op jit(solution)/shard_map/pallas_call | solution.py:459
  38.4 1.9 %collective-permute-start.5 = (f32[10,1024]{1,0:T(8,128)S(1)}, f32[10,1024]{1,0:T(8,128)S(1)}, u32[]{:S(2)}, u32[]{:S(2)}) collective-permute-start(f32[10,1024]{1,0:T(8,128)S(1)} %get-tuple-element.49), channel_id=1, source_target_pairs={{0,4},{4,8},{8,12},{12,16},{16,20},{20,24},{24,28},{28,32},{32,36}... | collective-permute-start | bytes 122888 | tf_op jit(solution)/shard_map/ppermute | solution.py:474
  40.3 5.8 %collective-permute-start.6 = (f32[10,1024]{1,0:T(8,128)S(1)}, f32[10,1024]{1,0:T(8,128)S(1)}, u32[]{:S(2)}, u32[]{:S(2)}) collective-permute-start(f32[10,1024]{1,0:T(8,128)S(1)} %get-tuple-element.50), channel_id=1, source_target_pairs={{4,0},{8,4},{12,8},{16,12},{20,16},{24,20},{28,24},{32,28},{36,32}... | collective-permute-start | bytes 122888 | tf_op jit(solution)/shard_map/ppermute | solution.py:473
  46.1 1.4 %collective-permute-start.4 = (f32[128,128]{1,0:T(8,128)S(1)}, f32[128,128]{1,0:T(8,128)S(1)}, u32[]{:S(2)}, u32[]{:S(2)}) collective-permute-start(f32[128,128]{1,0:T(8,128)S(1)} %constant_dynamic-update-slice_fusion.2.refs_8_), channel_id=1, source_target_pairs={{0,32},{4,36},{8,40},{12,44},{16,48},{20,52},{24,56},{28,60},{32,0... | collective-permute-start | bytes 196616 | tf_op jit(solution)/shard_map/ppermute | solution.py:414
  47.5 8.4 %shard_map.104 = (f32[17,16,1024]{2,1,0:T(8,128)S(1)}, f32[17,16,256]{2,1,0:T(8,128)S(1)}, f32[128,128]{1,0:T(8,128)S(1)}) custom-call(s32[8,320]{1,0:T(8,128)S(1)} %get-tuple-element.32.refs_0_, f32[2,16384]{1,0:T(2,128)S(1)} %copy-done.4, bf16[16,16,1024]{2,1,0:T(8,128)(2,1)S(1)} %get-tuple-element.33.refs_2_, ...), custom_call_target="tpu_custom_call" | custom-call | flops 8999999488 | bytes 100000 | tf_op jit(solution)/shard_map/pallas_call | solution.py:459
  56.0 5.1 %collective-permute-start.7 = (f32[256,128]{1,0:T(8,128)S(1)}, f32[256,128]{1,0:T(8,128)S(1)}, u32[]{:S(2)}, u32[]{:S(2)}) collective-permute-start(f32[256,128]{1,0:T(8,128)S(1)} %constant_dynamic-update-slice_fusion.4.refs_8_), channel_id=1, source_target_pairs={{0,64},{4,68},{8,72},{12,76},{16,80},{20,84},{24,88},{28,92},{32,9... | collective-permute-start | bytes 393224 | tf_op jit(solution)/shard_map/ppermute | solution.py:414
  61.1 9.3 %shard_map.105 = (f32[17,16,1024]{2,1,0:T(8,128)S(1)}, f32[17,16,256]{2,1,0:T(8,128)S(1)}, f32[256,128]{1,0:T(8,128)S(1)}) custom-call(s32[8,320]{1,0:T(8,128)S(1)} %get-tuple-element.32.refs_0_, f32[2,16384]{1,0:T(2,128)S(1)} %copy-done.4, bf16[16,16,1024]{2,1,0:T(8,128)(2,1)S(1)} %get-tuple-element.33.refs_2_, ...), custom_call_target="tpu_custom_call" | custom-call | flops 8999999488 | bytes 100000 | tf_op jit(solution)/shard_map/pallas_call | solution.py:459
  70.5 0.1 collective-permute-start.8
  70.6 8.6 %shard_map.106 = (f32[17,16,1024]{2,1,0:T(8,128)S(1)}, f32[17,16,256]{2,1,0:T(8,128)S(1)}, f32[512,128]{1,0:T(8,128)S(1)}) custom-call(s32[8,320]{1,0:T(8,128)S(1)} %get-tuple-element.32.refs_0_, f32[2,16384]{1,0:T(2,128)S(1)} %copy-done.4, bf16[16,16,1024]{2,1,0:T(8,128)(2,1)S(1)} %get-tuple-element.33.refs_2_, ...), custom_call_target="tpu_custom_call" | custom-call | flops 8999999488 | bytes 100000 | tf_op jit(solution)/shard_map/pallas_call | solution.py:459
  79.3 0.1 collective-permute-start.9
  79.4 10.0 %shard_map.108 = (f32[2,16384]{1,0:T(2,128)S(1)}, f32[2,16384]{1,0:T(2,128)S(1)}, f32[2,16384]{1,0:T(2,128)S(1)}, f32[2,16384]{1,0:T(2,128)S(1)}) custom-call(s32[8,320]{1,0:T(8,128)S(1)} %get-tuple-element.32.refs_0_, f32[2,16384]{1,0:T(2,128)S(1)} %copy-done.4, bf16[16,16,1024]{2,1,0:T(8,128)(2,1)S(1)} %get-tuple-element.33.refs_2_, ...), custom_call_target="tpu_custom_call" | custom-call | flops 8999999488 | bytes 100000 | tf_op jit(solution)/shard_map/pallas_call | solution.py:459
  89.4 3.0 %collective-permute-start.10 = (f32[2,16384]{1,0:T(2,128)S(1)}, f32[2,16384]{1,0:T(2,128)S(1)}, u32[]{:S(2)}, u32[]{:S(2)}) collective-permute-start(f32[2,16384]{1,0:T(2,128)S(1)} %get-tuple-element.56), channel_id=1, source_target_pairs={{0,2},{1,3},{2,0},{3,1},{4,6},{5,7},{6,4},{7,5},{8,10},{9,11},{10,... | collective-permute-start | bytes 393224 | tf_op jit(solution)/shard_map/ppermute | solution.py:411
  92.4 0.1 collective-permute-start.11
  92.5 1.0 %collective-permute-start.12 = (f32[2,16384]{1,0:T(2,128)S(1)}, f32[2,16384]{1,0:T(2,128)S(1)}, u32[]{:S(2)}, u32[]{:S(2)}) collective-permute-start(f32[2,16384]{1,0:T(2,128)S(1)} %get-tuple-element.58), channel_id=1, source_target_pairs={{0,3},{1,2},{2,1},{3,0},{4,7},{5,6},{6,5},{7,4},{8,11},{9,10},{10,... | collective-permute-start | bytes 393224 | tf_op jit(solution)/shard_map/ppermute | solution.py:411
  93.6 7.6 %shard_map.107 = f32[2,16384]{1,0:T(2,128)S(1)} custom-call(s32[2,124]{1,0:T(2,128)S(1)} %and_add_fusion.rows, f32[1024,128]{1,0:T(8,128)S(1)} %constant_dynamic-update-slice_fusion.8.own, f32[1024,128]{1,0:T(8,128)S(1)} %collective-permute-done.9.other, f32[2,64,64,124]{3,2,1,0:T(8,128)} %bitcast.3, f32[2,15,64,64]{3,2,1,0:T(8,128)S(1)} %copy-done.2, ...), custom_call_target="tpu_custom_call" | custom-call | flops 8000000000 | bytes 100000 | tf_op jit(solution)/shard_map/pallas_call | solution.py:485
  101.3 0.8 add_add_fusion
  (39 shorter events, 0.2 us)
Async XLA Ops:
  0.0 9.1 %collective-permute-start = (f32[2,16384]{1,0:T(2,128)}, f32[2,16384]{1,0:T(2,128)S(1)}, u32[]{:S(2)}, u32[]{:S(2)}) collective-permute-start(f32[2,16384]{1,0:T(2,128)} %refs_4_.1), channel_id=1, source_target_pairs={{0,1},{1,0},{2,3},{3,2},{4,5},{5,4},{6,7},{7,6},{8,9},{9,8},{10,11... | collective-permute-start | bytes 393224 | tf_op jit(solution)/shard_map/ppermute | solution.py:411
  1.7 0.9 copy-start.3
  2.6 0.7 copy-start.5
  3.3 0.7 copy-start.6
  3.9 5.2 %copy-start.7 = (s32[2,124]{1,0:T(2,128)S(1)}, s32[2,124]{1,0:T(2,128)}, u32[]{:S(2)}) copy-start(s32[2,124]{1,0:T(2,128)} %param.15) | copy-start | bytes 2980
  3.9 5.2 %copy-start.8 = (s32[124]{0:T(128)S(1)}, s32[124]{0:T(128)}, u32[]{:S(2)}) copy-start(s32[124]{0:T(128)} %constant.25.clone) | copy-start | bytes 1492
  3.9 5.2 %copy-start.9 = (s32[124]{0:T(128)S(1)}, s32[124]{0:T(128)}, u32[]{:S(2)}) copy-start(s32[124]{0:T(128)} %constant.34) | copy-start | bytes 1492
  3.9 5.2 %copy-start.10 = (s32[124]{0:T(128)S(1)}, s32[124]{0:T(128)}, u32[]{:S(2)}) copy-start(s32[124]{0:T(128)} %constant.36) | copy-start | bytes 1492
  3.9 5.2 %copy-start = (f32[2,16384]{1,0:T(2,128)S(1)}, f32[2,16384]{1,0:T(2,128)}, u32[]{:S(2)}) copy-start(f32[2,16384]{1,0:T(2,128)} %refs_4_.1) | copy-start | bytes 393220
  3.9 8.4 %copy-start.1 = (f32[16,64,1024]{2,1,0:T(8,128)S(1)}, f32[16,64,1024]{2,1,0:T(8,128)}, u32[]{:S(2)}) copy-start(f32[16,64,1024]{2,1,0:T(8,128)} %basis.3) | copy-start | bytes 12582916
  3.9 8.3 %copy-start.2 = (f32[2,15,64,64]{3,2,1,0:T(8,128)S(1)}, f32[2,15,64,64]{3,2,1,0:T(8,128)}, u32[]{:S(2)}) copy-start(f32[2,15,64,64]{3,2,1,0:T(8,128)} %transfer.3) | copy-start | bytes 1474564
  9.3 8.5 %copy-start.4 = (f32[2,16384]{1,0:T(2,128)S(1)}, f32[2,16384]{1,0:T(2,128)}, u32[]{:S(2)}) copy-start(f32[2,16384]{1,0:T(2,128)} %refs_1_.11) | copy-start | bytes 393220
  9.3 8.5 %collective-permute-start.1 = (f32[4,16384]{1,0:T(4,128)S(1)}, f32[4,16384]{1,0:T(4,128)S(1)}, u32[]{:S(2)}, u32[]{:S(2)}) collective-permute-start(f32[4,16384]{1,0:T(4,128)S(1)} %pad_maximum_fusion._), channel_id=1, source_target_pairs={{0,2},{1,3},{2,0},{3,1},{4,6},{5,7},{6,4},{7,5},{8,10},{9,11},{10,... | collective-permute-start | bytes 786440 | tf_op jit(solution)/shard_map/ppermute | solution.py:411
  14.7 10.3 %collective-permute-start.2 = (f32[32,128]{1,0:T(8,128)S(1)}, f32[32,128]{1,0:T(8,128)S(1)}, u32[]{:S(2)}, u32[]{:S(2)}) collective-permute-start(f32[32,128]{1,0:T(8,128)S(1)} %shard_map.101.refs_8_), channel_id=1, source_target_pairs={{0,8},{4,12},{8,0},{12,4},{16,24},{20,28},{24,16},{28,20},{32,40},... | collective-permute-start | bytes 49160 | tf_op jit(solution)/shard_map/ppermute | solution.py:414
  25.0 21.1 %collective-permute-start.3 = (f32[64,128]{1,0:T(8,128)S(1)}, f32[64,128]{1,0:T(8,128)S(1)}, u32[]{:S(2)}, u32[]{:S(2)}) collective-permute-start(f32[64,128]{1,0:T(8,128)S(1)} %constant_dynamic-update-slice_fusion.refs_8_), channel_id=1, source_target_pairs={{0,16},{4,20},{8,24},{12,28},{16,0},{20,4},{24,8},{28,12},{32,48},... | collective-permute-start | bytes 98312 | tf_op jit(solution)/shard_map/ppermute | solution.py:414
  38.4 32.2 %collective-permute-start.5 = (f32[10,1024]{1,0:T(8,128)S(1)}, f32[10,1024]{1,0:T(8,128)S(1)}, u32[]{:S(2)}, u32[]{:S(2)}) collective-permute-start(f32[10,1024]{1,0:T(8,128)S(1)} %get-tuple-element.49), channel_id=1, source_target_pairs={{0,4},{4,8},{8,12},{12,16},{16,20},{20,24},{24,28},{28,32},{32,36}... | collective-permute-start | bytes 122888 | tf_op jit(solution)/shard_map/ppermute | solution.py:474
  40.3 30.2 %collective-permute-start.6 = (f32[10,1024]{1,0:T(8,128)S(1)}, f32[10,1024]{1,0:T(8,128)S(1)}, u32[]{:S(2)}, u32[]{:S(2)}) collective-permute-start(f32[10,1024]{1,0:T(8,128)S(1)} %get-tuple-element.50), channel_id=1, source_target_pairs={{4,0},{8,4},{12,8},{16,12},{20,16},{24,20},{28,24},{32,28},{36,32}... | collective-permute-start | bytes 122888 | tf_op jit(solution)/shard_map/ppermute | solution.py:473
  46.1 9.8 %collective-permute-start.4 = (f32[128,128]{1,0:T(8,128)S(1)}, f32[128,128]{1,0:T(8,128)S(1)}, u32[]{:S(2)}, u32[]{:S(2)}) collective-permute-start(f32[128,128]{1,0:T(8,128)S(1)} %constant_dynamic-update-slice_fusion.2.refs_8_), channel_id=1, source_target_pairs={{0,32},{4,36},{8,40},{12,44},{16,48},{20,52},{24,56},{28,60},{32,0... | collective-permute-start | bytes 196616 | tf_op jit(solution)/shard_map/ppermute | solution.py:414
  56.0 14.5 %collective-permute-start.7 = (f32[256,128]{1,0:T(8,128)S(1)}, f32[256,128]{1,0:T(8,128)S(1)}, u32[]{:S(2)}, u32[]{:S(2)}) collective-permute-start(f32[256,128]{1,0:T(8,128)S(1)} %constant_dynamic-update-slice_fusion.4.refs_8_), channel_id=1, source_target_pairs={{0,64},{4,68},{8,72},{12,76},{16,80},{20,84},{24,88},{28,92},{32,9... | collective-permute-start | bytes 393224 | tf_op jit(solution)/shard_map/ppermute | solution.py:414
  70.5 8.8 %collective-permute-start.8 = (f32[512,128]{1,0:T(8,128)S(1)}, f32[512,128]{1,0:T(8,128)S(1)}, u32[]{:S(2)}, u32[]{:S(2)}) collective-permute-start(f32[512,128]{1,0:T(8,128)S(1)} %constant_dynamic-update-slice_fusion.6.refs_10_), channel_id=1, source_target_pairs={{0,128},{4,132},{8,136},{12,140},{16,144},{20,148},{24,152},{28,15... | collective-permute-start | bytes 786440 | tf_op jit(solution)/shard_map/ppermute | solution.py:414
  79.3 14.3 %collective-permute-start.9 = (f32[1024,128]{1,0:T(8,128)S(1)}, f32[1024,128]{1,0:T(8,128)S(1)}, u32[]{:S(2)}, u32[]{:S(2)}) collective-permute-start(f32[1024,128]{1,0:T(8,128)S(1)} %constant_dynamic-update-slice_fusion.8.own), channel_id=1, source_target_pairs={{0,4},{4,0},{8,12},{12,8},{16,20},{20,16},{24,28},{28,24},{32,36},... | collective-permute-start | bytes 1572872 | tf_op jit(solution)/shard_map/ppermute | solution.py:414
  89.4 11.8 %collective-permute-start.10 = (f32[2,16384]{1,0:T(2,128)S(1)}, f32[2,16384]{1,0:T(2,128)S(1)}, u32[]{:S(2)}, u32[]{:S(2)}) collective-permute-start(f32[2,16384]{1,0:T(2,128)S(1)} %get-tuple-element.56), channel_id=1, source_target_pairs={{0,2},{1,3},{2,0},{3,1},{4,6},{5,7},{6,4},{7,5},{8,10},{9,11},{10,... | collective-permute-start | bytes 393224 | tf_op jit(solution)/shard_map/ppermute | solution.py:411
  92.4 8.8 %collective-permute-start.11 = (f32[2,16384]{1,0:T(2,128)S(1)}, f32[2,16384]{1,0:T(2,128)S(1)}, u32[]{:S(2)}, u32[]{:S(2)}) collective-permute-start(f32[2,16384]{1,0:T(2,128)S(1)} %get-tuple-element.57), channel_id=1, source_target_pairs={{0,1},{1,0},{2,3},{3,2},{4,5},{5,4},{6,7},{7,6},{8,9},{9,8},{10,11... | collective-permute-start | bytes 393224 | tf_op jit(solution)/shard_map/ppermute | solution.py:411
  92.5 8.7 %collective-permute-start.12 = (f32[2,16384]{1,0:T(2,128)S(1)}, f32[2,16384]{1,0:T(2,128)S(1)}, u32[]{:S(2)}, u32[]{:S(2)}) collective-permute-start(f32[2,16384]{1,0:T(2,128)S(1)} %get-tuple-element.58), channel_id=1, source_target_pairs={{0,3},{1,2},{2,1},{3,0},{4,7},{5,6},{6,5},{7,4},{8,11},{9,10},{10,... | collective-permute-start | bytes 393224 | tf_op jit(solution)/shard_map/ppermute | solution.py:411

commit v3 on v2

--- a/solution.py
+++ b/solution.py
@@ -34,7 +34,7 @@
 HBM = pl.BlockSpec(memory_space=pltpu.HBM)
 VMEM = pl.BlockSpec(memory_space=pltpu.VMEM)
 SMEM = pl.BlockSpec(memory_space=pltpu.SMEM)
-PARAMS = pltpu.CompilerParams(vmem_limit_bytes=48 * 2**20)
+PARAMS = pltpu.CompilerParams(vmem_limit_bytes=24 * 2**20)
 
 
 def dot(a, b, dims):
@@ -102,7 +102,7 @@
     ).astype(B)
 
 
-def prep_kernel(meta, list_hbm, count_hbm, coords, lists, sf, tab, place, near_list, near_count, sems):
+def prep_kernel(meta, list_hbm, count_hbm, coords, _, lists, sf, tab, place, near_list, near_count, sems):
     copies = [
         pltpu.make_async_copy(list_hbm, near_list, sems.at[0]),
         pltpu.make_async_copy(count_hbm, near_count, sems.at[1]),
@@ -189,12 +189,15 @@
         own, first, second, place = take(4)
     else:
         cw, call_w, acc_in, quart_in = take(4)
-    if w >= WINDOWS - 2:
+    if w == WINDOWS - 2:
         halos = take(2)
     carried = take(n_carried)
     outs = take(4 if last else 2)
     if w == 0:
         cw, call_w, to_before, to_after = take(4)
+    if w == WINDOWS - 2:
+        sf_own, cw_own = sf, cw
+        sf, cw = take(2)
     for ref, out in zip(carried, take(n_carried)):
         out[...] = ref[...]
     kh_a, kl_a, kh_b, kl_b = take(4)
@@ -220,9 +223,7 @@
     else:
         acc[...] = acc_in[...]
         quart[...] = quart_in[...]
-    if w >= WINDOWS - 2:
-        sf_own, cw_own = sf, cw
-        sf, cw = take(2)
+    if w == WINDOWS - 2:
         sf[0:LEAVES] = sf_own[...]
         cw[0:LEAVES] = cw_own[...]
         for n, halo in enumerate(halos):
@@ -272,18 +273,20 @@
                 kh[at, lanes] = high
                 kl[at, lanes] = (k - high.astype(F)).astype(B)
 
-    def multiply(p, kh, kl, both):
+    def multiply(p, kh, kl, both, none=False):
         i, j = lists[0, p], lists[1, p]
         high, low_part = kh[...], kl[...]
-        acc[lists[2, p]] += dot(cw[j], high, NN) + dot(cw[j], low_part, NN)
+        to = jnp.where(none, LEAVES, lists[2, p])
+        acc[to] += dot(cw[j], high, NN) + dot(cw[j], low_part, NN)
         if both:
-            quart[lists[6, p]] += dot(call_w[i], high, NT) + dot(call_w[i], low_part, NT)
+            to = jnp.where(none, LEAVES, lists[6, p])
+            quart[to] += dot(call_w[i], high, NT) + dot(call_w[i], low_part, NT)
 
     def run(begin, end, both):
         def step(n, _):
             p = begin + 2 * n
             evaluate(p, kh_a, kl_a)
-            multiply(jnp.maximum(p - 1, begin), kh_b, kl_b, both)
+            multiply(jnp.maximum(p - 1, begin), kh_b, kl_b, both, n == 0)
             evaluate(p + 1, kh_b, kl_b)
             multiply(p, kh_a, kl_a, both)
             return 0
@@ -292,8 +295,6 @@
 
         @pl.when(steps > 0)
         def _():
-            kh_b[...] = jnp.zeros_like(kh_b)
-            kl_b[...] = jnp.zeros_like(kl_b)
             lax.fori_loop(0, steps, step, 0)
             multiply(begin + 2 * steps - 1, kh_b, kl_b, both)
 
@@ -327,7 +328,7 @@
     return v[0:8] + v[8:16]
 
 
-def up_kernel(charges, basis, transfer, _, out):
+def up_kernel(charges, basis, transfer, out):
     row = lax.broadcasted_iota(jnp.int32, (8, PTS), 0)
 
     def put(at, v):
@@ -414,15 +415,16 @@
         return lax.ppermute(v, "leaf", [(d, d ^ bit) for d in range(count)])
 
     first = swap_rhs(charges, 1)
+    onward = jnp.concatenate([charges, first], 0)
     lists, sf, tab, place = call(
         prep_kernel,
         [
-            jax.ShapeDtypeStruct((8, 320), jnp.int32),
+            jax.ShapeDtypeStruct((8, 128), jnp.int32),
             bf16(LEAVES, QUART, 32),
             bf16(LEAVES, 16, PTS),
             (2, LEAVES * QUART),
         ],
-        [SMEM, HBM, HBM, VMEM],
+        [SMEM, HBM, HBM, VMEM, ANY],
         [
             pltpu.SMEM((LEAVES, NEAR), jnp.int32),
             pltpu.SMEM((LEAVES,), jnp.int32),
@@ -430,11 +432,10 @@
         ],
         micros=4,
         smem_outs=1,
-    )(meta, near_list, near_count, coords)
-    onward = jnp.concatenate([charges, first], 0)
+    )(meta, near_list, near_count, coords, onward)
     second = swap_rhs(onward, 2)
-    (table,) = call(up_kernel, [(32, 2 * RANK)], [VMEM] * 3 + [ANY], micros=4)(
-        charges, leaf_basis, transfer, onward
+    (table,) = call(up_kernel, [(32, 2 * RANK)], [VMEM] * 3, micros=4)(
+        charges, leaf_basis, transfer
     )
 
     acc_shape, quart_shape = (LEAVES + 1, 16, PTS), (LEAVES + 1, 16, QUART)
@@ -451,9 +452,9 @@
             data += [cw, call_w, acc, quart]
         if w == WINDOWS - 1:
             scratch += [pltpu.VMEM(acc_shape, F), pltpu.VMEM(quart_shape, F)]
-        if w >= WINDOWS - 2:
+        if w == WINDOWS - 2:
             data += halos
-            scratch += [pltpu.VMEM((24, QUART, 32), B), pltpu.VMEM((24, 16, QUART), B)]
+            extra = [bf16(24, QUART, 32), bf16(24, 16, QUART)]
         carried = [after] if w < WINDOWS - 1 else []
         outs = [(2, LEAVES * PTS)] * 4 if w == WINDOWS - 1 else [acc_shape, quart_shape]
         result = call(
@@ -468,6 +469,8 @@
             break
         acc, quart = result[:2]
         after = jnp.concatenate([result[-1], swapped], 0)
+        if w == WINDOWS - 2:
+            sf, cw = result[2:4]
         if w == 0:
             cw, call_w, to_before, to_after = result[2:6]
             up = lax.ppermute(to_before, "leaf", [(i + 1, i) for i in range(count - 1)])

time: 100 us -> 96.9 us (0.969); the launches traced: 102 us -> 95.5 us
  Pallas kernels: 67.2 us -> 62.2 us
  starting transfers between devices: 29.2 us -> 25.2 us
  local copies, waits for them, and re-layouts: 2.43 us -> 4.53 us
    ppermute x6, starting transfers between devices: 12.7 us -> 8.69 us  [swap_leaf(): return lax.ppermute(v, 'leaf', [(d, d ^ bit) for d in range(count)])]
    pallas_call x1, Pallas kernels: 7.65 us -> 4.77 us  [shards(): call(down_kernel, [(2, LEAVES * PTS)], [SMEM] + [VMEM] * 5, [pltpu.VMEM((...]
    unnamed x27 -> x33, local copies, waits for them, and re-layouts: 2.38 us -> 4.48 us
    pallas_call x6, Pallas kernels: 52 us -> 50.1 us  [shards(): call(functools.partial(near_kernel, w, len(carried)), [*outs, *extra, *(v...]
  transfers between devices with their start and end apart: 13 -> 13, of which waited for: 1 -> 3; matrix products, arithmetic and copies ran while one was open for 0% -> 0% of each run, Pallas kernels for 66% -> 65%
where the time goes in v3:
time: 96.9 us; the launch traced here: 95.5 us
  Pallas kernels  62.2 us (64%)
  starting transfers between devices  25.2 us (26%)
  local copies, waits for them, and re-layouts  4.53 us (5%)
  waiting for transfers between devices  2.28 us (2%)
  other arithmetic  1 us (1%)
    pallas_call x6, Pallas kernels, shards(): call(functools.partial(near_kernel, w, len(carried)), [*outs, *extra, *(v...  50.1 us
    ppermute x5, starting transfers between devices, swap_rhs(): return lax.ppermute(v, 'rhs', [(i, i ^ k) for i in range(RHS)])  8.83 us
    ppermute x6, starting transfers between devices, swap_leaf(): return lax.ppermute(v, 'leaf', [(d, d ^ bit) for d in range(count)])  8.69 us
    ppermute x1, starting transfers between devices, shards(): up = lax.ppermute(to_before, 'leaf', [(i + 1, i) for i in range(count - 1)])  5.75 us
    pallas_call x1, Pallas kernels, shards(): call(prep_kernel, [jax.ShapeDtypeStruct((8, 128), jnp.int32), bf16(LEAVES...  4.93 us
    pallas_call x1, Pallas kernels, shards(): call(down_kernel, [(2, LEAVES * PTS)], [SMEM] + [VMEM] * 5, [pltpu.VMEM((...  4.77 us
    unnamed x33, local copies, waits for them, and re-layouts  4.48 us
    pallas_call x1, Pallas kernels, shards(): call(up_kernel, [(32, 2 * RANK)], [VMEM] * 3, micros=4)  2.4 us
  transfers between devices with their start and end apart: 13, of which 3 were waited for; matrix products, arithmetic and copies ran while one was open for 0% of the time, Pallas kernels for 65%

profile of v3, /device:TPU:6, one launch (start us, length us, event | category | flops | bytes accessed | tf_op | source)
XLA Modules:
  0.0 95.5 jit_solution(536405288940009876)
XLA Ops:
  0.0 1.7 %collective-permute-start = (f32[2,16384]{1,0:T(2,128)}, f32[2,16384]{1,0:T(2,128)S(1)}, u32[]{:S(2)}, u32[]{:S(2)}) collective-permute-start(f32[2,16384]{1,0:T(2,128)} %refs_4_.1), channel_id=1, source_target_pairs={{0,1},{1,0},{2,3},{3,2},{4,5},{5,4},{6,7},{7,6},{8,9},{9,8},{10,11... | collective-permute-start | bytes 393224 | tf_op jit(solution)/shard_map/ppermute | solution.py:412
  1.7 0.9 copy-done
  2.6 2.2 %copy-done.2 = f32[16,64,1024]{2,1,0:T(8,128)S(1)} copy-done((f32[16,64,1024]{2,1,0:T(8,128)S(1)}, f32[16,64,1024]{2,1,0:T(8,128)}, u32[]{:S(2)}) %copy-start.2) | copy-done | bytes 4194328
  4.8 1.2 %copy-done.5 = f32[2,15,64,64]{3,2,1,0:T(8,128)S(1)} copy-done((f32[2,15,64,64]{3,2,1,0:T(8,128)S(1)}, f32[2,15,64,64]{3,2,1,0:T(8,128)}, u32[]{:S(2)}) %copy-start.5) | copy-done | bytes 491544
  6.0 2.4 %shard_map.101.refs_8_ = f32[32,128]{1,0:T(8,128)S(1)} custom-call(f32[2,16384]{1,0:T(2,128)S(1)} %copy-done, f32[16,64,1024]{2,1,0:T(8,128)S(1)} %copy-done.2, f32[2,15,64,64]{3,2,1,0:T(8,128)S(1)} %copy-done.5), custom_call_target="tpu_custom_call" | custom-call | flops 4000000000 | bytes 100000 | tf_op jit(solution)/shard_map/pallas_call | solution.py:437
  8.4 1.9 %collective-permute-start.2 = (f32[32,128]{1,0:T(8,128)S(1)}, f32[32,128]{1,0:T(8,128)S(1)}, u32[]{:S(2)}, u32[]{:S(2)}) collective-permute-start(f32[32,128]{1,0:T(8,128)S(1)} %shard_map.101.refs_8_), channel_id=1, source_target_pairs={{0,8},{4,12},{8,0},{12,4},{16,24},{20,28},{24,16},{28,20},{32,40},... | collective-permute-start | bytes 49160 | tf_op jit(solution)/shard_map/ppermute | solution.py:415
  10.4 0.1 pad_add_fusion.meta
  10.5 0.1 pad_maximum_fusion._
  10.6 3.0 %collective-permute-start.1 = (f32[4,16384]{1,0:T(4,128)S(1)}, f32[4,16384]{1,0:T(4,128)S(1)}, u32[]{:S(2)}, u32[]{:S(2)}) collective-permute-start(f32[4,16384]{1,0:T(4,128)S(1)} %pad_maximum_fusion._), channel_id=1, source_target_pairs={{0,2},{1,3},{2,0},{3,1},{4,6},{5,7},{6,4},{7,5},{8,10},{9,11},{10,... | collective-permute-start | bytes 786440 | tf_op jit(solution)/shard_map/ppermute | solution.py:412
  13.6 4.9 %shard_map.100 = (s32[8,128]{1,0:T(8,128)S(1)}, bf16[16,256,32]{2,1,0:T(8,128)(2,1)S(1)}, bf16[16,16,1024]{2,1,0:T(8,128)(2,1)S(1)}, f32[2,4096]{1,0:T(2,128)S(1)}) custom-call(s32[2]{0:T(128)S(1)} %pad_add_fusion.meta, s32[16,9]{1,0:T(8,128)S(1)} %copy-done.8, s32[16]{0:T(128)S(1)} %copy-done.9, f32[2,16384]{1,0:T(2,128)S(1)} %copy-done.7, ...), custom_call_target="tpu_custom_call" | custom-call | flops 4000000000 | bytes 100000 | tf_op jit(solution)/shard_map/pallas_call | solution.py:419
  18.5 1.1 %collective-permute-done.1.refs_6_ = f32[4,16384]{1,0:T(4,128)S(1)} collective-permute-done((f32[4,16384]{1,0:T(4,128)S(1)}, f32[4,16384]{1,0:T(4,128)S(1)}, u32[]{:S(2)}, u32[]{:S(2)}) %collective-permute-start.1) | collective-permute-done | bytes 262176 | tf_op jit(solution)/shard_map/ppermute | solution.py:412
  19.7 7.1 %shard_map.102 = (f32[17,16,1024]{2,1,0:T(8,128)S(1)}, f32[17,16,256]{2,1,0:T(8,128)S(1)}, bf16[16,16,256]{2,1,0:T(8,128)(2,1)S(1)}, bf16[16,16,1024]{2,1,0:T(8,...) custom-call(s32[8,128]{1,0:T(8,128)S(1)} %get-tuple-element.34.refs_0_, ...), custom_call_target="tpu_custom_call" | custom-call | flops 8999999488 | bytes 100000 | tf_op jit(solution)/shard_map/pallas_call | solution.py:460
  26.8 0.0 collective-permute-done.2
  26.8 3.4 %collective-permute-start.3 = (f32[64,128]{1,0:T(8,128)S(1)}, f32[64,128]{1,0:T(8,128)S(1)}, u32[]{:S(2)}, u32[]{:S(2)}) collective-permute-start(f32[64,128]{1,0:T(8,128)S(1)} %constant_dynamic-update-slice_fusion.refs_8_), channel_id=1, source_target_pairs={{0,16},{4,20},{8,24},{12,28},{16,0},{20,4},{24,8},{28,12},{32,48},... | collective-permute-start | bytes 98312 | tf_op jit(solution)/shard_map/ppermute | solution.py:415
  30.2 8.3 %shard_map.103 = (f32[17,16,1024]{2,1,0:T(8,128)S(1)}, f32[17,16,256]{2,1,0:T(8,128)S(1)}, f32[64,128]{1,0:T(8,128)S(1)}) custom-call(s32[8,128]{1,0:T(8,128)S(1)} %get-tuple-element.34.refs_0_, f32[2,16384]{1,0:T(2,128)S(1)} %copy-done.7, bf16[16,16,1024]{2,1,0:T(8,128)(2,1)S(1)} %get-tuple-element.35.refs_2_, ...), custom_call_target="tpu_custom_call" | custom-call | flops 8999999488 | bytes 100000 | tf_op jit(solution)/shard_map/pallas_call | solution.py:460
  38.5 1.9 %collective-permute-start.5 = (f32[10,1024]{1,0:T(8,128)S(1)}, f32[10,1024]{1,0:T(8,128)S(1)}, u32[]{:S(2)}, u32[]{:S(2)}) collective-permute-start(f32[10,1024]{1,0:T(8,128)S(1)} %get-tuple-element.51), channel_id=1, source_target_pairs={{0,4},{4,8},{8,12},{12,16},{16,20},{20,24},{24,28},{28,32},{32,36}... | collective-permute-start | bytes 122888 | tf_op jit(solution)/shard_map/ppermute | solution.py:477
  40.5 5.8 %collective-permute-start.6 = (f32[10,1024]{1,0:T(8,128)S(1)}, f32[10,1024]{1,0:T(8,128)S(1)}, u32[]{:S(2)}, u32[]{:S(2)}) collective-permute-start(f32[10,1024]{1,0:T(8,128)S(1)} %get-tuple-element.52), channel_id=1, source_target_pairs={{4,0},{8,4},{12,8},{16,12},{20,16},{24,20},{28,24},{32,28},{36,32}... | collective-permute-start | bytes 122888 | tf_op jit(solution)/shard_map/ppermute | solution.py:476
  46.3 0.3 collective-permute-start.4
  46.5 8.3 %shard_map.104 = (f32[17,16,1024]{2,1,0:T(8,128)S(1)}, f32[17,16,256]{2,1,0:T(8,128)S(1)}, f32[128,128]{1,0:T(8,128)S(1)}) custom-call(s32[8,128]{1,0:T(8,128)S(1)} %get-tuple-element.34.refs_0_, f32[2,16384]{1,0:T(2,128)S(1)} %copy-done.7, bf16[16,16,1024]{2,1,0:T(8,128)(2,1)S(1)} %get-tuple-element.35.refs_2_, ...), custom_call_target="tpu_custom_call" | custom-call | flops 8999999488 | bytes 100000 | tf_op jit(solution)/shard_map/pallas_call | solution.py:460
  54.9 1.6 %collective-permute-start.7 = (f32[256,128]{1,0:T(8,128)S(1)}, f32[256,128]{1,0:T(8,128)S(1)}, u32[]{:S(2)}, u32[]{:S(2)}) collective-permute-start(f32[256,128]{1,0:T(8,128)S(1)} %constant_dynamic-update-slice_fusion.4.refs_8_), channel_id=1, source_target_pairs={{0,64},{4,68},{8,72},{12,76},{16,80},{20,84},{24,88},{28,92},{32,9... | collective-permute-start | bytes 393224 | tf_op jit(solution)/shard_map/ppermute | solution.py:415
  56.6 8.3 %shard_map.105 = (f32[17,16,1024]{2,1,0:T(8,128)S(1)}, f32[17,16,256]{2,1,0:T(8,128)S(1)}, f32[256,128]{1,0:T(8,128)S(1)}) custom-call(s32[8,128]{1,0:T(8,128)S(1)} %get-tuple-element.34.refs_0_, f32[2,16384]{1,0:T(2,128)S(1)} %copy-done.7, bf16[16,16,1024]{2,1,0:T(8,128)(2,1)S(1)} %get-tuple-element.35.refs_2_, ...), custom_call_target="tpu_custom_call" | custom-call | flops 8999999488 | bytes 100000 | tf_op jit(solution)/shard_map/pallas_call | solution.py:460
  65.0 0.1 collective-permute-start.8
  65.1 8.6 %shard_map.106 = (f32[17,16,1024]{2,1,0:T(8,128)S(1)}, f32[17,16,256]{2,1,0:T(8,128)S(1)}, bf16[24,256,32]{2,1,0:T(8,128)(2,1)S(1)}, bf16[24,16,256]{2,1,0:T(8,128)(2,1)S(1)}, f32[512,128]{1,0:T(8,128)S(1)}) custom-call(s32[8,128]{1,0:T(8,128)S(1)} %get-tuple-element.34.refs_0_, f32[2,16384]{1,0:T(2,128)S(1)} %copy-done.7, ...), custom_call_target="tpu_custom_call" | custom-call | flops 8999999488 | bytes 100000 | tf_op jit(solution)/shard_map/pallas_call | solution.py:460
  73.8 1.4 %collective-permute-start.9 = (f32[1024,128]{1,0:T(8,128)S(1)}, f32[1024,128]{1,0:T(8,128)S(1)}, u32[]{:S(2)}, u32[]{:S(2)}) collective-permute-start(f32[1024,128]{1,0:T(8,128)S(1)} %constant_dynamic-update-slice_fusion.8.own), channel_id=1, source_target_pairs={{0,4},{4,0},{8,12},{12,8},{16,20},{20,16},{24,28},{28,24},{32,36},... | collective-permute-start | bytes 1572872 | tf_op jit(solution)/shard_map/ppermute | solution.py:415
  75.2 9.4 %shard_map.108 = (f32[2,16384]{1,0:T(2,128)S(1)}, f32[2,16384]{1,0:T(2,128)S(1)}, f32[2,16384]{1,0:T(2,128)S(1)}, f32[2,16384]{1,0:T(2,128)S(1)}) custom-call(s32[8,128]{1,0:T(8,128)S(1)} %get-tuple-element.34.refs_0_, f32[2,16384]{1,0:T(2,128)S(1)} %copy-done.7, bf16[16,16,1024]{2,1,0:T(8,128)(2,1)S(1)} %get-tuple-element.35.refs_2_, ...), custom_call_target="tpu_custom_call" | custom-call | flops 8999999488 | bytes 100000 | tf_op jit(solution)/shard_map/pallas_call | solution.py:460
  84.6 3.0 %collective-permute-start.10 = (f32[2,16384]{1,0:T(2,128)S(1)}, f32[2,16384]{1,0:T(2,128)S(1)}, u32[]{:S(2)}, u32[]{:S(2)}) collective-permute-start(f32[2,16384]{1,0:T(2,128)S(1)} %get-tuple-element.60), channel_id=1, source_target_pairs={{0,2},{1,3},{2,0},{3,1},{4,6},{5,7},{6,4},{7,5},{8,10},{9,11},{10,... | collective-permute-start | bytes 393224 | tf_op jit(solution)/shard_map/ppermute | solution.py:412
  87.6 0.1 collective-permute-start.11
  87.7 1.1 %collective-permute-start.12 = (f32[2,16384]{1,0:T(2,128)S(1)}, f32[2,16384]{1,0:T(2,128)S(1)}, u32[]{:S(2)}, u32[]{:S(2)}) collective-permute-start(f32[2,16384]{1,0:T(2,128)S(1)} %get-tuple-element.62), channel_id=1, source_target_pairs={{0,3},{1,2},{2,1},{3,0},{4,7},{5,6},{6,5},{7,4},{8,11},{9,10},{10,... | collective-permute-start | bytes 393224 | tf_op jit(solution)/shard_map/ppermute | solution.py:412
  88.8 4.8 %shard_map.107 = f32[2,16384]{1,0:T(2,128)S(1)} custom-call(s32[2,124]{1,0:T(2,128)S(1)} %and_add_fusion.rows, f32[1024,128]{1,0:T(8,128)S(1)} %constant_dynamic-update-slice_fusion.8.own, f32[1024,128]{1,0:T(8,128)S(1)} %collective-permute-done.9.other, f32[2,64,64,124]{3,2,1,0:T(8,128)S(1)} %bitcast.3, f32[2,15,64,64]{3,2,1,0:T(8,128)S(1)} %copy-done.6, ...), custom_call_target="tpu_custom_call" | custom-call | flops 8000000000 | bytes 100000 | tf_op jit(solution)/shard_map/pallas_call | solution.py:488
  93.6 0.4 collective-permute-done.11
  94.0 0.7 collective-permute-done.12
  94.7 0.8 add_add_fusion
  (45 shorter events, 0.2 us)
Async XLA Ops:
  0.0 10.4 %copy-start.11 = (s32[124]{0:T(128)S(1)}, s32[124]{0:T(128)}, u32[]{:S(2)}) copy-start(s32[124]{0:T(128)} %constant.25.clone) | copy-start | bytes 1492
  0.0 10.4 %copy-start.12 = (s32[124]{0:T(128)S(1)}, s32[124]{0:T(128)}, u32[]{:S(2)}) copy-start(s32[124]{0:T(128)} %constant.34) | copy-start | bytes 1492
  0.0 10.4 %copy-start.13 = (s32[124]{0:T(128)S(1)}, s32[124]{0:T(128)}, u32[]{:S(2)}) copy-start(s32[124]{0:T(128)} %constant.36) | copy-start | bytes 1492
  0.0 10.5 %collective-permute-start = (f32[2,16384]{1,0:T(2,128)}, f32[2,16384]{1,0:T(2,128)S(1)}, u32[]{:S(2)}, u32[]{:S(2)}) collective-permute-start(f32[2,16384]{1,0:T(2,128)} %refs_4_.1), channel_id=1, source_target_pairs={{0,1},{1,0},{2,3},{3,2},{4,5},{5,4},{6,7},{7,6},{8,9},{9,8},{10,11... | collective-permute-start | bytes 393224 | tf_op jit(solution)/shard_map/ppermute | solution.py:412
  1.7 0.9 copy-start
  2.6 2.2 %copy-start.2 = (f32[16,64,1024]{2,1,0:T(8,128)S(1)}, f32[16,64,1024]{2,1,0:T(8,128)}, u32[]{:S(2)}) copy-start(f32[16,64,1024]{2,1,0:T(8,128)} %basis.3) | copy-start | bytes 12582916
  4.8 1.2 %copy-start.5 = (f32[2,15,64,64]{3,2,1,0:T(8,128)S(1)}, f32[2,15,64,64]{3,2,1,0:T(8,128)}, u32[]{:S(2)}) copy-start(f32[2,15,64,64]{3,2,1,0:T(8,128)} %transfer.3) | copy-start | bytes 1474564
  6.0 4.4 %copy-start.10 = (s32[2,124]{1,0:T(2,128)S(1)}, s32[2,124]{1,0:T(2,128)}, u32[]{:S(2)}) copy-start(s32[2,124]{1,0:T(2,128)} %param.15) | copy-start | bytes 2980
  6.0 4.5 %copy-start.1 = (f32[2,16384]{1,0:T(2,128)S(1)}, f32[2,16384]{1,0:T(2,128)}, u32[]{:S(2)}) copy-start(f32[2,16384]{1,0:T(2,128)} %refs_4_.1) | copy-start | bytes 393220
  6.0 7.6 %copy-start.7 = (f32[2,16384]{1,0:T(2,128)S(1)}, f32[2,16384]{1,0:T(2,128)}, u32[]{:S(2)}) copy-start(f32[2,16384]{1,0:T(2,128)} %refs_1_.11) | copy-start | bytes 393220
  6.0 7.6 %copy-start.8 = (s32[16,9]{1,0:T(8,128)S(1)}, s32[16,9]{1,0:T(8,128)}, u32[]{:S(2)}) copy-start(s32[16,9]{1,0:T(8,128)} %list_hbm.1) | copy-start | bytes 1732
  6.0 7.6 %copy-start.9 = (s32[16]{0:T(128)S(1)}, s32[16]{0:T(128)}, u32[]{:S(2)}) copy-start(s32[16]{0:T(128)} %count_hbm.1) | copy-start | bytes 196
  8.4 18.4 %collective-permute-start.2 = (f32[32,128]{1,0:T(8,128)S(1)}, f32[32,128]{1,0:T(8,128)S(1)}, u32[]{:S(2)}, u32[]{:S(2)}) collective-permute-start(f32[32,128]{1,0:T(8,128)S(1)} %shard_map.101.refs_8_), channel_id=1, source_target_pairs={{0,8},{4,12},{8,0},{12,4},{16,24},{20,28},{24,16},{28,20},{32,40},... | collective-permute-start | bytes 49160 | tf_op jit(solution)/shard_map/ppermute | solution.py:415
  10.6 9.1 %collective-permute-start.1 = (f32[4,16384]{1,0:T(4,128)S(1)}, f32[4,16384]{1,0:T(4,128)S(1)}, u32[]{:S(2)}, u32[]{:S(2)}) collective-permute-start(f32[4,16384]{1,0:T(4,128)S(1)} %pad_maximum_fusion._), channel_id=1, source_target_pairs={{0,2},{1,3},{2,0},{3,1},{4,6},{5,7},{6,4},{7,5},{8,10},{9,11},{10,... | collective-permute-start | bytes 786440 | tf_op jit(solution)/shard_map/ppermute | solution.py:412
  26.8 19.4 %collective-permute-start.3 = (f32[64,128]{1,0:T(8,128)S(1)}, f32[64,128]{1,0:T(8,128)S(1)}, u32[]{:S(2)}, u32[]{:S(2)}) collective-permute-start(f32[64,128]{1,0:T(8,128)S(1)} %constant_dynamic-update-slice_fusion.refs_8_), channel_id=1, source_target_pairs={{0,16},{4,20},{8,24},{12,28},{16,0},{20,4},{24,8},{28,12},{32,48},... | collective-permute-start | bytes 98312 | tf_op jit(solution)/shard_map/ppermute | solution.py:415
  38.5 26.6 %collective-permute-start.5 = (f32[10,1024]{1,0:T(8,128)S(1)}, f32[10,1024]{1,0:T(8,128)S(1)}, u32[]{:S(2)}, u32[]{:S(2)}) collective-permute-start(f32[10,1024]{1,0:T(8,128)S(1)} %get-tuple-element.51), channel_id=1, source_target_pairs={{0,4},{4,8},{8,12},{12,16},{16,20},{20,24},{24,28},{28,32},{32,36}... | collective-permute-start | bytes 122888 | tf_op jit(solution)/shard_map/ppermute | solution.py:477
  40.5 24.6 %collective-permute-start.6 = (f32[10,1024]{1,0:T(8,128)S(1)}, f32[10,1024]{1,0:T(8,128)S(1)}, u32[]{:S(2)}, u32[]{:S(2)}) collective-permute-start(f32[10,1024]{1,0:T(8,128)S(1)} %get-tuple-element.52), channel_id=1, source_target_pairs={{4,0},{8,4},{12,8},{16,12},{20,16},{24,20},{28,24},{32,28},{36,32}... | collective-permute-start | bytes 122888 | tf_op jit(solution)/shard_map/ppermute | solution.py:476
  46.3 8.7 %collective-permute-start.4 = (f32[128,128]{1,0:T(8,128)S(1)}, f32[128,128]{1,0:T(8,128)S(1)}, u32[]{:S(2)}, u32[]{:S(2)}) collective-permute-start(f32[128,128]{1,0:T(8,128)S(1)} %constant_dynamic-update-slice_fusion.2.refs_8_), channel_id=1, source_target_pairs={{0,32},{4,36},{8,40},{12,44},{16,48},{20,52},{24,56},{28,60},{32,0... | collective-permute-start | bytes 196616 | tf_op jit(solution)/shard_map/ppermute | solution.py:415
  54.9 10.0 %collective-permute-start.7 = (f32[256,128]{1,0:T(8,128)S(1)}, f32[256,128]{1,0:T(8,128)S(1)}, u32[]{:S(2)}, u32[]{:S(2)}) collective-permute-start(f32[256,128]{1,0:T(8,128)S(1)} %constant_dynamic-update-slice_fusion.4.refs_8_), channel_id=1, source_target_pairs={{0,64},{4,68},{8,72},{12,76},{16,80},{20,84},{24,88},{28,92},{32,9... | collective-permute-start | bytes 393224 | tf_op jit(solution)/shard_map/ppermute | solution.py:415
  65.0 8.8 %collective-permute-start.8 = (f32[512,128]{1,0:T(8,128)S(1)}, f32[512,128]{1,0:T(8,128)S(1)}, u32[]{:S(2)}, u32[]{:S(2)}) collective-permute-start(f32[512,128]{1,0:T(8,128)S(1)} %constant_dynamic-update-slice_fusion.6.refs_10_), channel_id=1, source_target_pairs={{0,128},{4,132},{8,136},{12,140},{16,144},{20,148},{24,152},{28,15... | collective-permute-start | bytes 786440 | tf_op jit(solution)/shard_map/ppermute | solution.py:415
  73.8 15.0 %collective-permute-start.9 = (f32[1024,128]{1,0:T(8,128)S(1)}, f32[1024,128]{1,0:T(8,128)S(1)}, u32[]{:S(2)}, u32[]{:S(2)}) collective-permute-start(f32[1024,128]{1,0:T(8,128)S(1)} %constant_dynamic-update-slice_fusion.8.own), channel_id=1, source_target_pairs={{0,4},{4,0},{8,12},{12,8},{16,20},{20,16},{24,28},{28,24},{32,36},... | collective-permute-start | bytes 1572872 | tf_op jit(solution)/shard_map/ppermute | solution.py:415
  75.2 13.6 %copy-start.3 = (f32[16,64,1024]{2,1,0:T(8,128)S(1)}, f32[16,64,1024]{2,1,0:T(8,128)}, u32[]{:S(2)}) copy-start(f32[16,64,1024]{2,1,0:T(8,128)} %basis.3) | copy-start | bytes 12582916
  75.2 13.6 %copy-start.4 = (f32[2,124,64,64]{1,3,2,0:T(8,128)S(1)}, f32[2,124,64,64]{1,3,2,0:T(8,128)}, u32[]{:S(2)}) copy-start(f32[2,124,64,64]{1,3,2,0:T(8,128)} %param.14) | copy-start | bytes 12189700
  75.2 13.6 %copy-start.6 = (f32[2,15,64,64]{3,2,1,0:T(8,128)S(1)}, f32[2,15,64,64]{3,2,1,0:T(8,128)}, u32[]{:S(2)}) copy-start(f32[2,15,64,64]{3,2,1,0:T(8,128)} %transfer.3) | copy-start | bytes 1474564
  84.6 9.0 %collective-permute-start.10 = (f32[2,16384]{1,0:T(2,128)S(1)}, f32[2,16384]{1,0:T(2,128)S(1)}, u32[]{:S(2)}, u32[]{:S(2)}) collective-permute-start(f32[2,16384]{1,0:T(2,128)S(1)} %get-tuple-element.60), channel_id=1, source_target_pairs={{0,2},{1,3},{2,0},{3,1},{4,6},{5,7},{6,4},{7,5},{8,10},{9,11},{10,... | collective-permute-start | bytes 393224 | tf_op jit(solution)/shard_map/ppermute | solution.py:412
  87.6 6.4 %collective-permute-start.11 = (f32[2,16384]{1,0:T(2,128)S(1)}, f32[2,16384]{1,0:T(2,128)S(1)}, u32[]{:S(2)}, u32[]{:S(2)}) collective-permute-start(f32[2,16384]{1,0:T(2,128)S(1)} %get-tuple-element.61), channel_id=1, source_target_pairs={{0,1},{1,0},{2,3},{3,2},{4,5},{5,4},{6,7},{7,6},{8,9},{9,8},{10,11... | collective-permute-start | bytes 393224 | tf_op jit(solution)/shard_map/ppermute | solution.py:412
  87.7 6.9 %collective-permute-start.12 = (f32[2,16384]{1,0:T(2,128)S(1)}, f32[2,16384]{1,0:T(2,128)S(1)}, u32[]{:S(2)}, u32[]{:S(2)}) collective-permute-start(f32[2,16384]{1,0:T(2,128)S(1)} %get-tuple-element.62), channel_id=1, source_target_pairs={{0,3},{1,2},{2,1},{3,0},{4,7},{5,6},{6,5},{7,4},{8,11},{9,10},{10,... | collective-permute-start | bytes 393224 | tf_op jit(solution)/shard_map/ppermute | solution.py:412

commit v4 on v3

--- a/solution.py
+++ b/solution.py
@@ -30,6 +30,8 @@
 PAIRS = 124
 WINDOWS = 6
 SINGLE = 80
+EDGE = 128
+SHIFTS = (-8, -1, 2, -4, 32, -16)
 ANY = pl.BlockSpec(memory_space=pl.ANY)
 HBM = pl.BlockSpec(memory_space=pltpu.HBM)
 VMEM = pl.BlockSpec(memory_space=pltpu.VMEM)
@@ -194,7 +196,7 @@
     carried = take(n_carried)
     outs = take(4 if last else 2)
     if w == 0:
-        cw, call_w, to_before, to_after = take(4)
+        cw, call_w, payload = take(3)
     if w == WINDOWS - 2:
         sf_own, cw_own = sf, cw
         sf, cw = take(2)
@@ -210,14 +212,17 @@
             at = slice(j * PTS, (j + 1) * PTS)
             call_w[j] = weights(jnp.concatenate([own[:, at], first[:, at], second[:, at]], axis=0))
             cw[j] = call_w[j, :, mine]
-        for ref, start in ((to_before, 0), (to_after, 12)):
-            ref[0:2] = place[:, start * QUART : (start + 4) * QUART]
-            for j in range(4):
-                at = slice(j * QUART, (j + 1) * QUART)
-                source = pl.ds(pl.multiple_of(r * QUART + (start + j) * PTS, QUART), QUART)
-                ref[2:4, at] = own[:, source]
-                ref[4:6, at] = first[:, source]
-                ref[6:10, at] = second[:, source]
+        payload[...] = jnp.zeros_like(payload)
+        for end, start in enumerate((0, 12)):
+            for m in range(8):
+                top = end * EDGE + 16 * m
+                at = (start + m // 2) * QUART + m % 2 * 128
+                payload[top : top + 2] = place[:, at : at + 128]
+                at = r * QUART + (start + m // 2) * PTS + m % 2 * 128
+                source = pl.ds(pl.multiple_of(at, 128), 128)
+                payload[top + 2 : top + 4] = own[:, source]
+                payload[top + 4 : top + 6] = first[:, source]
+                payload[top + 6 : top + 10] = second[:, source]
         acc[...] = jnp.zeros_like(acc)
         quart[...] = jnp.zeros_like(quart)
     else:
@@ -227,6 +232,7 @@
         sf[0:LEAVES] = sf_own[...]
         cw[0:LEAVES] = cw_own[...]
         for n, halo in enumerate(halos):
+            halo = jnp.concatenate([halo[16 * m : 16 * m + 10] for m in range(8)], axis=1)
             put_sources(halo[0:2] - 0.5, sf, LEAVES + 4 * n)
             for j in range(4):
                 cw[LEAVES + 4 * n + j] = weights(halo[2:10, j * QUART : (j + 1) * QUART])
@@ -411,8 +417,8 @@
     def swap_rhs(v, k):
         return lax.ppermute(v, "rhs", [(i, i ^ k) for i in range(RHS)])
 
-    def swap_leaf(v, bit):
-        return lax.ppermute(v, "leaf", [(d, d ^ bit) for d in range(count)])
+    def shift_leaf(v, s):
+        return lax.ppermute(v, "leaf", [(d, (d + s) % count) for d in range(count)])
 
     first = swap_rhs(charges, 1)
     onward = jnp.concatenate([charges, first], 0)
@@ -439,21 +445,25 @@
     )
 
     acc_shape, quart_shape = (LEAVES + 1, 16, PTS), (LEAVES + 1, 16, QUART)
-    halo_shape = (10, 4 * QUART)
     values = [pltpu.VMEM((QUART, PTS), B)] * 4
-    after, halos = table, []
-    for w, bit in enumerate((2, 4, 8, 16, 32, 1)):
-        swapped = swap_leaf(after, bit)
+    after, edges = table, None
+    for w, s in enumerate(SHIFTS):
+        rows = after.shape[0]
+        got = shift_leaf(after if edges is None else jnp.concatenate([after, edges], 0), s)
+        if w == 1:
+            up, edges = got[rows : rows + EDGE], got[rows + EDGE :]
+        if w == 2:
+            down, edges = got[rows:], None
         data, extra, scratch = [lists, coords, tab, sf], [], [*values]
         if w == 0:
             data += [charges, first, second, place]
-            extra = [bf16(LEAVES, 16, QUART), bf16(LEAVES, 16, PTS), halo_shape, halo_shape]
+            extra = [bf16(LEAVES, 16, QUART), bf16(LEAVES, 16, PTS), (2 * EDGE, 128)]
         else:
             data += [cw, call_w, acc, quart]
         if w == WINDOWS - 1:
             scratch += [pltpu.VMEM(acc_shape, F), pltpu.VMEM(quart_shape, F)]
         if w == WINDOWS - 2:
-            data += halos
+            data += [down, up]
             extra = [bf16(24, QUART, 32), bf16(24, 16, QUART)]
         carried = [after] if w < WINDOWS - 1 else []
         outs = [(2, LEAVES * PTS)] * 4 if w == WINDOWS - 1 else [acc_shape, quart_shape]
@@ -468,22 +478,26 @@
             whole = result
             break
         acc, quart = result[:2]
-        after = jnp.concatenate([result[-1], swapped], 0)
+        after = jnp.concatenate([result[-1], got[:rows]], 0)
+        if w == 0:
+            cw, call_w, edges = result[2:5]
         if w == WINDOWS - 2:
             sf, cw = result[2:4]
-        if w == 0:
-            cw, call_w, to_before, to_after = result[2:6]
-            up = lax.ppermute(to_before, "leaf", [(i + 1, i) for i in range(count - 1)])
-            down = lax.ppermute(to_after, "leaf", [(i, i + 1) for i in range(count - 1)])
-            halos = [down, up]
-    other = swapped
+    other = got
 
     level = jnp.asarray([k for k in range(5) for _ in range(64 >> k)], jnp.int32)[None, :]
     owner = lax.shift_right_logical(far_pairs, 4 - level)
     inside = far_pairs & (lax.shift_left(jnp.int32(1), 4 - level) - 1)
     start = jnp.asarray([LEVEL_ROW[k] for k in range(5) for _ in range(64 >> k)], jnp.int32)[None, :]
-    apart = device ^ owner
-    rows = ((apart & 1) * (count // 2) + (apart >> 1)) * 32 + start + inside
+    place_on = (owner - device) & (count - 1)
+    bit_1 = place_on & 1
+    half = lax.shift_right_logical(place_on, 1)
+    bit_2 = half & 1
+    fourth = lax.shift_right_logical(half + bit_2, 1)
+    bit_3 = fourth & 1
+    bit_0, bit_5, bit_4 = (lax.shift_right_logical(fourth, n) & 1 for n in (1, 2, 3))
+    block = bit_0 + 2 * bit_1 + 4 * bit_2 + 8 * bit_3 + 16 * bit_4 + 32 * bit_5
+    rows = block * 32 + start + inside
     back = [swap_rhs(whole[k], k) for k in (2, 1, 3)]
     (distant,) = call(
         down_kernel,

time: 96.9 us -> 93.4 us (0.964)
  the two profiles are of different devices: /device:TPU:6 before, /device:TPU:34 now
where the time goes in v4:
time: 93.4 us; the launch traced here: 92.8 us
  Pallas kernels  60.7 us (65%)
  starting transfers between devices  23.7 us (25%)
  local copies, waits for them, and re-layouts  4.56 us (5%)
  waiting for transfers between devices  2.44 us (3%)
  other arithmetic  1.09 us (1%)
    pallas_call x6, Pallas kernels, shards(): call(functools.partial(near_kernel, w, len(carried)), [*outs, *extra, *(v...  48.7 us
    ppermute x6, starting transfers between devices, shift_leaf(): return lax.ppermute(v, 'leaf', [(d, (d + s) % count) for d in range(count)])  14.9 us
    ppermute x5, starting transfers between devices, swap_rhs(): return lax.ppermute(v, 'rhs', [(i, i ^ k) for i in range(RHS)])  8.83 us
    pallas_call x1, Pallas kernels, shards(): call(prep_kernel, [jax.ShapeDtypeStruct((8, 128), jnp.int32), bf16(LEAVES...  4.84 us
    pallas_call x1, Pallas kernels, shards(): call(down_kernel, [(2, LEAVES * PTS)], [SMEM] + [VMEM] * 5, [pltpu.VMEM((...  4.77 us
    unnamed x30, local copies, waits for them, and re-layouts  4.44 us
    ppermute x5, waiting for transfers between devices, swap_rhs(): return lax.ppermute(v, 'rhs', [(i, i ^ k) for i in range(RHS)])  2.43 us
    pallas_call x1, Pallas kernels, shards(): call(up_kernel, [(32, 2 * RANK)], [VMEM] * 3, micros=4)  2.4 us
  transfers between devices with their start and end apart: 11, of which 2 were waited for; matrix products, arithmetic and copies ran while one was open for 0% of the time, Pallas kernels for 65%

profile of v4, /device:TPU:34, one launch (start us, length us, event | category | flops | bytes accessed | tf_op | source)
XLA Modules:
  0.0 92.8 jit_solution(18062039725980344207)
XLA Ops:
  0.0 1.7 %collective-permute-start = (f32[2,16384]{1,0:T(2,128)}, f32[2,16384]{1,0:T(2,128)S(1)}, u32[]{:S(2)}, u32[]{:S(2)}) collective-permute-start(f32[2,16384]{1,0:T(2,128)} %refs_4_.1), channel_id=1, source_target_pairs={{0,1},{1,0},{2,3},{3,2},{4,5},{5,4},{6,7},{7,6},{8,9},{9,8},{10,11... | collective-permute-start | bytes 393224 | tf_op jit(solution)/shard_map/ppermute | solution.py:418
  1.7 0.9 %copy-done = f32[2,16384]{1,0:T(2,128)S(1)} copy-done((f32[2,16384]{1,0:T(2,128)S(1)}, f32[2,16384]{1,0:T(2,128)}, u32[]{:S(2)}) %copy-start) | copy-done | bytes 131096
  2.6 2.2 %copy-done.2 = f32[16,64,1024]{2,1,0:T(8,128)S(1)} copy-done((f32[16,64,1024]{2,1,0:T(8,128)S(1)}, f32[16,64,1024]{2,1,0:T(8,128)}, u32[]{:S(2)}) %copy-start.2) | copy-done | bytes 4194328
  4.8 1.2 %copy-done.5 = f32[2,15,64,64]{3,2,1,0:T(8,128)S(1)} copy-done((f32[2,15,64,64]{3,2,1,0:T(8,128)S(1)}, f32[2,15,64,64]{3,2,1,0:T(8,128)}, u32[]{:S(2)}) %copy-start.5) | copy-done | bytes 491544
  6.0 2.4 %shard_map.101.refs_8_ = f32[32,128]{1,0:T(8,128)S(1)} custom-call(f32[2,16384]{1,0:T(2,128)S(1)} %copy-done, f32[16,64,1024]{2,1,0:T(8,128)S(1)} %copy-done.2, f32[2,15,64,64]{3,2,1,0:T(8,128)S(1)} %copy-done.5), custom_call_target="tpu_custom_call" | custom-call | flops 4000000000 | bytes 100000 | tf_op jit(solution)/shard_map/pallas_call | solution.py:443
  8.4 6.3 %collective-permute-start.2 = (f32[32,128]{1,0:T(8,128)S(1)}, f32[32,128]{1,0:T(8,128)S(1)}, u32[]{:S(2)}, u32[]{:S(2)}) collective-permute-start(f32[32,128]{1,0:T(8,128)S(1)} %shard_map.101.refs_8_), channel_id=1, source_target_pairs={{0,224},{4,228},{8,232},{12,236},{16,240},{20,244},{24,248},{28,25... | collective-permute-start | bytes 49160 | tf_op jit(solution)/shard_map/ppermute | solution.py:421
  14.7 0.1 pad_add_fusion.meta
  14.8 0.1 pad_maximum_fusion._
  15.0 3.0 %collective-permute-start.1 = (f32[4,16384]{1,0:T(4,128)S(1)}, f32[4,16384]{1,0:T(4,128)S(1)}, u32[]{:S(2)}, u32[]{:S(2)}) collective-permute-start(f32[4,16384]{1,0:T(4,128)S(1)} %pad_maximum_fusion._), channel_id=1, source_target_pairs={{0,2},{1,3},{2,0},{3,1},{4,6},{5,7},{6,4},{7,5},{8,10},{9,11},{10,... | collective-permute-start | bytes 786440 | tf_op jit(solution)/shard_map/ppermute | solution.py:418
  17.9 4.8 %shard_map.100 = (s32[8,128]{1,0:T(8,128)S(1)}, bf16[16,256,32]{2,1,0:T(8,128)(2,1)S(1)}, bf16[16,16,1024]{2,1,0:T(8,128)(2,1)S(1)}, f32[2,4096]{1,0:T(2,128)S(1)}) custom-call(s32[2]{0:T(128)S(1)} %pad_add_fusion.meta, s32[16,9]{1,0:T(8,128)S(1)} %copy-done.8, s32[16]{0:T(128)S(1)} %copy-done.9, f32[2,16384]{1,0:T(2,128)S(1)} %copy-done.7, ...), custom_call_target="tpu_custom_call" | custom-call | flops 4000000000 | bytes 100000 | tf_op jit(solution)/shard_map/pallas_call | solution.py:425
  22.8 1.2 %collective-permute-done.1.refs_6_ = f32[4,16384]{1,0:T(4,128)S(1)} collective-permute-done((f32[4,16384]{1,0:T(4,128)S(1)}, f32[4,16384]{1,0:T(4,128)S(1)}, u32[]{:S(2)}, u32[]{:S(2)}) %collective-permute-start.1) | collective-permute-done | bytes 262176 | tf_op jit(solution)/shard_map/ppermute | solution.py:418
  24.0 7.1 %shard_map.102 = (f32[17,16,1024]{2,1,0:T(8,128)S(1)}, f32[17,16,256]{2,1,0:T(8,128)S(1)}, bf16[16,16,256]{2,1,0:T(8,128)(2,1)S(1)}, bf16[16,16,1024]{2,1,0:T(8,...) custom-call(s32[8,128]{1,0:T(8,128)S(1)} %get-tuple-element.33.refs_0_, f32[2,16384]{1,0:T(2,128)S(1)} %copy-done.7, ...), custom_call_target="tpu_custom_call" | custom-call | flops 8999999488 | bytes 100000 | tf_op jit(solution)/shard_map/pallas_call | solution.py:470
  31.1 0.0 collective-permute-done.2
  31.2 0.1 collective-permute-start.3
  31.3 8.3 %shard_map.103 = (f32[17,16,1024]{2,1,0:T(8,128)S(1)}, f32[17,16,256]{2,1,0:T(8,128)S(1)}, f32[64,128]{1,0:T(8,128)S(1)}) custom-call(s32[8,128]{1,0:T(8,128)S(1)} %get-tuple-element.33.refs_0_, f32[2,16384]{1,0:T(2,128)S(1)} %copy-done.7, bf16[16,16,1024]{2,1,0:T(8,128)(2,1)S(1)} %get-tuple-element.34.refs_2_, ...), custom_call_target="tpu_custom_call" | custom-call | flops 8999999488 | bytes 100000 | tf_op jit(solution)/shard_map/pallas_call | solution.py:470
  39.7 2.7 %collective-permute-start.4 = (f32[256,128]{1,0:T(8,128)S(1)}, f32[256,128]{1,0:T(8,128)S(1)}, u32[]{:S(2)}, u32[]{:S(2)}) collective-permute-start(f32[256,128]{1,0:T(8,128)S(1)} %pad_maximum_fusion.2), channel_id=1, source_target_pairs={{0,8},{4,12},{8,16},{12,20},{16,24},{20,28},{24,32},{28,36},{32,40... | collective-permute-start | bytes 393224 | tf_op jit(solution)/shard_map/ppermute | solution.py:421
  42.4 6.9 %shard_map.104 = (f32[17,16,1024]{2,1,0:T(8,128)S(1)}, f32[17,16,256]{2,1,0:T(8,128)S(1)}, f32[128,128]{1,0:T(8,128)S(1)}) custom-call(s32[8,128]{1,0:T(8,128)S(1)} %get-tuple-element.33.refs_0_, f32[2,16384]{1,0:T(2,128)S(1)} %copy-done.7, bf16[16,16,1024]{2,1,0:T(8,128)(2,1)S(1)} %get-tuple-element.34.refs_2_, ...), custom_call_target="tpu_custom_call" | custom-call | flops 8999999488 | bytes 100000 | tf_op jit(solution)/shard_map/pallas_call | solution.py:470
  49.4 0.0 collective-permute-done.4
  49.4 0.1 collective-permute-start.5
  49.5 8.3 %shard_map.105 = (f32[17,16,1024]{2,1,0:T(8,128)S(1)}, f32[17,16,256]{2,1,0:T(8,128)S(1)}, f32[256,128]{1,0:T(8,128)S(1)}) custom-call(s32[8,128]{1,0:T(8,128)S(1)} %get-tuple-element.33.refs_0_, f32[2,16384]{1,0:T(2,128)S(1)} %copy-done.7, bf16[16,16,1024]{2,1,0:T(8,128)(2,1)S(1)} %get-tuple-element.34.refs_2_, ...), custom_call_target="tpu_custom_call" | custom-call | flops 8999999488 | bytes 100000 | tf_op jit(solution)/shard_map/pallas_call | solution.py:470
  57.9 0.0 collective-permute-done.5
  57.9 1.8 %collective-permute-start.6 = (f32[512,128]{1,0:T(8,128)S(1)}, f32[512,128]{1,0:T(8,128)S(1)}, u32[]{:S(2)}, u32[]{:S(2)}) collective-permute-start(f32[512,128]{1,0:T(8,128)S(1)} %constant_dynamic-update-slice_fusion.refs_10_), channel_id=1, source_target_pairs={{0,128},{4,132},{8,136},{12,140},{16,144},{20,148},{24,152},{28,15... | collective-permute-start | bytes 786440 | tf_op jit(solution)/shard_map/ppermute | solution.py:421
  59.7 9.6 %shard_map.106 = (f32[17,16,1024]{2,1,0:T(8,128)S(1)}, f32[17,16,256]{2,1,0:T(8,128)S(1)}, bf16[24,256,32]{2,1,0:T(8,128)(2,1)S(1)}, bf16[24,16,256]{2,1,0:T(8,128)(2,1)S(1)}, f32[512,128]{1,0:T(8,128)S(1)}) custom-call(s32[8,128]{1,0:T(8,128)S(1)} %get-tuple-element.33.refs_0_, f32[2,16384]{1,0:T(2,128)S(1)} %copy-done.7, ...), custom_call_target="tpu_custom_call" | custom-call | flops 8999999488 | bytes 100000 | tf_op jit(solution)/shard_map/pallas_call | solution.py:470
  69.3 4.0 %collective-permute-start.7 = (f32[1024,128]{1,0:T(8,128)S(1)}, f32[1024,128]{1,0:T(8,128)S(1)}, u32[]{:S(2)}, u32[]{:S(2)}) collective-permute-start(f32[1024,128]{1,0:T(8,128)S(1)} %constant_dynamic-update-slice_fusion.2.own), channel_id=1, source_target_pairs={{0,192},{4,196},{8,200},{12,204},{16,208},{20,212},{24,216},{28,22... | collective-permute-start | bytes 1572872 | tf_op jit(solution)/shard_map/ppermute | solution.py:421
  73.3 8.5 %shard_map.108 = (f32[2,16384]{1,0:T(2,128)S(1)}, f32[2,16384]{1,0:T(2,128)S(1)}, f32[2,16384]{1,0:T(2,128)S(1)}, f32[2,16384]{1,0:T(2,128)S(1)}) custom-call(s32[8,128]{1,0:T(8,128)S(1)} %get-tuple-element.33.refs_0_, f32[2,16384]{1,0:T(2,128)S(1)} %copy-done.7, bf16[16,16,1024]{2,1,0:T(8,128)(2,1)S(1)} %get-tuple-element.34.refs_2_, ...), custom_call_target="tpu_custom_call" | custom-call | flops 8999999488 | bytes 100000 | tf_op jit(solution)/shard_map/pallas_call | solution.py:470
  81.8 2.2 %collective-permute-start.10 = (f32[2,16384]{1,0:T(2,128)S(1)}, f32[2,16384]{1,0:T(2,128)S(1)}, u32[]{:S(2)}, u32[]{:S(2)}) collective-permute-start(f32[2,16384]{1,0:T(2,128)S(1)} %get-tuple-element.60), channel_id=1, source_target_pairs={{0,3},{1,2},{2,1},{3,0},{4,7},{5,6},{6,5},{7,4},{8,11},{9,10},{10,... | collective-permute-start | bytes 393224 | tf_op jit(solution)/shard_map/ppermute | solution.py:418
  84.0 0.8 collective-permute-start.8
  84.9 1.1 %collective-permute-start.9 = (f32[2,16384]{1,0:T(2,128)S(1)}, f32[2,16384]{1,0:T(2,128)S(1)}, u32[]{:S(2)}, u32[]{:S(2)}) collective-permute-start(f32[2,16384]{1,0:T(2,128)S(1)} %get-tuple-element.59), channel_id=1, source_target_pairs={{0,1},{1,0},{2,3},{3,2},{4,5},{5,4},{6,7},{7,6},{8,9},{9,8},{10,11... | collective-permute-start | bytes 393224 | tf_op jit(solution)/shard_map/ppermute | solution.py:418
  86.0 0.0 collective-permute-done.7.other
  86.0 4.8 %shard_map.107 = f32[2,16384]{1,0:T(2,128)S(1)} custom-call(s32[2,124]{1,0:T(2,128)S(1)} %and_add_fusion.1.rows, f32[1024,128]{1,0:T(8,128)S(1)} %constant_dynamic-update-slice_fusion.2.own, f32[1024,128]{1,0:T(8,128)S(1)} %collective-permute-done.7.other, f32[2,64,64,124]{3,2,1,0:T(8,128)S(1)} %bitcast.3, f32[2,15,64,64]{3,2,1,0:T(8,128)S(1)} %copy-done.6, ...), custom_call_target="tpu_custom_call" | custom-call | flops 8000000000 | bytes 100000 | tf_op jit(solution)/shard_map/pallas_call | solution.py:502
  90.8 1.2 %collective-permute-done.8 = f32[2,16384]{1,0:T(2,128)S(1)} collective-permute-done((f32[2,16384]{1,0:T(2,128)S(1)}, f32[2,16384]{1,0:T(2,128)S(1)}, u32[]{:S(2)}, u32[]{:S(2)}) %collective-permute-start.8) | collective-permute-done | bytes 131104 | tf_op jit(solution)/shard_map/ppermute | solution.py:418
  92.0 0.8 add_add_fusion
  (43 shorter events, 0.3 us)
Async XLA Ops:
  0.0 14.7 %copy-start.11 = (s32[124]{0:T(128)S(1)}, s32[124]{0:T(128)}, u32[]{:S(2)}) copy-start(s32[124]{0:T(128)} %constant.35.clone) | copy-start | bytes 1492
  0.0 14.7 %copy-start.12 = (s32[124]{0:T(128)S(1)}, s32[124]{0:T(128)}, u32[]{:S(2)}) copy-start(s32[124]{0:T(128)} %constant.44) | copy-start | bytes 1492
  0.0 14.7 %copy-start.13 = (s32[124]{0:T(128)S(1)}, s32[124]{0:T(128)}, u32[]{:S(2)}) copy-start(s32[124]{0:T(128)} %constant.46) | copy-start | bytes 1492
  0.0 14.8 %collective-permute-start = (f32[2,16384]{1,0:T(2,128)}, f32[2,16384]{1,0:T(2,128)S(1)}, u32[]{:S(2)}, u32[]{:S(2)}) collective-permute-start(f32[2,16384]{1,0:T(2,128)} %refs_4_.1), channel_id=1, source_target_pairs={{0,1},{1,0},{2,3},{3,2},{4,5},{5,4},{6,7},{7,6},{8,9},{9,8},{10,11... | collective-permute-start | bytes 393224 | tf_op jit(solution)/shard_map/ppermute | solution.py:418
  1.7 0.9 %copy-start = (f32[2,16384]{1,0:T(2,128)S(1)}, f32[2,16384]{1,0:T(2,128)}, u32[]{:S(2)}) copy-start(f32[2,16384]{1,0:T(2,128)} %refs_4_.1) | copy-start | bytes 393220
  2.6 2.2 %copy-start.2 = (f32[16,64,1024]{2,1,0:T(8,128)S(1)}, f32[16,64,1024]{2,1,0:T(8,128)}, u32[]{:S(2)}) copy-start(f32[16,64,1024]{2,1,0:T(8,128)} %basis.3) | copy-start | bytes 12582916
  4.8 1.2 %copy-start.5 = (f32[2,15,64,64]{3,2,1,0:T(8,128)S(1)}, f32[2,15,64,64]{3,2,1,0:T(8,128)}, u32[]{:S(2)}) copy-start(f32[2,15,64,64]{3,2,1,0:T(8,128)} %transfer.3) | copy-start | bytes 1474564
  6.0 8.7 %copy-start.10 = (s32[2,124]{1,0:T(2,128)S(1)}, s32[2,124]{1,0:T(2,128)}, u32[]{:S(2)}) copy-start(s32[2,124]{1,0:T(2,128)} %param.15) | copy-start | bytes 2980
  6.0 8.8 %copy-start.1 = (f32[2,16384]{1,0:T(2,128)S(1)}, f32[2,16384]{1,0:T(2,128)}, u32[]{:S(2)}) copy-start(f32[2,16384]{1,0:T(2,128)} %refs_4_.1) | copy-start | bytes 393220
  6.0 11.9 %copy-start.7 = (f32[2,16384]{1,0:T(2,128)S(1)}, f32[2,16384]{1,0:T(2,128)}, u32[]{:S(2)}) copy-start(f32[2,16384]{1,0:T(2,128)} %refs_1_.11) | copy-start | bytes 393220
  6.0 11.9 %copy-start.8 = (s32[16,9]{1,0:T(8,128)S(1)}, s32[16,9]{1,0:T(8,128)}, u32[]{:S(2)}) copy-start(s32[16,9]{1,0:T(8,128)} %list_hbm.1) | copy-start | bytes 1732
  6.0 11.9 %copy-start.9 = (s32[16]{0:T(128)S(1)}, s32[16]{0:T(128)}, u32[]{:S(2)}) copy-start(s32[16]{0:T(128)} %count_hbm.1) | copy-start | bytes 196
  8.4 22.7 %collective-permute-start.2 = (f32[32,128]{1,0:T(8,128)S(1)}, f32[32,128]{1,0:T(8,128)S(1)}, u32[]{:S(2)}, u32[]{:S(2)}) collective-permute-start(f32[32,128]{1,0:T(8,128)S(1)} %shard_map.101.refs_8_), channel_id=1, source_target_pairs={{0,224},{4,228},{8,232},{12,236},{16,240},{20,244},{24,248},{28,25... | collective-permute-start | bytes 49160 | tf_op jit(solution)/shard_map/ppermute | solution.py:421
  15.0 9.1 %collective-permute-start.1 = (f32[4,16384]{1,0:T(4,128)S(1)}, f32[4,16384]{1,0:T(4,128)S(1)}, u32[]{:S(2)}, u32[]{:S(2)}) collective-permute-start(f32[4,16384]{1,0:T(4,128)S(1)} %pad_maximum_fusion._), channel_id=1, source_target_pairs={{0,2},{1,3},{2,0},{3,1},{4,6},{5,7},{6,4},{7,5},{8,10},{9,11},{10,... | collective-permute-start | bytes 786440 | tf_op jit(solution)/shard_map/ppermute | solution.py:418
  31.2 8.4 %collective-permute-start.3 = (f32[320,128]{1,0:T(8,128)S(1)}, f32[320,128]{1,0:T(8,128)S(1)}, u32[]{:S(2)}, u32[]{:S(2)}) collective-permute-start(f32[320,128]{1,0:T(8,128)S(1)} %pad_maximum_fusion.1), channel_id=1, source_target_pairs={{0,252},{4,0},{8,4},{12,8},{16,12},{20,16},{24,20},{28,24},{32,28}... | collective-permute-start | bytes 491528 | tf_op jit(solution)/shard_map/ppermute | solution.py:421
  39.7 9.6 %collective-permute-start.4 = (f32[256,128]{1,0:T(8,128)S(1)}, f32[256,128]{1,0:T(8,128)S(1)}, u32[]{:S(2)}, u32[]{:S(2)}) collective-permute-start(f32[256,128]{1,0:T(8,128)S(1)} %pad_maximum_fusion.2), channel_id=1, source_target_pairs={{0,8},{4,12},{8,16},{12,20},{16,24},{20,28},{24,32},{28,36},{32,40... | collective-permute-start | bytes 393224 | tf_op jit(solution)/shard_map/ppermute | solution.py:421
  49.4 8.5 %collective-permute-start.5 = (f32[256,128]{1,0:T(8,128)S(1)}, f32[256,128]{1,0:T(8,128)S(1)}, u32[]{:S(2)}, u32[]{:S(2)}) collective-permute-start(f32[256,128]{1,0:T(8,128)S(1)} %pad_maximum_fusion.3.refs_8_), channel_id=1, source_target_pairs={{0,240},{4,244},{8,248},{12,252},{16,0},{20,4},{24,8},{28,12},{32,... | collective-permute-start | bytes 393224 | tf_op jit(solution)/shard_map/ppermute | solution.py:421
  57.9 11.4 %collective-permute-start.6 = (f32[512,128]{1,0:T(8,128)S(1)}, f32[512,128]{1,0:T(8,128)S(1)}, u32[]{:S(2)}, u32[]{:S(2)}) collective-permute-start(f32[512,128]{1,0:T(8,128)S(1)} %constant_dynamic-update-slice_fusion.refs_10_), channel_id=1, source_target_pairs={{0,128},{4,132},{8,136},{12,140},{16,144},{20,148},{24,152},{28,15... | collective-permute-start | bytes 786440 | tf_op jit(solution)/shard_map/ppermute | solution.py:421
  69.3 16.6 %collective-permute-start.7 = (f32[1024,128]{1,0:T(8,128)S(1)}, f32[1024,128]{1,0:T(8,128)S(1)}, u32[]{:S(2)}, u32[]{:S(2)}) collective-permute-start(f32[1024,128]{1,0:T(8,128)S(1)} %constant_dynamic-update-slice_fusion.2.own), channel_id=1, source_target_pairs={{0,192},{4,196},{8,200},{12,204},{16,208},{20,212},{24,216},{28,22... | collective-permute-start | bytes 1572872 | tf_op jit(solution)/shard_map/ppermute | solution.py:421
  73.3 12.7 %copy-start.3 = (f32[16,64,1024]{2,1,0:T(8,128)S(1)}, f32[16,64,1024]{2,1,0:T(8,128)}, u32[]{:S(2)}) copy-start(f32[16,64,1024]{2,1,0:T(8,128)} %basis.3) | copy-start | bytes 12582916
  73.3 12.7 %copy-start.4 = (f32[2,124,64,64]{1,3,2,0:T(8,128)S(1)}, f32[2,124,64,64]{1,3,2,0:T(8,128)}, u32[]{:S(2)}) copy-start(f32[2,124,64,64]{1,3,2,0:T(8,128)} %param.14) | copy-start | bytes 12189700
  73.3 12.7 %copy-start.6 = (f32[2,15,64,64]{3,2,1,0:T(8,128)S(1)}, f32[2,15,64,64]{3,2,1,0:T(8,128)}, u32[]{:S(2)}) copy-start(f32[2,15,64,64]{3,2,1,0:T(8,128)} %transfer.3) | copy-start | bytes 1474564
  81.8 9.0 %collective-permute-start.10 = (f32[2,16384]{1,0:T(2,128)S(1)}, f32[2,16384]{1,0:T(2,128)S(1)}, u32[]{:S(2)}, u32[]{:S(2)}) collective-permute-start(f32[2,16384]{1,0:T(2,128)S(1)} %get-tuple-element.60), channel_id=1, source_target_pairs={{0,3},{1,2},{2,1},{3,0},{4,7},{5,6},{6,5},{7,4},{8,11},{9,10},{10,... | collective-permute-start | bytes 393224 | tf_op jit(solution)/shard_map/ppermute | solution.py:418
  84.0 7.9 %collective-permute-start.8 = (f32[2,16384]{1,0:T(2,128)S(1)}, f32[2,16384]{1,0:T(2,128)S(1)}, u32[]{:S(2)}, u32[]{:S(2)}) collective-permute-start(f32[2,16384]{1,0:T(2,128)S(1)} %get-tuple-element.58), channel_id=1, source_target_pairs={{0,2},{1,3},{2,0},{3,1},{4,6},{5,7},{6,4},{7,5},{8,10},{9,11},{10,... | collective-permute-start | bytes 393224 | tf_op jit(solution)/shard_map/ppermute | solution.py:418
  84.9 7.1 %collective-permute-start.9 = (f32[2,16384]{1,0:T(2,128)S(1)}, f32[2,16384]{1,0:T(2,128)S(1)}, u32[]{:S(2)}, u32[]{:S(2)}) collective-permute-start(f32[2,16384]{1,0:T(2,128)S(1)} %get-tuple-element.59), channel_id=1, source_target_pairs={{0,1},{1,0},{2,3},{3,2},{4,5},{5,4},{6,7},{7,6},{8,9},{9,8},{10,11... | collective-permute-start | bytes 393224 | tf_op jit(solution)/shard_map/ppermute | solution.py:418

commit v5 on v4

--- a/solution.py
+++ b/solution.py
@@ -31,7 +31,7 @@
 WINDOWS = 6
 SINGLE = 80
 EDGE = 128
-SHIFTS = (-8, -1, 2, -4, 32, -16)
+SHIFTS = (-16, -1, 2, -8, -4, 32)
 ANY = pl.BlockSpec(memory_space=pl.ANY)
 HBM = pl.BlockSpec(memory_space=pltpu.HBM)
 VMEM = pl.BlockSpec(memory_space=pltpu.VMEM)
@@ -494,8 +494,7 @@
     half = lax.shift_right_logical(place_on, 1)
     bit_2 = half & 1
     fourth = lax.shift_right_logical(half + bit_2, 1)
-    bit_3 = fourth & 1
-    bit_0, bit_5, bit_4 = (lax.shift_right_logical(fourth, n) & 1 for n in (1, 2, 3))
+    bit_4, bit_3, bit_0, bit_5 = (lax.shift_right_logical(fourth, n) & 1 for n in range(4))
     block = bit_0 + 2 * bit_1 + 4 * bit_2 + 8 * bit_3 + 16 * bit_4 + 32 * bit_5
     rows = block * 32 + start + inside
     back = [swap_rhs(whole[k], k) for k in (2, 1, 3)]

time: 93.4 us -> 96.8 us (1.036)
  the two profiles are of different devices: /device:TPU:34 before, /device:TPU:32 now
where the time goes in v5:
time: 96.8 us; the launch traced here: 97.1 us
  Pallas kernels  64.8 us (67%)
  starting transfers between devices  20.7 us (21%)
  waiting for transfers between devices  5.88 us (6%)
  local copies, waits for them, and re-layouts  4.53 us (5%)
  other arithmetic  1.09 us (1%)
    pallas_call x6, Pallas kernels, shards(): call(functools.partial(near_kernel, w, len(carried)), [*outs, *extra, *(v...  52.6 us
    ppermute x6, starting transfers between devices, shift_leaf(): return lax.ppermute(v, 'leaf', [(d, (d + s) % count) for d in range(count)])  11.8 us
    ppermute x5, starting transfers between devices, swap_rhs(): return lax.ppermute(v, 'rhs', [(i, i ^ k) for i in range(RHS)])  8.83 us
    pallas_call x1, Pallas kernels, shards(): call(prep_kernel, [jax.ShapeDtypeStruct((8, 128), jnp.int32), bf16(LEAVES...  5.04 us
    pallas_call x1, Pallas kernels, shards(): call(down_kernel, [(2, LEAVES * PTS)], [SMEM] + [VMEM] * 5, [pltpu.VMEM((...  4.77 us
    unnamed x30, local copies, waits for them, and re-layouts  4.42 us
    ppermute x6, waiting for transfers between devices, shift_leaf(): return lax.ppermute(v, 'leaf', [(d, (d + s) % count) for d in range(count)])  3.63 us
    pallas_call x1, Pallas kernels, shards(): call(up_kernel, [(32, 2 * RANK)], [VMEM] * 3, micros=4)  2.4 us
  transfers between devices with their start and end apart: 11, of which 4 were waited for; matrix products, arithmetic and copies ran while one was open for 0% of the time, Pallas kernels for 67%

profile of v5, /device:TPU:32, one launch (start us, length us, event | category | flops | bytes accessed | tf_op | source)
XLA Modules:
  0.0 97.1 jit_solution(5393082222273750684)
XLA Ops:
  0.0 1.7 %collective-permute-start = (f32[2,16384]{1,0:T(2,128)}, f32[2,16384]{1,0:T(2,128)S(1)}, u32[]{:S(2)}, u32[]{:S(2)}) collective-permute-start(f32[2,16384]{1,0:T(2,128)} %refs_4_.1), channel_id=1, source_target_pairs={{0,1},{1,0},{2,3},{3,2},{4,5},{5,4},{6,7},{7,6},{8,9},{9,8},{10,11... | collective-permute-start | bytes 393224 | tf_op jit(solution)/shard_map/ppermute | solution.py:418
  1.7 0.9 copy-done
  2.6 2.2 %copy-done.2 = f32[16,64,1024]{2,1,0:T(8,128)S(1)} copy-done((f32[16,64,1024]{2,1,0:T(8,128)S(1)}, f32[16,64,1024]{2,1,0:T(8,128)}, u32[]{:S(2)}) %copy-start.2) | copy-done | bytes 4194328
  4.8 1.2 %copy-done.5 = f32[2,15,64,64]{3,2,1,0:T(8,128)S(1)} copy-done((f32[2,15,64,64]{3,2,1,0:T(8,128)S(1)}, f32[2,15,64,64]{3,2,1,0:T(8,128)}, u32[]{:S(2)}) %copy-start.5) | copy-done | bytes 491544
  6.0 2.4 %shard_map.101.refs_8_ = f32[32,128]{1,0:T(8,128)S(1)} custom-call(f32[2,16384]{1,0:T(2,128)S(1)} %copy-done, f32[16,64,1024]{2,1,0:T(8,128)S(1)} %copy-done.2, f32[2,15,64,64]{3,2,1,0:T(8,128)S(1)} %copy-done.5), custom_call_target="tpu_custom_call" | custom-call | flops 4000000000 | bytes 100000 | tf_op jit(solution)/shard_map/pallas_call | solution.py:443
  8.4 2.8 %collective-permute-start.2 = (f32[32,128]{1,0:T(8,128)S(1)}, f32[32,128]{1,0:T(8,128)S(1)}, u32[]{:S(2)}, u32[]{:S(2)}) collective-permute-start(f32[32,128]{1,0:T(8,128)S(1)} %shard_map.101.refs_8_), channel_id=1, source_target_pairs={{0,192},{4,196},{8,200},{12,204},{16,208},{20,212},{24,216},{28,22... | collective-permute-start | bytes 49160 | tf_op jit(solution)/shard_map/ppermute | solution.py:421
  11.2 0.1 pad_add_fusion.meta
  11.3 0.0 collective-permute-done.refs_5_
  11.3 0.1 pad_maximum_fusion._
  11.4 3.0 %collective-permute-start.1 = (f32[4,16384]{1,0:T(4,128)S(1)}, f32[4,16384]{1,0:T(4,128)S(1)}, u32[]{:S(2)}, u32[]{:S(2)}) collective-permute-start(f32[4,16384]{1,0:T(4,128)S(1)} %pad_maximum_fusion._), channel_id=1, source_target_pairs={{0,2},{1,3},{2,0},{3,1},{4,6},{5,7},{6,4},{7,5},{8,10},{9,11},{10,... | collective-permute-start | bytes 786440 | tf_op jit(solution)/shard_map/ppermute | solution.py:418
  14.4 5.0 %shard_map.100 = (s32[8,128]{1,0:T(8,128)S(1)}, bf16[16,256,32]{2,1,0:T(8,128)(2,1)S(1)}, bf16[16,16,1024]{2,1,0:T(8,128)(2,1)S(1)}, f32[2,4096]{1,0:T(2,128)S(1)}) custom-call(s32[2]{0:T(128)S(1)} %pad_add_fusion.meta, s32[16,9]{1,0:T(8,128)S(1)} %copy-done.8, s32[16]{0:T(128)S(1)} %copy-done.9, f32[2,16384]{1,0:T(2,128)S(1)} %copy-done.7, ...), custom_call_target="tpu_custom_call" | custom-call | flops 4000000000 | bytes 100000 | tf_op jit(solution)/shard_map/pallas_call | solution.py:425
  19.5 1.0 %collective-permute-done.1.refs_6_ = f32[4,16384]{1,0:T(4,128)S(1)} collective-permute-done((f32[4,16384]{1,0:T(4,128)S(1)}, f32[4,16384]{1,0:T(4,128)S(1)}, u32[]{:S(2)}, u32[]{:S(2)}) %collective-permute-start.1) | collective-permute-done | bytes 262176 | tf_op jit(solution)/shard_map/ppermute | solution.py:418
  20.5 8.5 %shard_map.102 = (f32[17,16,1024]{2,1,0:T(8,128)S(1)}, f32[17,16,256]{2,1,0:T(8,128)S(1)}, bf16[16,16,256]{2,1,0:T(8,128)(2,1)S(1)}, bf16[16,16,1024]{2,1,0:T(8,...) custom-call(s32[8,128]{1,0:T(8,128)S(1)} %get-tuple-element.33.refs_0_, f32[2,16384]{1,0:T(2,128)S(1)} %copy-done.7, ...), custom_call_target="tpu_custom_call" | custom-call | flops 8999999488 | bytes 100000 | tf_op jit(solution)/shard_map/pallas_call | solution.py:470
  29.1 0.1 collective-permute-start.3
  29.2 8.3 %shard_map.103 = (f32[17,16,1024]{2,1,0:T(8,128)S(1)}, f32[17,16,256]{2,1,0:T(8,128)S(1)}, f32[64,128]{1,0:T(8,128)S(1)}) custom-call(s32[8,128]{1,0:T(8,128)S(1)} %get-tuple-element.33.refs_0_, f32[2,16384]{1,0:T(2,128)S(1)} %copy-done.7, bf16[16,16,1024]{2,1,0:T(8,128)(2,1)S(1)} %get-tuple-element.34.refs_2_, ...), custom_call_target="tpu_custom_call" | custom-call | flops 8999999488 | bytes 100000 | tf_op jit(solution)/shard_map/pallas_call | solution.py:470
  37.6 0.0 collective-permute-done.3
  37.7 0.3 collective-permute-start.4
  37.9 8.3 %shard_map.104 = (f32[17,16,1024]{2,1,0:T(8,128)S(1)}, f32[17,16,256]{2,1,0:T(8,128)S(1)}, f32[128,128]{1,0:T(8,128)S(1)}) custom-call(s32[8,128]{1,0:T(8,128)S(1)} %get-tuple-element.33.refs_0_, f32[2,16384]{1,0:T(2,128)S(1)} %copy-done.7, bf16[16,16,1024]{2,1,0:T(8,128)(2,1)S(1)} %get-tuple-element.34.refs_2_, ...), custom_call_target="tpu_custom_call" | custom-call | flops 8999999488 | bytes 100000 | tf_op jit(solution)/shard_map/pallas_call | solution.py:470
  46.3 0.1 collective-permute-start.5
  46.4 8.2 %shard_map.105 = (f32[17,16,1024]{2,1,0:T(8,128)S(1)}, f32[17,16,256]{2,1,0:T(8,128)S(1)}, f32[256,128]{1,0:T(8,128)S(1)}) custom-call(s32[8,128]{1,0:T(8,128)S(1)} %get-tuple-element.33.refs_0_, f32[2,16384]{1,0:T(2,128)S(1)} %copy-done.7, bf16[16,16,1024]{2,1,0:T(8,128)(2,1)S(1)} %get-tuple-element.34.refs_2_, ...), custom_call_target="tpu_custom_call" | custom-call | flops 8999999488 | bytes 100000 | tf_op jit(solution)/shard_map/pallas_call | solution.py:470
  54.7 3.0 %collective-permute-done.5 = f32[256,128]{1,0:T(8,128)S(1)} collective-permute-done((f32[256,128]{1,0:T(8,128)S(1)}, f32[256,128]{1,0:T(8,128)S(1)}, u32[]{:S(2)}, u32[]{:S(2)}) %collective-permute-start.5) | collective-permute-done | bytes 131104 | tf_op jit(solution)/shard_map/ppermute | solution.py:421
  57.7 7.5 %collective-permute-start.6 = (f32[512,128]{1,0:T(8,128)S(1)}, f32[512,128]{1,0:T(8,128)S(1)}, u32[]{:S(2)}, u32[]{:S(2)}) collective-permute-start(f32[512,128]{1,0:T(8,128)S(1)} %constant_dynamic-update-slice_fusion.refs_10_), channel_id=1, source_target_pairs={{0,240},{4,244},{8,248},{12,252},{16,0},{20,4},{24,8},{28,12},{32,... | collective-permute-start | bytes 786440 | tf_op jit(solution)/shard_map/ppermute | solution.py:421
  65.2 9.7 %shard_map.106 = (f32[17,16,1024]{2,1,0:T(8,128)S(1)}, f32[17,16,256]{2,1,0:T(8,128)S(1)}, bf16[24,256,32]{2,1,0:T(8,128)(2,1)S(1)}, bf16[24,16,256]{2,1,0:T(8,128)(2,1)S(1)}, f32[512,128]{1,0:T(8,128)S(1)}) custom-call(s32[8,128]{1,0:T(8,128)S(1)} %get-tuple-element.33.refs_0_, f32[2,16384]{1,0:T(2,128)S(1)} %copy-done.7, ...), custom_call_target="tpu_custom_call" | custom-call | flops 8999999488 | bytes 100000 | tf_op jit(solution)/shard_map/pallas_call | solution.py:470
  74.9 0.6 collective-permute-done.6
  75.5 1.1 %collective-permute-start.7 = (f32[1024,128]{1,0:T(8,128)S(1)}, f32[1024,128]{1,0:T(8,128)S(1)}, u32[]{:S(2)}, u32[]{:S(2)}) collective-permute-start(f32[1024,128]{1,0:T(8,128)S(1)} %constant_dynamic-update-slice_fusion.2.own), channel_id=1, source_target_pairs={{0,128},{4,132},{8,136},{12,140},{16,144},{20,148},{24,152},{28,15... | collective-permute-start | bytes 1572872 | tf_op jit(solution)/shard_map/ppermute | solution.py:421
  76.7 9.5 %shard_map.108 = (f32[2,16384]{1,0:T(2,128)S(1)}, f32[2,16384]{1,0:T(2,128)S(1)}, f32[2,16384]{1,0:T(2,128)S(1)}, f32[2,16384]{1,0:T(2,128)S(1)}) custom-call(s32[8,128]{1,0:T(8,128)S(1)} %get-tuple-element.33.refs_0_, f32[2,16384]{1,0:T(2,128)S(1)} %copy-done.7, bf16[16,16,1024]{2,1,0:T(8,128)(2,1)S(1)} %get-tuple-element.34.refs_2_, ...), custom_call_target="tpu_custom_call" | custom-call | flops 8999999488 | bytes 100000 | tf_op jit(solution)/shard_map/pallas_call | solution.py:470
  86.1 2.3 %collective-permute-start.10 = (f32[2,16384]{1,0:T(2,128)S(1)}, f32[2,16384]{1,0:T(2,128)S(1)}, u32[]{:S(2)}, u32[]{:S(2)}) collective-permute-start(f32[2,16384]{1,0:T(2,128)S(1)} %get-tuple-element.60), channel_id=1, source_target_pairs={{0,3},{1,2},{2,1},{3,0},{4,7},{5,6},{6,5},{7,4},{8,11},{9,10},{10,... | collective-permute-start | bytes 393224 | tf_op jit(solution)/shard_map/ppermute | solution.py:418
  88.4 0.8 collective-permute-start.8
  89.2 1.1 %collective-permute-start.9 = (f32[2,16384]{1,0:T(2,128)S(1)}, f32[2,16384]{1,0:T(2,128)S(1)}, u32[]{:S(2)}, u32[]{:S(2)}) collective-permute-start(f32[2,16384]{1,0:T(2,128)S(1)} %get-tuple-element.59), channel_id=1, source_target_pairs={{0,1},{1,0},{2,3},{3,2},{4,5},{5,4},{6,7},{7,6},{8,9},{9,8},{10,11... | collective-permute-start | bytes 393224 | tf_op jit(solution)/shard_map/ppermute | solution.py:418
  90.3 4.8 %shard_map.107 = f32[2,16384]{1,0:T(2,128)S(1)} custom-call(s32[2,124]{1,0:T(2,128)S(1)} %and_add_fusion.1.rows, f32[1024,128]{1,0:T(8,128)S(1)} %constant_dynamic-update-slice_fusion.2.own, f32[1024,128]{1,0:T(8,128)S(1)} %collective-permute-done.7.other, f32[2,64,64,124]{3,2,1,0:T(8,128)S(1)} %bitcast.3, f32[2,15,64,64]{3,2,1,0:T(8,128)S(1)} %copy-done.6, ...), custom_call_target="tpu_custom_call" | custom-call | flops 8000000000 | bytes 100000 | tf_op jit(solution)/shard_map/pallas_call | solution.py:501
  95.1 1.2 %collective-permute-done.8 = f32[2,16384]{1,0:T(2,128)S(1)} collective-permute-done((f32[2,16384]{1,0:T(2,128)S(1)}, f32[2,16384]{1,0:T(2,128)S(1)}, u32[]{:S(2)}, u32[]{:S(2)}) %collective-permute-start.8) | collective-permute-done | bytes 131104 | tf_op jit(solution)/shard_map/ppermute | solution.py:418
  96.3 0.8 add_add_fusion
  (43 shorter events, 0.3 us)
Async XLA Ops:
  0.0 11.2 %copy-start.11 = (s32[124]{0:T(128)S(1)}, s32[124]{0:T(128)}, u32[]{:S(2)}) copy-start(s32[124]{0:T(128)} %constant.37.clone) | copy-start | bytes 1492
  0.0 11.2 %copy-start.12 = (s32[124]{0:T(128)S(1)}, s32[124]{0:T(128)}, u32[]{:S(2)}) copy-start(s32[124]{0:T(128)} %constant.46) | copy-start | bytes 1492
  0.0 11.2 %copy-start.13 = (s32[124]{0:T(128)S(1)}, s32[124]{0:T(128)}, u32[]{:S(2)}) copy-start(s32[124]{0:T(128)} %constant.48) | copy-start | bytes 1492
  0.0 11.3 %collective-permute-start = (f32[2,16384]{1,0:T(2,128)}, f32[2,16384]{1,0:T(2,128)S(1)}, u32[]{:S(2)}, u32[]{:S(2)}) collective-permute-start(f32[2,16384]{1,0:T(2,128)} %refs_4_.1), channel_id=1, source_target_pairs={{0,1},{1,0},{2,3},{3,2},{4,5},{5,4},{6,7},{7,6},{8,9},{9,8},{10,11... | collective-permute-start | bytes 393224 | tf_op jit(solution)/shard_map/ppermute | solution.py:418
  1.7 0.9 copy-start
  2.6 2.2 %copy-start.2 = (f32[16,64,1024]{2,1,0:T(8,128)S(1)}, f32[16,64,1024]{2,1,0:T(8,128)}, u32[]{:S(2)}) copy-start(f32[16,64,1024]{2,1,0:T(8,128)} %basis.3) | copy-start | bytes 12582916
  4.8 1.2 %copy-start.5 = (f32[2,15,64,64]{3,2,1,0:T(8,128)S(1)}, f32[2,15,64,64]{3,2,1,0:T(8,128)}, u32[]{:S(2)}) copy-start(f32[2,15,64,64]{3,2,1,0:T(8,128)} %transfer.3) | copy-start | bytes 1474564
  6.0 5.2 %copy-start.10 = (s32[2,124]{1,0:T(2,128)S(1)}, s32[2,124]{1,0:T(2,128)}, u32[]{:S(2)}) copy-start(s32[2,124]{1,0:T(2,128)} %param.15) | copy-start | bytes 2980
  6.0 5.3 %copy-start.1 = (f32[2,16384]{1,0:T(2,128)S(1)}, f32[2,16384]{1,0:T(2,128)}, u32[]{:S(2)}) copy-start(f32[2,16384]{1,0:T(2,128)} %refs_4_.1) | copy-start | bytes 393220
  6.0 8.4 %copy-start.7 = (f32[2,16384]{1,0:T(2,128)S(1)}, f32[2,16384]{1,0:T(2,128)}, u32[]{:S(2)}) copy-start(f32[2,16384]{1,0:T(2,128)} %refs_1_.11) | copy-start | bytes 393220
  6.0 8.4 %copy-start.8 = (s32[16,9]{1,0:T(8,128)S(1)}, s32[16,9]{1,0:T(8,128)}, u32[]{:S(2)}) copy-start(s32[16,9]{1,0:T(8,128)} %list_hbm.1) | copy-start | bytes 1732
  6.0 8.4 %copy-start.9 = (s32[16]{0:T(128)S(1)}, s32[16]{0:T(128)}, u32[]{:S(2)}) copy-start(s32[16]{0:T(128)} %count_hbm.1) | copy-start | bytes 196
  8.4 20.6 %collective-permute-start.2 = (f32[32,128]{1,0:T(8,128)S(1)}, f32[32,128]{1,0:T(8,128)S(1)}, u32[]{:S(2)}, u32[]{:S(2)}) collective-permute-start(f32[32,128]{1,0:T(8,128)S(1)} %shard_map.101.refs_8_), channel_id=1, source_target_pairs={{0,192},{4,196},{8,200},{12,204},{16,208},{20,212},{24,216},{28,22... | collective-permute-start | bytes 49160 | tf_op jit(solution)/shard_map/ppermute | solution.py:421
  11.4 9.1 %collective-permute-start.1 = (f32[4,16384]{1,0:T(4,128)S(1)}, f32[4,16384]{1,0:T(4,128)S(1)}, u32[]{:S(2)}, u32[]{:S(2)}) collective-permute-start(f32[4,16384]{1,0:T(4,128)S(1)} %pad_maximum_fusion._), channel_id=1, source_target_pairs={{0,2},{1,3},{2,0},{3,1},{4,6},{5,7},{6,4},{7,5},{8,10},{9,11},{10,... | collective-permute-start | bytes 786440 | tf_op jit(solution)/shard_map/ppermute | solution.py:418
  29.1 8.4 %collective-permute-start.3 = (f32[320,128]{1,0:T(8,128)S(1)}, f32[320,128]{1,0:T(8,128)S(1)}, u32[]{:S(2)}, u32[]{:S(2)}) collective-permute-start(f32[320,128]{1,0:T(8,128)S(1)} %pad_maximum_fusion.1), channel_id=1, source_target_pairs={{0,252},{4,0},{8,4},{12,8},{16,12},{20,16},{24,20},{28,24},{32,28}... | collective-permute-start | bytes 491528 | tf_op jit(solution)/shard_map/ppermute | solution.py:421
  37.7 8.6 %collective-permute-start.4 = (f32[256,128]{1,0:T(8,128)S(1)}, f32[256,128]{1,0:T(8,128)S(1)}, u32[]{:S(2)}, u32[]{:S(2)}) collective-permute-start(f32[256,128]{1,0:T(8,128)S(1)} %pad_maximum_fusion.2), channel_id=1, source_target_pairs={{0,8},{4,12},{8,16},{12,20},{16,24},{20,28},{24,32},{28,36},{32,40... | collective-permute-start | bytes 393224 | tf_op jit(solution)/shard_map/ppermute | solution.py:421
  46.3 11.4 %collective-permute-start.5 = (f32[256,128]{1,0:T(8,128)S(1)}, f32[256,128]{1,0:T(8,128)S(1)}, u32[]{:S(2)}, u32[]{:S(2)}) collective-permute-start(f32[256,128]{1,0:T(8,128)S(1)} %pad_maximum_fusion.3.refs_8_), channel_id=1, source_target_pairs={{0,224},{4,228},{8,232},{12,236},{16,240},{20,244},{24,248},{28,25... | collective-permute-start | bytes 393224 | tf_op jit(solution)/shard_map/ppermute | solution.py:421
  57.7 17.8 %collective-permute-start.6 = (f32[512,128]{1,0:T(8,128)S(1)}, f32[512,128]{1,0:T(8,128)S(1)}, u32[]{:S(2)}, u32[]{:S(2)}) collective-permute-start(f32[512,128]{1,0:T(8,128)S(1)} %constant_dynamic-update-slice_fusion.refs_10_), channel_id=1, source_target_pairs={{0,240},{4,244},{8,248},{12,252},{16,0},{20,4},{24,8},{28,12},{32,... | collective-permute-start | bytes 786440 | tf_op jit(solution)/shard_map/ppermute | solution.py:421
  75.5 14.8 %collective-permute-start.7 = (f32[1024,128]{1,0:T(8,128)S(1)}, f32[1024,128]{1,0:T(8,128)S(1)}, u32[]{:S(2)}, u32[]{:S(2)}) collective-permute-start(f32[1024,128]{1,0:T(8,128)S(1)} %constant_dynamic-update-slice_fusion.2.own), channel_id=1, source_target_pairs={{0,128},{4,132},{8,136},{12,140},{16,144},{20,148},{24,152},{28,15... | collective-permute-start | bytes 1572872 | tf_op jit(solution)/shard_map/ppermute | solution.py:421
  76.6 13.7 %copy-start.3 = (f32[16,64,1024]{2,1,0:T(8,128)S(1)}, f32[16,64,1024]{2,1,0:T(8,128)}, u32[]{:S(2)}) copy-start(f32[16,64,1024]{2,1,0:T(8,128)} %basis.3) | copy-start | bytes 12582916
  76.6 13.7 %copy-start.4 = (f32[2,124,64,64]{1,3,2,0:T(8,128)S(1)}, f32[2,124,64,64]{1,3,2,0:T(8,128)}, u32[]{:S(2)}) copy-start(f32[2,124,64,64]{1,3,2,0:T(8,128)} %param.14) | copy-start | bytes 12189700
  76.6 13.7 %copy-start.6 = (f32[2,15,64,64]{3,2,1,0:T(8,128)S(1)}, f32[2,15,64,64]{3,2,1,0:T(8,128)}, u32[]{:S(2)}) copy-start(f32[2,15,64,64]{3,2,1,0:T(8,128)} %transfer.3) | copy-start | bytes 1474564
  86.1 9.0 %collective-permute-start.10 = (f32[2,16384]{1,0:T(2,128)S(1)}, f32[2,16384]{1,0:T(2,128)S(1)}, u32[]{:S(2)}, u32[]{:S(2)}) collective-permute-start(f32[2,16384]{1,0:T(2,128)S(1)} %get-tuple-element.60), channel_id=1, source_target_pairs={{0,3},{1,2},{2,1},{3,0},{4,7},{5,6},{6,5},{7,4},{8,11},{9,10},{10,... | collective-permute-start | bytes 393224 | tf_op jit(solution)/shard_map/ppermute | solution.py:418
  88.4 7.9 %collective-permute-start.8 = (f32[2,16384]{1,0:T(2,128)S(1)}, f32[2,16384]{1,0:T(2,128)S(1)}, u32[]{:S(2)}, u32[]{:S(2)}) collective-permute-start(f32[2,16384]{1,0:T(2,128)S(1)} %get-tuple-element.58), channel_id=1, source_target_pairs={{0,2},{1,3},{2,0},{3,1},{4,6},{5,7},{6,4},{7,5},{8,10},{9,11},{10,... | collective-permute-start | bytes 393224 | tf_op jit(solution)/shard_map/ppermute | solution.py:418
  89.2 7.1 %collective-permute-start.9 = (f32[2,16384]{1,0:T(2,128)S(1)}, f32[2,16384]{1,0:T(2,128)S(1)}, u32[]{:S(2)}, u32[]{:S(2)}) collective-permute-start(f32[2,16384]{1,0:T(2,128)S(1)} %get-tuple-element.59), channel_id=1, source_target_pairs={{0,1},{1,0},{2,3},{3,2},{4,5},{5,4},{6,7},{7,6},{8,9},{9,8},{10,11... | collective-permute-start | bytes 393224 | tf_op jit(solution)/shard_map/ppermute | solution.py:418

commit v6 on v5

--- a/solution.py
+++ b/solution.py
@@ -31,7 +31,8 @@
 WINDOWS = 6
 SINGLE = 80
 EDGE = 128
-SHIFTS = (-16, -1, 2, -8, -4, 32)
+SWAP = 8
+SHIFTS = (0, -1, 2, -4, 32, -16)
 ANY = pl.BlockSpec(memory_space=pl.ANY)
 HBM = pl.BlockSpec(memory_space=pltpu.HBM)
 VMEM = pl.BlockSpec(memory_space=pltpu.VMEM)
@@ -418,7 +419,8 @@
         return lax.ppermute(v, "rhs", [(i, i ^ k) for i in range(RHS)])
 
     def shift_leaf(v, s):
-        return lax.ppermute(v, "leaf", [(d, (d + s) % count) for d in range(count)])
+        pairs = [(d, (d + s) % count if s else d ^ SWAP) for d in range(count)]
+        return lax.ppermute(v, "leaf", pairs)
 
     first = swap_rhs(charges, 1)
     onward = jnp.concatenate([charges, first], 0)
@@ -489,12 +491,13 @@
     owner = lax.shift_right_logical(far_pairs, 4 - level)
     inside = far_pairs & (lax.shift_left(jnp.int32(1), 4 - level) - 1)
     start = jnp.asarray([LEVEL_ROW[k] for k in range(5) for _ in range(64 >> k)], jnp.int32)[None, :]
-    place_on = (owner - device) & (count - 1)
+    bit_0 = lax.shift_right_logical(owner - device + 2, 3) & 1
+    place_on = ((owner ^ (SWAP * bit_0)) - device) & (count - 1)
     bit_1 = place_on & 1
     half = lax.shift_right_logical(place_on, 1)
     bit_2 = half & 1
     fourth = lax.shift_right_logical(half + bit_2, 1)
-    bit_4, bit_3, bit_0, bit_5 = (lax.shift_right_logical(fourth, n) & 1 for n in range(4))
+    bit_3, bit_5, bit_4 = (lax.shift_right_logical(fourth, n) & 1 for n in (0, 2, 3))
     block = bit_0 + 2 * bit_1 + 4 * bit_2 + 8 * bit_3 + 16 * bit_4 + 32 * bit_5
     rows = block * 32 + start + inside
     back = [swap_rhs(whole[k], k) for k in (2, 1, 3)]

time: 96.8 us -> 93.5 us (0.966)
  Pallas kernels: 64.8 us -> 48.8 us
  starting transfers between devices: 20.7 us -> 35.2 us
  waiting for transfers between devices: 5.88 us -> 3.42 us
    pallas_call x6, Pallas kernels: 52.6 us -> 37.5 us  [shards(): call(functools.partial(near_kernel, w, len(carried)), [*outs, *extra, *(v...]
    ppermute x6, starting transfers between devices: 11.8 us -> 26.4 us  [shift_leaf(): return lax.ppermute(v, 'leaf', pairs)]
    ppermute x6, waiting for transfers between devices: 3.63 us -> 0.02 us  [shift_leaf(): return lax.ppermute(v, 'leaf', pairs)]
    ppermute x5, waiting for transfers between devices: 2.25 us -> 3.41 us  [swap_rhs(): return lax.ppermute(v, 'rhs', [(i, i ^ k) for i in range(RHS)])]
  transfers between devices with their start and end apart: 11 -> 11, of which waited for: 4 -> 4; matrix products, arithmetic and copies ran while one was open for 0% -> 0% of each run, Pallas kernels for 67% -> 52%
where the time goes in v6:
time: 93.5 us; the launch traced here: 93.3 us
  Pallas kernels  48.8 us (52%)
  starting transfers between devices  35.2 us (38%)
  local copies, waits for them, and re-layouts  4.53 us (5%)
  waiting for transfers between devices  3.42 us (4%)
  other arithmetic  1.1 us (1%)
    pallas_call x6, Pallas kernels, shards(): call(functools.partial(near_kernel, w, len(carried)), [*outs, *extra, *(v...  37.5 us
    ppermute x6, starting transfers between devices, shift_leaf(): return lax.ppermute(v, 'leaf', pairs)  26.4 us
    ppermute x5, starting transfers between devices, swap_rhs(): return lax.ppermute(v, 'rhs', [(i, i ^ k) for i in range(RHS)])  8.85 us
    pallas_call x1, Pallas kernels, shards(): call(down_kernel, [(2, LEAVES * PTS)], [SMEM] + [VMEM] * 5, [pltpu.VMEM((...  4.77 us
    unnamed x30, local copies, waits for them, and re-layouts  4.42 us
    pallas_call x1, Pallas kernels, shards(): call(prep_kernel, [jax.ShapeDtypeStruct((8, 128), jnp.int32), bf16(LEAVES...  4.18 us
    ppermute x5, waiting for transfers between devices, swap_rhs(): return lax.ppermute(v, 'rhs', [(i, i ^ k) for i in range(RHS)])  3.41 us
    pallas_call x1, Pallas kernels, shards(): call(up_kernel, [(32, 2 * RANK)], [VMEM] * 3, micros=4)  2.4 us
  transfers between devices with their start and end apart: 11, of which 4 were waited for; matrix products, arithmetic and copies ran while one was open for 0% of the time, Pallas kernels for 52%

profile of v6, /device:TPU:32, one launch (start us, length us, event | category | flops | bytes accessed | tf_op | source)
XLA Modules:
  0.0 93.3 jit_solution(4856747536029303635)
XLA Ops:
  0.0 1.7 %collective-permute-start = (f32[2,16384]{1,0:T(2,128)}, f32[2,16384]{1,0:T(2,128)S(1)}, u32[]{:S(2)}, u32[]{:S(2)}) collective-permute-start(f32[2,16384]{1,0:T(2,128)} %refs_4_.1), channel_id=1, source_target_pairs={{0,1},{1,0},{2,3},{3,2},{4,5},{5,4},{6,7},{7,6},{8,9},{9,8},{10,11... | collective-permute-start | bytes 393224 | tf_op jit(solution)/shard_map/ppermute | solution.py:419
  1.7 0.9 %copy-done = f32[2,16384]{1,0:T(2,128)S(1)} copy-done((f32[2,16384]{1,0:T(2,128)S(1)}, f32[2,16384]{1,0:T(2,128)}, u32[]{:S(2)}) %copy-start) | copy-done | bytes 131096
  2.6 2.2 %copy-done.2 = f32[16,64,1024]{2,1,0:T(8,128)S(1)} copy-done((f32[16,64,1024]{2,1,0:T(8,128)S(1)}, f32[16,64,1024]{2,1,0:T(8,128)}, u32[]{:S(2)}) %copy-start.2) | copy-done | bytes 4194328
  4.8 1.2 %copy-done.5 = f32[2,15,64,64]{3,2,1,0:T(8,128)S(1)} copy-done((f32[2,15,64,64]{3,2,1,0:T(8,128)S(1)}, f32[2,15,64,64]{3,2,1,0:T(8,128)}, u32[]{:S(2)}) %copy-start.5) | copy-done | bytes 491544
  6.0 2.4 %shard_map.101.refs_8_ = f32[32,128]{1,0:T(8,128)S(1)} custom-call(f32[2,16384]{1,0:T(2,128)S(1)} %copy-done, f32[16,64,1024]{2,1,0:T(8,128)S(1)} %copy-done.2, f32[2,15,64,64]{3,2,1,0:T(8,128)S(1)} %copy-done.5), custom_call_target="tpu_custom_call" | custom-call | flops 4000000000 | bytes 100000 | tf_op jit(solution)/shard_map/pallas_call | solution.py:445
  8.4 6.3 %collective-permute-start.2 = (f32[32,128]{1,0:T(8,128)S(1)}, f32[32,128]{1,0:T(8,128)S(1)}, u32[]{:S(2)}, u32[]{:S(2)}) collective-permute-start(f32[32,128]{1,0:T(8,128)S(1)} %shard_map.101.refs_8_), channel_id=1, source_target_pairs={{0,32},{4,36},{8,40},{12,44},{16,48},{20,52},{24,56},{28,60},{32,0... | collective-permute-start | bytes 49160 | tf_op jit(solution)/shard_map/ppermute | solution.py:423
  14.8 0.1 pad_add_fusion.meta
  14.9 0.0 collective-permute-done.refs_5_
  14.9 0.1 pad_maximum_fusion._
  15.0 3.0 %collective-permute-start.1 = (f32[4,16384]{1,0:T(4,128)S(1)}, f32[4,16384]{1,0:T(4,128)S(1)}, u32[]{:S(2)}, u32[]{:S(2)}) collective-permute-start(f32[4,16384]{1,0:T(4,128)S(1)} %pad_maximum_fusion._), channel_id=1, source_target_pairs={{0,2},{1,3},{2,0},{3,1},{4,6},{5,7},{6,4},{7,5},{8,10},{9,11},{10,... | collective-permute-start | bytes 786440 | tf_op jit(solution)/shard_map/ppermute | solution.py:419
  18.0 4.2 %shard_map.100 = (s32[8,128]{1,0:T(8,128)S(1)}, bf16[16,256,32]{2,1,0:T(8,128)(2,1)S(1)}, bf16[16,16,1024]{2,1,0:T(8,128)(2,1)S(1)}, f32[2,4096]{1,0:T(2,128)S(1)}) custom-call(s32[2]{0:T(128)S(1)} %pad_add_fusion.meta, s32[16,9]{1,0:T(8,128)S(1)} %copy-done.8, s32[16]{0:T(128)S(1)} %copy-done.9, f32[2,16384]{1,0:T(2,128)S(1)} %copy-done.7, ...), custom_call_target="tpu_custom_call" | custom-call | flops 4000000000 | bytes 100000 | tf_op jit(solution)/shard_map/pallas_call | solution.py:427
  22.2 1.9 %collective-permute-done.1.refs_6_ = f32[4,16384]{1,0:T(4,128)S(1)} collective-permute-done((f32[4,16384]{1,0:T(4,128)S(1)}, f32[4,16384]{1,0:T(4,128)S(1)}, u32[]{:S(2)}, u32[]{:S(2)}) %collective-permute-start.1) | collective-permute-done | bytes 262176 | tf_op jit(solution)/shard_map/ppermute | solution.py:419
  24.1 5.7 %shard_map.102 = (f32[17,16,1024]{2,1,0:T(8,128)S(1)}, f32[17,16,256]{2,1,0:T(8,128)S(1)}, bf16[16,16,256]{2,1,0:T(8,128)(2,1)S(1)}, bf16[16,16,1024]{2,1,0:T(8,...) custom-call(s32[8,128]{1,0:T(8,128)S(1)} %get-tuple-element.33.refs_0_, f32[2,16384]{1,0:T(2,128)S(1)} %copy-done.7, ...), custom_call_target="tpu_custom_call" | custom-call | flops 8999999488 | bytes 100000 | tf_op jit(solution)/shard_map/pallas_call | solution.py:472
  29.8 0.0 collective-permute-done.2
  29.8 0.1 collective-permute-start.3
  29.9 5.5 %shard_map.103 = (f32[17,16,1024]{2,1,0:T(8,128)S(1)}, f32[17,16,256]{2,1,0:T(8,128)S(1)}, f32[64,128]{1,0:T(8,128)S(1)}) custom-call(s32[8,128]{1,0:T(8,128)S(1)} %get-tuple-element.33.refs_0_, f32[2,16384]{1,0:T(2,128)S(1)} %copy-done.7, bf16[16,16,1024]{2,1,0:T(8,128)(2,1)S(1)} %get-tuple-element.34.refs_2_, ...), custom_call_target="tpu_custom_call" | custom-call | flops 8999999488 | bytes 100000 | tf_op jit(solution)/shard_map/pallas_call | solution.py:472
  35.5 3.1 %collective-permute-start.4 = (f32[256,128]{1,0:T(8,128)S(1)}, f32[256,128]{1,0:T(8,128)S(1)}, u32[]{:S(2)}, u32[]{:S(2)}) collective-permute-start(f32[256,128]{1,0:T(8,128)S(1)} %pad_maximum_fusion.2), channel_id=1, source_target_pairs={{0,8},{4,12},{8,16},{12,20},{16,24},{20,28},{24,32},{28,36},{32,40... | collective-permute-start | bytes 393224 | tf_op jit(solution)/shard_map/ppermute | solution.py:423
  38.5 5.5 %shard_map.104 = (f32[17,16,1024]{2,1,0:T(8,128)S(1)}, f32[17,16,256]{2,1,0:T(8,128)S(1)}, f32[128,128]{1,0:T(8,128)S(1)}) custom-call(s32[8,128]{1,0:T(8,128)S(1)} %get-tuple-element.33.refs_0_, f32[2,16384]{1,0:T(2,128)S(1)} %copy-done.7, bf16[16,16,1024]{2,1,0:T(8,128)(2,1)S(1)} %get-tuple-element.34.refs_2_, ...), custom_call_target="tpu_custom_call" | custom-call | flops 8999999488 | bytes 100000 | tf_op jit(solution)/shard_map/pallas_call | solution.py:472
  44.1 6.2 %collective-permute-start.5 = (f32[256,128]{1,0:T(8,128)S(1)}, f32[256,128]{1,0:T(8,128)S(1)}, u32[]{:S(2)}, u32[]{:S(2)}) collective-permute-start(f32[256,128]{1,0:T(8,128)S(1)} %pad_maximum_fusion.3.refs_8_), channel_id=1, source_target_pairs={{0,240},{4,244},{8,248},{12,252},{16,0},{20,4},{24,8},{28,12},{32,... | collective-permute-start | bytes 393224 | tf_op jit(solution)/shard_map/ppermute | solution.py:423
  50.2 6.8 %shard_map.105 = (f32[17,16,1024]{2,1,0:T(8,128)S(1)}, f32[17,16,256]{2,1,0:T(8,128)S(1)}, f32[256,128]{1,0:T(8,128)S(1)}) custom-call(s32[8,128]{1,0:T(8,128)S(1)} %get-tuple-element.33.refs_0_, f32[2,16384]{1,0:T(2,128)S(1)} %copy-done.7, bf16[16,16,1024]{2,1,0:T(8,128)(2,1)S(1)} %get-tuple-element.34.refs_2_, ...), custom_call_target="tpu_custom_call" | custom-call | flops 8999999488 | bytes 100000 | tf_op jit(solution)/shard_map/pallas_call | solution.py:472
  57.1 5.1 %collective-permute-start.6 = (f32[512,128]{1,0:T(8,128)S(1)}, f32[512,128]{1,0:T(8,128)S(1)}, u32[]{:S(2)}, u32[]{:S(2)}) collective-permute-start(f32[512,128]{1,0:T(8,128)S(1)} %constant_dynamic-update-slice_fusion.refs_10_), channel_id=1, source_target_pairs={{0,128},{4,132},{8,136},{12,140},{16,144},{20,148},{24,152},{28,15... | collective-permute-start | bytes 786440 | tf_op jit(solution)/shard_map/ppermute | solution.py:423
  62.2 6.6 %shard_map.106 = (f32[17,16,1024]{2,1,0:T(8,128)S(1)}, f32[17,16,256]{2,1,0:T(8,128)S(1)}, bf16[24,256,32]{2,1,0:T(8,128)(2,1)S(1)}, bf16[24,16,256]{2,1,0:T(8,128)(2,1)S(1)}, f32[512,128]{1,0:T(8,128)S(1)}) custom-call(s32[8,128]{1,0:T(8,128)S(1)} %get-tuple-element.33.refs_0_, f32[2,16384]{1,0:T(2,128)S(1)} %copy-done.7, ...), custom_call_target="tpu_custom_call" | custom-call | flops 8999999488 | bytes 100000 | tf_op jit(solution)/shard_map/pallas_call | solution.py:472
  68.9 5.7 %collective-permute-start.7 = (f32[1024,128]{1,0:T(8,128)S(1)}, f32[1024,128]{1,0:T(8,128)S(1)}, u32[]{:S(2)}, u32[]{:S(2)}) collective-permute-start(f32[1024,128]{1,0:T(8,128)S(1)} %constant_dynamic-update-slice_fusion.2.own), channel_id=1, source_target_pairs={{0,192},{4,196},{8,200},{12,204},{16,208},{20,212},{24,216},{28,22... | collective-permute-start | bytes 1572872 | tf_op jit(solution)/shard_map/ppermute | solution.py:423
  74.6 7.4 %shard_map.108 = (f32[2,16384]{1,0:T(2,128)S(1)}, f32[2,16384]{1,0:T(2,128)S(1)}, f32[2,16384]{1,0:T(2,128)S(1)}, f32[2,16384]{1,0:T(2,128)S(1)}) custom-call(s32[8,128]{1,0:T(8,128)S(1)} %get-tuple-element.33.refs_0_, f32[2,16384]{1,0:T(2,128)S(1)} %copy-done.7, bf16[16,16,1024]{2,1,0:T(8,128)(2,1)S(1)} %get-tuple-element.34.refs_2_, ...), custom_call_target="tpu_custom_call" | custom-call | flops 8999999488 | bytes 100000 | tf_op jit(solution)/shard_map/pallas_call | solution.py:472
  82.0 2.3 %collective-permute-start.10 = (f32[2,16384]{1,0:T(2,128)S(1)}, f32[2,16384]{1,0:T(2,128)S(1)}, u32[]{:S(2)}, u32[]{:S(2)}) collective-permute-start(f32[2,16384]{1,0:T(2,128)S(1)} %get-tuple-element.60), channel_id=1, source_target_pairs={{0,3},{1,2},{2,1},{3,0},{4,7},{5,6},{6,5},{7,4},{8,11},{9,10},{10,... | collective-permute-start | bytes 393224 | tf_op jit(solution)/shard_map/ppermute | solution.py:419
  84.3 0.8 collective-permute-start.8
  85.1 1.1 %collective-permute-start.9 = (f32[2,16384]{1,0:T(2,128)S(1)}, f32[2,16384]{1,0:T(2,128)S(1)}, u32[]{:S(2)}, u32[]{:S(2)}) collective-permute-start(f32[2,16384]{1,0:T(2,128)S(1)} %get-tuple-element.59), channel_id=1, source_target_pairs={{0,1},{1,0},{2,3},{3,2},{4,5},{5,4},{6,7},{7,6},{8,9},{9,8},{10,11... | collective-permute-start | bytes 393224 | tf_op jit(solution)/shard_map/ppermute | solution.py:419
  86.2 4.8 %shard_map.107 = f32[2,16384]{1,0:T(2,128)S(1)} custom-call(s32[2,124]{1,0:T(2,128)S(1)} %and_add_fusion.1.rows, f32[1024,128]{1,0:T(8,128)S(1)} %constant_dynamic-update-slice_fusion.2.own, f32[1024,128]{1,0:T(8,128)S(1)} %collective-permute-done.7.other, f32[2,64,64,124]{3,2,1,0:T(8,128)S(1)} %bitcast.3, f32[2,15,64,64]{3,2,1,0:T(8,128)S(1)} %copy-done.6, ...), custom_call_target="tpu_custom_call" | custom-call | flops 8000000000 | bytes 100000 | tf_op jit(solution)/shard_map/pallas_call | solution.py:504
  91.0 0.6 collective-permute-done.10
  91.6 0.6 collective-permute-done.8
  92.2 0.3 collective-permute-done.9
  92.5 0.8 add_add_fusion
  (43 shorter events, 0.3 us)
Async XLA Ops:
  0.0 14.7 %copy-start.11 = (s32[124]{0:T(128)S(1)}, s32[124]{0:T(128)}, u32[]{:S(2)}) copy-start(s32[124]{0:T(128)} %constant.37.clone) | copy-start | bytes 1492
  0.0 14.7 %copy-start.12 = (s32[124]{0:T(128)S(1)}, s32[124]{0:T(128)}, u32[]{:S(2)}) copy-start(s32[124]{0:T(128)} %constant.46) | copy-start | bytes 1492
  0.0 14.7 %copy-start.13 = (s32[124]{0:T(128)S(1)}, s32[124]{0:T(128)}, u32[]{:S(2)}) copy-start(s32[124]{0:T(128)} %constant.48) | copy-start | bytes 1492
  0.0 14.8 %collective-permute-start = (f32[2,16384]{1,0:T(2,128)}, f32[2,16384]{1,0:T(2,128)S(1)}, u32[]{:S(2)}, u32[]{:S(2)}) collective-permute-start(f32[2,16384]{1,0:T(2,128)} %refs_4_.1), channel_id=1, source_target_pairs={{0,1},{1,0},{2,3},{3,2},{4,5},{5,4},{6,7},{7,6},{8,9},{9,8},{10,11... | collective-permute-start | bytes 393224 | tf_op jit(solution)/shard_map/ppermute | solution.py:419
  1.7 0.9 %copy-start = (f32[2,16384]{1,0:T(2,128)S(1)}, f32[2,16384]{1,0:T(2,128)}, u32[]{:S(2)}) copy-start(f32[2,16384]{1,0:T(2,128)} %refs_4_.1) | copy-start | bytes 393220
  2.6 2.2 %copy-start.2 = (f32[16,64,1024]{2,1,0:T(8,128)S(1)}, f32[16,64,1024]{2,1,0:T(8,128)}, u32[]{:S(2)}) copy-start(f32[16,64,1024]{2,1,0:T(8,128)} %basis.3) | copy-start | bytes 12582916
  4.8 1.2 %copy-start.5 = (f32[2,15,64,64]{3,2,1,0:T(8,128)S(1)}, f32[2,15,64,64]{3,2,1,0:T(8,128)}, u32[]{:S(2)}) copy-start(f32[2,15,64,64]{3,2,1,0:T(8,128)} %transfer.3) | copy-start | bytes 1474564
  6.0 8.7 %copy-start.10 = (s32[2,124]{1,0:T(2,128)S(1)}, s32[2,124]{1,0:T(2,128)}, u32[]{:S(2)}) copy-start(s32[2,124]{1,0:T(2,128)} %param.15) | copy-start | bytes 2980
  6.0 8.9 %copy-start.1 = (f32[2,16384]{1,0:T(2,128)S(1)}, f32[2,16384]{1,0:T(2,128)}, u32[]{:S(2)}) copy-start(f32[2,16384]{1,0:T(2,128)} %refs_4_.1) | copy-start | bytes 393220
  6.0 12.0 %copy-start.7 = (f32[2,16384]{1,0:T(2,128)S(1)}, f32[2,16384]{1,0:T(2,128)}, u32[]{:S(2)}) copy-start(f32[2,16384]{1,0:T(2,128)} %refs_1_.11) | copy-start | bytes 393220
  6.0 12.0 %copy-start.8 = (s32[16,9]{1,0:T(8,128)S(1)}, s32[16,9]{1,0:T(8,128)}, u32[]{:S(2)}) copy-start(s32[16,9]{1,0:T(8,128)} %list_hbm.1) | copy-start | bytes 1732
  6.0 12.0 %copy-start.9 = (s32[16]{0:T(128)S(1)}, s32[16]{0:T(128)}, u32[]{:S(2)}) copy-start(s32[16]{0:T(128)} %count_hbm.1) | copy-start | bytes 196
  8.4 21.3 %collective-permute-start.2 = (f32[32,128]{1,0:T(8,128)S(1)}, f32[32,128]{1,0:T(8,128)S(1)}, u32[]{:S(2)}, u32[]{:S(2)}) collective-permute-start(f32[32,128]{1,0:T(8,128)S(1)} %shard_map.101.refs_8_), channel_id=1, source_target_pairs={{0,32},{4,36},{8,40},{12,44},{16,48},{20,52},{24,56},{28,60},{32,0... | collective-permute-start | bytes 49160 | tf_op jit(solution)/shard_map/ppermute | solution.py:423
  15.0 9.1 %collective-permute-start.1 = (f32[4,16384]{1,0:T(4,128)S(1)}, f32[4,16384]{1,0:T(4,128)S(1)}, u32[]{:S(2)}, u32[]{:S(2)}) collective-permute-start(f32[4,16384]{1,0:T(4,128)S(1)} %pad_maximum_fusion._), channel_id=1, source_target_pairs={{0,2},{1,3},{2,0},{3,1},{4,6},{5,7},{6,4},{7,5},{8,10},{9,11},{10,... | collective-permute-start | bytes 786440 | tf_op jit(solution)/shard_map/ppermute | solution.py:419
  29.8 5.6 %collective-permute-start.3 = (f32[320,128]{1,0:T(8,128)S(1)}, f32[320,128]{1,0:T(8,128)S(1)}, u32[]{:S(2)}, u32[]{:S(2)}) collective-permute-start(f32[320,128]{1,0:T(8,128)S(1)} %pad_maximum_fusion.1), channel_id=1, source_target_pairs={{0,252},{4,0},{8,4},{12,8},{16,12},{20,16},{24,20},{28,24},{32,28}... | collective-permute-start | bytes 491528 | tf_op jit(solution)/shard_map/ppermute | solution.py:423
  35.5 8.5 %collective-permute-start.4 = (f32[256,128]{1,0:T(8,128)S(1)}, f32[256,128]{1,0:T(8,128)S(1)}, u32[]{:S(2)}, u32[]{:S(2)}) collective-permute-start(f32[256,128]{1,0:T(8,128)S(1)} %pad_maximum_fusion.2), channel_id=1, source_target_pairs={{0,8},{4,12},{8,16},{12,20},{16,24},{20,28},{24,32},{28,36},{32,40... | collective-permute-start | bytes 393224 | tf_op jit(solution)/shard_map/ppermute | solution.py:423
  44.1 13.0 %collective-permute-start.5 = (f32[256,128]{1,0:T(8,128)S(1)}, f32[256,128]{1,0:T(8,128)S(1)}, u32[]{:S(2)}, u32[]{:S(2)}) collective-permute-start(f32[256,128]{1,0:T(8,128)S(1)} %pad_maximum_fusion.3.refs_8_), channel_id=1, source_target_pairs={{0,240},{4,244},{8,248},{12,252},{16,0},{20,4},{24,8},{28,12},{32,... | collective-permute-start | bytes 393224 | tf_op jit(solution)/shard_map/ppermute | solution.py:423
  57.1 11.8 %collective-permute-start.6 = (f32[512,128]{1,0:T(8,128)S(1)}, f32[512,128]{1,0:T(8,128)S(1)}, u32[]{:S(2)}, u32[]{:S(2)}) collective-permute-start(f32[512,128]{1,0:T(8,128)S(1)} %constant_dynamic-update-slice_fusion.refs_10_), channel_id=1, source_target_pairs={{0,128},{4,132},{8,136},{12,140},{16,144},{20,148},{24,152},{28,15... | collective-permute-start | bytes 786440 | tf_op jit(solution)/shard_map/ppermute | solution.py:423
  68.9 17.3 %collective-permute-start.7 = (f32[1024,128]{1,0:T(8,128)S(1)}, f32[1024,128]{1,0:T(8,128)S(1)}, u32[]{:S(2)}, u32[]{:S(2)}) collective-permute-start(f32[1024,128]{1,0:T(8,128)S(1)} %constant_dynamic-update-slice_fusion.2.own), channel_id=1, source_target_pairs={{0,192},{4,196},{8,200},{12,204},{16,208},{20,212},{24,216},{28,22... | collective-permute-start | bytes 1572872 | tf_op jit(solution)/shard_map/ppermute | solution.py:423
  74.6 11.7 %copy-start.3 = (f32[16,64,1024]{2,1,0:T(8,128)S(1)}, f32[16,64,1024]{2,1,0:T(8,128)}, u32[]{:S(2)}) copy-start(f32[16,64,1024]{2,1,0:T(8,128)} %basis.3) | copy-start | bytes 12582916
  74.6 11.7 %copy-start.4 = (f32[2,124,64,64]{1,3,2,0:T(8,128)S(1)}, f32[2,124,64,64]{1,3,2,0:T(8,128)}, u32[]{:S(2)}) copy-start(f32[2,124,64,64]{1,3,2,0:T(8,128)} %param.14) | copy-start | bytes 12189700
  74.6 11.7 %copy-start.6 = (f32[2,15,64,64]{3,2,1,0:T(8,128)S(1)}, f32[2,15,64,64]{3,2,1,0:T(8,128)}, u32[]{:S(2)}) copy-start(f32[2,15,64,64]{3,2,1,0:T(8,128)} %transfer.3) | copy-start | bytes 1474564
  82.0 9.6 %collective-permute-start.10 = (f32[2,16384]{1,0:T(2,128)S(1)}, f32[2,16384]{1,0:T(2,128)S(1)}, u32[]{:S(2)}, u32[]{:S(2)}) collective-permute-start(f32[2,16384]{1,0:T(2,128)S(1)} %get-tuple-element.60), channel_id=1, source_target_pairs={{0,3},{1,2},{2,1},{3,0},{4,7},{5,6},{6,5},{7,4},{8,11},{9,10},{10,... | collective-permute-start | bytes 393224 | tf_op jit(solution)/shard_map/ppermute | solution.py:419
  84.3 7.9 %collective-permute-start.8 = (f32[2,16384]{1,0:T(2,128)S(1)}, f32[2,16384]{1,0:T(2,128)S(1)}, u32[]{:S(2)}, u32[]{:S(2)}) collective-permute-start(f32[2,16384]{1,0:T(2,128)S(1)} %get-tuple-element.58), channel_id=1, source_target_pairs={{0,2},{1,3},{2,0},{3,1},{4,6},{5,7},{6,4},{7,5},{8,10},{9,11},{10,... | collective-permute-start | bytes 393224 | tf_op jit(solution)/shard_map/ppermute | solution.py:419
  85.1 7.4 %collective-permute-start.9 = (f32[2,16384]{1,0:T(2,128)S(1)}, f32[2,16384]{1,0:T(2,128)S(1)}, u32[]{:S(2)}, u32[]{:S(2)}) collective-permute-start(f32[2,16384]{1,0:T(2,128)S(1)} %get-tuple-element.59), channel_id=1, source_target_pairs={{0,1},{1,0},{2,3},{3,2},{4,5},{5,4},{6,7},{7,6},{8,9},{9,8},{10,11... | collective-permute-start | bytes 393224 | tf_op jit(solution)/shard_map/ppermute | solution.py:419

commit v7 on v6

--- a/solution.py
+++ b/solution.py
@@ -105,13 +105,14 @@
     ).astype(B)
 
 
-def prep_kernel(meta, list_hbm, count_hbm, coords, _, lists, sf, tab, place, near_list, near_count, sems):
+def prep_kernel(meta, list_hbm, count_hbm, coords, _, skeleton, lists, sf, tab, place, handed, near_list, near_count, sems):
     copies = [
         pltpu.make_async_copy(list_hbm, near_list, sems.at[0]),
         pltpu.make_async_copy(count_hbm, near_count, sems.at[1]),
     ]
     for copy in copies:
         copy.start()
+    handed[...] = skeleton[...]
     first, r = meta[0], meta[1]
     for i in range(LEAVES):
         source = pl.ds(pl.multiple_of(r * QUART + i * PTS, QUART), QUART)
@@ -424,15 +425,19 @@
 
     first = swap_rhs(charges, 1)
     onward = jnp.concatenate([charges, first], 0)
-    lists, sf, tab, place = call(
+    (table,) = call(up_kernel, [(32, 2 * RANK)], [VMEM] * 3, micros=4)(
+        charges, leaf_basis, transfer
+    )
+    lists, sf, tab, place, table = call(
         prep_kernel,
         [
             jax.ShapeDtypeStruct((8, 128), jnp.int32),
             bf16(LEAVES, QUART, 32),
             bf16(LEAVES, 16, PTS),
             (2, LEAVES * QUART),
+            (32, 2 * RANK),
         ],
-        [SMEM, HBM, HBM, VMEM, ANY],
+        [SMEM, HBM, HBM, VMEM, ANY, VMEM],
         [
             pltpu.SMEM((LEAVES, NEAR), jnp.int32),
             pltpu.SMEM((LEAVES,), jnp.int32),
@@ -440,12 +445,8 @@
         ],
         micros=4,
         smem_outs=1,
-    )(meta, near_list, near_count, coords, onward)
+    )(meta, near_list, near_count, coords, onward, table)
     second = swap_rhs(onward, 2)
-    (table,) = call(up_kernel, [(32, 2 * RANK)], [VMEM] * 3, micros=4)(
-        charges, leaf_basis, transfer
-    )
-
     acc_shape, quart_shape = (LEAVES + 1, 16, PTS), (LEAVES + 1, 16, QUART)
     values = [pltpu.VMEM((QUART, PTS), B)] * 4
     after, edges = table, None

time: 93.5 us -> 92.5 us (0.989)
  the two profiles are of different devices: /device:TPU:32 before, /device:TPU:34 now
where the time goes in v7:
time: 92.5 us; the launch traced here: 91.3 us
  Pallas kernels  62.2 us (67%)
  starting transfers between devices  23.1 us (25%)
  local copies, waits for them, and re-layouts  4.55 us (5%)
  other arithmetic  1.1 us (1%)
    pallas_call x6, Pallas kernels, shards(): call(functools.partial(near_kernel, w, len(carried)), [*outs, *extra, *(v...  50.1 us
    ppermute x6, starting transfers between devices, shift_leaf(): return lax.ppermute(v, 'leaf', pairs)  14.3 us
    ppermute x5, starting transfers between devices, swap_rhs(): return lax.ppermute(v, 'rhs', [(i, i ^ k) for i in range(RHS)])  8.74 us
    pallas_call x1, Pallas kernels, shards(): call(prep_kernel, [jax.ShapeDtypeStruct((8, 128), jnp.int32), bf16(LEAVES...  4.93 us
    pallas_call x1, Pallas kernels, shards(): call(down_kernel, [(2, LEAVES * PTS)], [SMEM] + [VMEM] * 5, [pltpu.VMEM((...  4.77 us
    unnamed x30, local copies, waits for them, and re-layouts  4.43 us
    pallas_call x1, Pallas kernels, shards(): call(up_kernel, [(32, 2 * RANK)], [VMEM] * 3, micros=4)  2.4 us
  transfers between devices with their start and end apart: 11, of which 0 were waited for; matrix products, arithmetic and copies ran while one was open for 0% of the time, Pallas kernels for 68%

profile of v7, /device:TPU:34, one launch (start us, length us, event | category | flops | bytes accessed | tf_op | source)
XLA Modules:
  0.0 91.3 jit_solution(9308087482086495952)
XLA Ops:
  0.0 1.6 %collective-permute-start = (f32[2,16384]{1,0:T(2,128)}, f32[2,16384]{1,0:T(2,128)S(1)}, u32[]{:S(2)}, u32[]{:S(2)}) collective-permute-start(f32[2,16384]{1,0:T(2,128)} %refs_4_.1), channel_id=1, source_target_pairs={{0,1},{1,0},{2,3},{3,2},{4,5},{5,4},{6,7},{7,6},{8,9},{9,8},{10,11... | collective-permute-start | bytes 393224 | tf_op jit(solution)/shard_map/ppermute | solution.py:420
  1.6 0.9 %copy-done = f32[2,16384]{1,0:T(2,128)S(1)} copy-done((f32[2,16384]{1,0:T(2,128)S(1)}, f32[2,16384]{1,0:T(2,128)}, u32[]{:S(2)}) %copy-start) | copy-done | bytes 131096
  2.5 2.2 %copy-done.2 = f32[16,64,1024]{2,1,0:T(8,128)S(1)} copy-done((f32[16,64,1024]{2,1,0:T(8,128)S(1)}, f32[16,64,1024]{2,1,0:T(8,128)}, u32[]{:S(2)}) %copy-start.2) | copy-done | bytes 4194328
  4.7 1.2 %copy-done.5 = f32[2,15,64,64]{3,2,1,0:T(8,128)S(1)} copy-done((f32[2,15,64,64]{3,2,1,0:T(8,128)S(1)}, f32[2,15,64,64]{3,2,1,0:T(8,128)}, u32[]{:S(2)}) %copy-start.5) | copy-done | bytes 491544
  6.0 2.4 %shard_map.100.skeleton = f32[32,128]{1,0:T(8,128)S(1)} custom-call(f32[2,16384]{1,0:T(2,128)S(1)} %copy-done, f32[16,64,1024]{2,1,0:T(8,128)S(1)} %copy-done.2, f32[2,15,64,64]{3,2,1,0:T(8,128)S(1)} %copy-done.5), custom_call_target="tpu_custom_call" | custom-call | flops 4000000000 | bytes 100000 | tf_op jit(solution)/shard_map/pallas_call | solution.py:428
  8.4 0.0 copy-done.13
  8.4 0.1 pad_add_fusion.meta
  8.5 0.0 collective-permute-done.refs_5_
  8.5 0.1 pad_maximum_fusion._
  8.6 3.0 %collective-permute-start.1 = (f32[4,16384]{1,0:T(4,128)S(1)}, f32[4,16384]{1,0:T(4,128)S(1)}, u32[]{:S(2)}, u32[]{:S(2)}) collective-permute-start(f32[4,16384]{1,0:T(4,128)S(1)} %pad_maximum_fusion._), channel_id=1, source_target_pairs={{0,2},{1,3},{2,0},{3,1},{4,6},{5,7},{6,4},{7,5},{8,10},{9,11},{10,... | collective-permute-start | bytes 786440 | tf_op jit(solution)/shard_map/ppermute | solution.py:420
  11.6 4.9 %shard_map.101 = (s32[8,128]{1,0:T(8,128)S(1)}, bf16[16,256,32]{2,1,0:T(8,128)(2,1)S(1)}, bf16[16,16,1024]{2,1,0:T(8,128)(2,1)S(1)}, f32[2,4096]{1,0:T(2,128)S(1)}, f32[32,128]{1,0:T(8,128)S(1)}) custom-call(s32[2]{0:T(128)S(1)} %pad_add_fusion.meta, s32[16,9]{1,0:T(8,128)S(1)} %copy-done.8, s32[16]{0:T(128)S(1)} %copy-done.9, f32[2,16384]{1,0:T(2,128)S(1)} %copy-done.7, ...), custom_call_target="tpu_custom_call" | custom-call | flops 4000000000 | bytes 100000 | tf_op jit(solution)/shard_map/pallas_call | solution.py:431
  16.6 5.8 %collective-permute-start.2 = (f32[32,128]{1,0:T(8,128)S(1)}, f32[32,128]{1,0:T(8,128)S(1)}, u32[]{:S(2)}, u32[]{:S(2)}) collective-permute-start(f32[32,128]{1,0:T(8,128)S(1)} %get-tuple-element.38.refs_8_), channel_id=1, source_target_pairs={{0,32},{4,36},{8,40},{12,44},{16,48},{20,52},{24,56},{28,60},{32,0... | collective-permute-start | bytes 49160 | tf_op jit(solution)/shard_map/ppermute | solution.py:424
  22.3 7.1 %shard_map.102 = (f32[17,16,1024]{2,1,0:T(8,128)S(1)}, f32[17,16,256]{2,1,0:T(8,128)S(1)}, bf16[16,16,256]{2,1,0:T(8,128)(2,1)S(1)}, bf16[16,16,1024]{2,1,0:T(8,...) custom-call(s32[8,128]{1,0:T(8,128)S(1)} %get-tuple-element.34.refs_0_, f32[2,16384]{1,0:T(2,128)S(1)} %copy-done.7, ...), custom_call_target="tpu_custom_call" | custom-call | flops 8999999488 | bytes 100000 | tf_op jit(solution)/shard_map/pallas_call | solution.py:473
  29.5 0.1 collective-permute-start.3
  29.6 8.3 %shard_map.103 = (f32[17,16,1024]{2,1,0:T(8,128)S(1)}, f32[17,16,256]{2,1,0:T(8,128)S(1)}, f32[64,128]{1,0:T(8,128)S(1)}) custom-call(s32[8,128]{1,0:T(8,128)S(1)} %get-tuple-element.34.refs_0_, f32[2,16384]{1,0:T(2,128)S(1)} %copy-done.7, bf16[16,16,1024]{2,1,0:T(8,128)(2,1)S(1)} %get-tuple-element.35.refs_2_, ...), custom_call_target="tpu_custom_call" | custom-call | flops 8999999488 | bytes 100000 | tf_op jit(solution)/shard_map/pallas_call | solution.py:473
  37.9 0.0 collective-permute-done.3
  38.0 3.0 %collective-permute-start.4 = (f32[256,128]{1,0:T(8,128)S(1)}, f32[256,128]{1,0:T(8,128)S(1)}, u32[]{:S(2)}, u32[]{:S(2)}) collective-permute-start(f32[256,128]{1,0:T(8,128)S(1)} %pad_maximum_fusion.2), channel_id=1, source_target_pairs={{0,8},{4,12},{8,16},{12,20},{16,24},{20,28},{24,32},{28,36},{32,40... | collective-permute-start | bytes 393224 | tf_op jit(solution)/shard_map/ppermute | solution.py:424
  41.0 8.3 %shard_map.104 = (f32[17,16,1024]{2,1,0:T(8,128)S(1)}, f32[17,16,256]{2,1,0:T(8,128)S(1)}, f32[128,128]{1,0:T(8,128)S(1)}) custom-call(s32[8,128]{1,0:T(8,128)S(1)} %get-tuple-element.34.refs_0_, f32[2,16384]{1,0:T(2,128)S(1)} %copy-done.7, bf16[16,16,1024]{2,1,0:T(8,128)(2,1)S(1)} %get-tuple-element.35.refs_2_, ...), custom_call_target="tpu_custom_call" | custom-call | flops 8999999488 | bytes 100000 | tf_op jit(solution)/shard_map/pallas_call | solution.py:473
  49.4 0.1 collective-permute-start.5
  49.5 8.2 %shard_map.105 = (f32[17,16,1024]{2,1,0:T(8,128)S(1)}, f32[17,16,256]{2,1,0:T(8,128)S(1)}, f32[256,128]{1,0:T(8,128)S(1)}) custom-call(s32[8,128]{1,0:T(8,128)S(1)} %get-tuple-element.34.refs_0_, f32[2,16384]{1,0:T(2,128)S(1)} %copy-done.7, bf16[16,16,1024]{2,1,0:T(8,128)(2,1)S(1)} %get-tuple-element.35.refs_2_, ...), custom_call_target="tpu_custom_call" | custom-call | flops 8999999488 | bytes 100000 | tf_op jit(solution)/shard_map/pallas_call | solution.py:473
  57.8 5.4 %collective-permute-start.6 = (f32[512,128]{1,0:T(8,128)S(1)}, f32[512,128]{1,0:T(8,128)S(1)}, u32[]{:S(2)}, u32[]{:S(2)}) collective-permute-start(f32[512,128]{1,0:T(8,128)S(1)} %constant_dynamic-update-slice_fusion.refs_10_), channel_id=1, source_target_pairs={{0,128},{4,132},{8,136},{12,140},{16,144},{20,148},{24,152},{28,15... | collective-permute-start | bytes 786440 | tf_op jit(solution)/shard_map/ppermute | solution.py:424
  63.1 8.6 %shard_map.106 = (f32[17,16,1024]{2,1,0:T(8,128)S(1)}, f32[17,16,256]{2,1,0:T(8,128)S(1)}, bf16[24,256,32]{2,1,0:T(8,128)(2,1)S(1)}, bf16[24,16,256]{2,1,0:T(8,128)(2,1)S(1)}, f32[512,128]{1,0:T(8,128)S(1)}) custom-call(s32[8,128]{1,0:T(8,128)S(1)} %get-tuple-element.34.refs_0_, f32[2,16384]{1,0:T(2,128)S(1)} %copy-done.7, ...), custom_call_target="tpu_custom_call" | custom-call | flops 8999999488 | bytes 100000 | tf_op jit(solution)/shard_map/pallas_call | solution.py:473
  71.9 0.1 collective-permute-start.7
  71.9 0.0 copy-start.3
  72.0 0.0 copy-start.4
  72.0 0.0 copy-start.6
  72.0 9.5 %shard_map.108 = (f32[2,16384]{1,0:T(2,128)S(1)}, f32[2,16384]{1,0:T(2,128)S(1)}, f32[2,16384]{1,0:T(2,128)S(1)}, f32[2,16384]{1,0:T(2,128)S(1)}) custom-call(s32[8,128]{1,0:T(8,128)S(1)} %get-tuple-element.34.refs_0_, f32[2,16384]{1,0:T(2,128)S(1)} %copy-done.7, bf16[16,16,1024]{2,1,0:T(8,128)(2,1)S(1)} %get-tuple-element.35.refs_2_, ...), custom_call_target="tpu_custom_call" | custom-call | flops 8999999488 | bytes 100000 | tf_op jit(solution)/shard_map/pallas_call | solution.py:473
  81.5 0.3 collective-permute-start.10
  81.8 2.0 %collective-permute-start.8 = (f32[2,16384]{1,0:T(2,128)S(1)}, f32[2,16384]{1,0:T(2,128)S(1)}, u32[]{:S(2)}, u32[]{:S(2)}) collective-permute-start(f32[2,16384]{1,0:T(2,128)S(1)} %get-tuple-element.60), channel_id=1, source_target_pairs={{0,2},{1,3},{2,0},{3,1},{4,6},{5,7},{6,4},{7,5},{8,10},{9,11},{10,... | collective-permute-start | bytes 393224 | tf_op jit(solution)/shard_map/ppermute | solution.py:420
  83.8 1.9 %collective-permute-start.9 = (f32[2,16384]{1,0:T(2,128)S(1)}, f32[2,16384]{1,0:T(2,128)S(1)}, u32[]{:S(2)}, u32[]{:S(2)}) collective-permute-start(f32[2,16384]{1,0:T(2,128)S(1)} %get-tuple-element.61), channel_id=1, source_target_pairs={{0,1},{1,0},{2,3},{3,2},{4,5},{5,4},{6,7},{7,6},{8,9},{9,8},{10,11... | collective-permute-start | bytes 393224 | tf_op jit(solution)/shard_map/ppermute | solution.py:420
  85.7 4.8 %shard_map.107 = f32[2,16384]{1,0:T(2,128)S(1)} custom-call(s32[2,124]{1,0:T(2,128)S(1)} %and_add_fusion.1.rows, f32[1024,128]{1,0:T(8,128)S(1)} %constant_dynamic-update-slice_fusion.2.own, f32[1024,128]{1,0:T(8,128)S(1)} %collective-permute-done.7.other, f32[2,64,64,124]{3,2,1,0:T(8,128)S(1)} %bitcast.3, f32[2,15,64,64]{3,2,1,0:T(8,128)S(1)} %copy-done.6, ...), custom_call_target="tpu_custom_call" | custom-call | flops 8000000000 | bytes 100000 | tf_op jit(solution)/shard_map/pallas_call | solution.py:505
  90.5 0.8 add_add_fusion
  (43 shorter events, 0.3 us)
Async XLA Ops:
  0.0 8.5 %collective-permute-start = (f32[2,16384]{1,0:T(2,128)}, f32[2,16384]{1,0:T(2,128)S(1)}, u32[]{:S(2)}, u32[]{:S(2)}) collective-permute-start(f32[2,16384]{1,0:T(2,128)} %refs_4_.1), channel_id=1, source_target_pairs={{0,1},{1,0},{2,3},{3,2},{4,5},{5,4},{6,7},{7,6},{8,9},{9,8},{10,11... | collective-permute-start | bytes 393224 | tf_op jit(solution)/shard_map/ppermute | solution.py:420
  1.6 0.9 %copy-start = (f32[2,16384]{1,0:T(2,128)S(1)}, f32[2,16384]{1,0:T(2,128)}, u32[]{:S(2)}) copy-start(f32[2,16384]{1,0:T(2,128)} %refs_4_.1) | copy-start | bytes 393220
  2.5 2.2 %copy-start.2 = (f32[16,64,1024]{2,1,0:T(8,128)S(1)}, f32[16,64,1024]{2,1,0:T(8,128)}, u32[]{:S(2)}) copy-start(f32[16,64,1024]{2,1,0:T(8,128)} %basis.3) | copy-start | bytes 12582916
  4.7 1.2 %copy-start.5 = (f32[2,15,64,64]{3,2,1,0:T(8,128)S(1)}, f32[2,15,64,64]{3,2,1,0:T(8,128)}, u32[]{:S(2)}) copy-start(f32[2,15,64,64]{3,2,1,0:T(8,128)} %transfer.3) | copy-start | bytes 1474564
  5.9 2.5 %copy-start.10 = (s32[2,124]{1,0:T(2,128)S(1)}, s32[2,124]{1,0:T(2,128)}, u32[]{:S(2)}) copy-start(s32[2,124]{1,0:T(2,128)} %param.15) | copy-start | bytes 2980
  5.9 2.5 %copy-start.11 = (s32[124]{0:T(128)S(1)}, s32[124]{0:T(128)}, u32[]{:S(2)}) copy-start(s32[124]{0:T(128)} %constant.37.clone) | copy-start | bytes 1492
  5.9 2.5 %copy-start.12 = (s32[124]{0:T(128)S(1)}, s32[124]{0:T(128)}, u32[]{:S(2)}) copy-start(s32[124]{0:T(128)} %constant.46) | copy-start | bytes 1492
  5.9 2.5 %copy-start.13 = (s32[124]{0:T(128)S(1)}, s32[124]{0:T(128)}, u32[]{:S(2)}) copy-start(s32[124]{0:T(128)} %constant.48) | copy-start | bytes 1492
  5.9 2.6 %copy-start.1 = (f32[2,16384]{1,0:T(2,128)S(1)}, f32[2,16384]{1,0:T(2,128)}, u32[]{:S(2)}) copy-start(f32[2,16384]{1,0:T(2,128)} %refs_4_.1) | copy-start | bytes 393220
  5.9 5.7 %copy-start.7 = (f32[2,16384]{1,0:T(2,128)S(1)}, f32[2,16384]{1,0:T(2,128)}, u32[]{:S(2)}) copy-start(f32[2,16384]{1,0:T(2,128)} %refs_1_.11) | copy-start | bytes 393220
  5.9 5.7 %copy-start.8 = (s32[16,9]{1,0:T(8,128)S(1)}, s32[16,9]{1,0:T(8,128)}, u32[]{:S(2)}) copy-start(s32[16,9]{1,0:T(8,128)} %list_hbm.1) | copy-start | bytes 1732
  5.9 5.7 %copy-start.9 = (s32[16]{0:T(128)S(1)}, s32[16]{0:T(128)}, u32[]{:S(2)}) copy-start(s32[16]{0:T(128)} %count_hbm.1) | copy-start | bytes 196
  8.6 13.7 %collective-permute-start.1 = (f32[4,16384]{1,0:T(4,128)S(1)}, f32[4,16384]{1,0:T(4,128)S(1)}, u32[]{:S(2)}, u32[]{:S(2)}) collective-permute-start(f32[4,16384]{1,0:T(4,128)S(1)} %pad_maximum_fusion._), channel_id=1, source_target_pairs={{0,2},{1,3},{2,0},{3,1},{4,6},{5,7},{6,4},{7,5},{8,10},{9,11},{10,... | collective-permute-start | bytes 786440 | tf_op jit(solution)/shard_map/ppermute | solution.py:420
  16.6 12.9 %collective-permute-start.2 = (f32[32,128]{1,0:T(8,128)S(1)}, f32[32,128]{1,0:T(8,128)S(1)}, u32[]{:S(2)}, u32[]{:S(2)}) collective-permute-start(f32[32,128]{1,0:T(8,128)S(1)} %get-tuple-element.38.refs_8_), channel_id=1, source_target_pairs={{0,32},{4,36},{8,40},{12,44},{16,48},{20,52},{24,56},{28,60},{32,0... | collective-permute-start | bytes 49160 | tf_op jit(solution)/shard_map/ppermute | solution.py:424
  29.5 8.4 %collective-permute-start.3 = (f32[320,128]{1,0:T(8,128)S(1)}, f32[320,128]{1,0:T(8,128)S(1)}, u32[]{:S(2)}, u32[]{:S(2)}) collective-permute-start(f32[320,128]{1,0:T(8,128)S(1)} %pad_maximum_fusion.1), channel_id=1, source_target_pairs={{0,252},{4,0},{8,4},{12,8},{16,12},{20,16},{24,20},{28,24},{32,28}... | collective-permute-start | bytes 491528 | tf_op jit(solution)/shard_map/ppermute | solution.py:424
  38.0 11.3 %collective-permute-start.4 = (f32[256,128]{1,0:T(8,128)S(1)}, f32[256,128]{1,0:T(8,128)S(1)}, u32[]{:S(2)}, u32[]{:S(2)}) collective-permute-start(f32[256,128]{1,0:T(8,128)S(1)} %pad_maximum_fusion.2), channel_id=1, source_target_pairs={{0,8},{4,12},{8,16},{12,20},{16,24},{20,28},{24,32},{28,36},{32,40... | collective-permute-start | bytes 393224 | tf_op jit(solution)/shard_map/ppermute | solution.py:424
  49.4 8.3 %collective-permute-start.5 = (f32[256,128]{1,0:T(8,128)S(1)}, f32[256,128]{1,0:T(8,128)S(1)}, u32[]{:S(2)}, u32[]{:S(2)}) collective-permute-start(f32[256,128]{1,0:T(8,128)S(1)} %pad_maximum_fusion.3.refs_8_), channel_id=1, source_target_pairs={{0,240},{4,244},{8,248},{12,252},{16,0},{20,4},{24,8},{28,12},{32,... | collective-permute-start | bytes 393224 | tf_op jit(solution)/shard_map/ppermute | solution.py:424
  57.8 14.0 %collective-permute-start.6 = (f32[512,128]{1,0:T(8,128)S(1)}, f32[512,128]{1,0:T(8,128)S(1)}, u32[]{:S(2)}, u32[]{:S(2)}) collective-permute-start(f32[512,128]{1,0:T(8,128)S(1)} %constant_dynamic-update-slice_fusion.refs_10_), channel_id=1, source_target_pairs={{0,128},{4,132},{8,136},{12,140},{16,144},{20,148},{24,152},{28,15... | collective-permute-start | bytes 786440 | tf_op jit(solution)/shard_map/ppermute | solution.py:424
  71.9 13.8 %collective-permute-start.7 = (f32[1024,128]{1,0:T(8,128)S(1)}, f32[1024,128]{1,0:T(8,128)S(1)}, u32[]{:S(2)}, u32[]{:S(2)}) collective-permute-start(f32[1024,128]{1,0:T(8,128)S(1)} %constant_dynamic-update-slice_fusion.2.own), channel_id=1, source_target_pairs={{0,192},{4,196},{8,200},{12,204},{16,208},{20,212},{24,216},{28,22... | collective-permute-start | bytes 1572872 | tf_op jit(solution)/shard_map/ppermute | solution.py:424
  71.9 13.7 %copy-start.3 = (f32[16,64,1024]{2,1,0:T(8,128)S(1)}, f32[16,64,1024]{2,1,0:T(8,128)}, u32[]{:S(2)}) copy-start(f32[16,64,1024]{2,1,0:T(8,128)} %basis.3) | copy-start | bytes 12582916
  72.0 13.7 %copy-start.4 = (f32[2,124,64,64]{1,3,2,0:T(8,128)S(1)}, f32[2,124,64,64]{1,3,2,0:T(8,128)}, u32[]{:S(2)}) copy-start(f32[2,124,64,64]{1,3,2,0:T(8,128)} %param.14) | copy-start | bytes 12189700
  72.0 13.7 %copy-start.6 = (f32[2,15,64,64]{3,2,1,0:T(8,128)S(1)}, f32[2,15,64,64]{3,2,1,0:T(8,128)}, u32[]{:S(2)}) copy-start(f32[2,15,64,64]{3,2,1,0:T(8,128)} %transfer.3) | copy-start | bytes 1474564
  81.5 9.0 %collective-permute-start.10 = (f32[2,16384]{1,0:T(2,128)S(1)}, f32[2,16384]{1,0:T(2,128)S(1)}, u32[]{:S(2)}, u32[]{:S(2)}) collective-permute-start(f32[2,16384]{1,0:T(2,128)S(1)} %get-tuple-element.62), channel_id=1, source_target_pairs={{0,3},{1,2},{2,1},{3,0},{4,7},{5,6},{6,5},{7,4},{8,11},{9,10},{10,... | collective-permute-start | bytes 393224 | tf_op jit(solution)/shard_map/ppermute | solution.py:420
  81.8 8.7 %collective-permute-start.8 = (f32[2,16384]{1,0:T(2,128)S(1)}, f32[2,16384]{1,0:T(2,128)S(1)}, u32[]{:S(2)}, u32[]{:S(2)}) collective-permute-start(f32[2,16384]{1,0:T(2,128)S(1)} %get-tuple-element.60), channel_id=1, source_target_pairs={{0,2},{1,3},{2,0},{3,1},{4,6},{5,7},{6,4},{7,5},{8,10},{9,11},{10,... | collective-permute-start | bytes 393224 | tf_op jit(solution)/shard_map/ppermute | solution.py:420
  83.8 6.7 %collective-permute-start.9 = (f32[2,16384]{1,0:T(2,128)S(1)}, f32[2,16384]{1,0:T(2,128)S(1)}, u32[]{:S(2)}, u32[]{:S(2)}) collective-permute-start(f32[2,16384]{1,0:T(2,128)S(1)} %get-tuple-element.61), channel_id=1, source_target_pairs={{0,1},{1,0},{2,3},{3,2},{4,5},{5,4},{6,7},{7,6},{8,9},{9,8},{10,11... | collective-permute-start | bytes 393224 | tf_op jit(solution)/shard_map/ppermute | solution.py:420
